TPU v7x, 512 devices: a whole 4x8x8 slice. The times are simulated.
512 devices in a mesh: tower: 32 (over y, x), shard: 16 (over z, core).
Axes of the slice: x: 4, y: 8, z: 8, core: 2. Of those that a mesh axis runs over, the one named last changes fastest.
Arguments:
- quotient_rows: bfloat16 [512, 256, 128], P('tower', 'shard'), may hold values from -6 to 6
- remainder_rows: bfloat16 [512, 128, 128], P('tower'), may hold values from -6 to 6
- quotient_index: int32 [512, 16, 512], P('tower', 'shard'), may hold values from 0 to 255
- remainder_index: int32 [512, 16, 512], P('tower', 'shard'), may hold values from 0 to 127
- bag_sizes: int32 [512, 16, 128], P('tower', 'shard'), may hold values from 1 to 16, 512 in all within a row
- tower_weight: bfloat16 [32, 2048, 256], P('tower'), may hold values from -5 to 5
- norm_gain: bfloat16 [8192], replicated, may hold values from 0.25 to 1.75
- cotangent: bfloat16 [16, 128, 8192], P('shard', 'tower'), may hold values from -1.25 to 1.25
Outputs:
- joint: bfloat16 [16, 128, 8192], P('shard', 'tower')
- weight_grad: float32 [32, 2048, 256], P('tower')
- quotient_grad: float32 [512, 256, 128], P('tower', 'shard')
- remainder_grad: float32 [512, 128, 128], P('tower', 'shard')
Inputs may be any that keep to these rules, and one draw needn't show every extreme that they name: `bag_sizes`: each row sums to 512; lookups are ordered by example.
All inputs are finite; a program needn't handle non-finite values.
Results may differ from a plain program's by a relative error of at most 0.0093.
Values may be sent and summed in bfloat16 or wider, within the bound.
No kernel may reach another device: no remote copies, remote signals or barrier semaphores. Data moves between devices by JAX's collectives and lax.ppermute only.
A program may use at most 64 MiB of HBM per device.

v0:
```python
import jax
import jax.numpy as jnp
from jax import lax
from jax.sharding import PartitionSpec as P

norm_eps = 1e-05


def layer_norm(values, gain):
    center = values - jnp.mean(values, axis=-1, keepdims=True)
    spread = jnp.mean(center * center, axis=-1, keepdims=True)
    return center * lax.rsqrt(spread + norm_eps) * gain


def on_device(
    quotient_rows,
    remainder_rows,
    quotient_index,
    remainder_index,
    bag_sizes,
    tower_weight,
    norm_gain,
    cotangent,
):
    feats, rows_dev, width = quotient_rows.shape
    shards = lax.axis_size("shard")
    owned = bag_sizes.shape[2]
    lookups = quotient_index.shape[2]
    table_count = rows_dev * shards
    remainder_count = remainder_rows.shape[1]
    positions = jnp.arange(lookups, dtype=jnp.int32)
    quot_pick = quotient_index[:, 0]
    rem_pick = remainder_index[:, 0]
    sizes_here = bag_sizes[:, 0]
    bag_ends = jnp.cumsum(sizes_here, axis=1)
    bag_starts = bag_ends - sizes_here
    member = (positions[None, None, :] >= bag_starts[:, :, None]) & (
        positions[None, None, :] < bag_ends[:, :, None]
    )
    member_wide = member.astype(jnp.float32)
    member_narrow = member.astype(jnp.bfloat16)
    quot_hot = quot_pick[:, :, None] == jnp.arange(table_count, dtype=jnp.int32)[None, None, :]
    rem_hot = rem_pick[:, :, None] == jnp.arange(remainder_count, dtype=jnp.int32)[None, None, :]
    all_rows = lax.all_gather(quotient_rows, "shard", axis=1, tiled=True)
    quot_looked = jnp.einsum(
        "flq,fqw->flw", quot_hot.astype(jnp.bfloat16), all_rows, preferred_element_type=jnp.float32
    )
    rem_looked = jnp.einsum(
        "flr,frw->flw",
        rem_hot.astype(jnp.bfloat16),
        remainder_rows,
        preferred_element_type=jnp.float32,
    )
    composed = quot_looked * rem_looked
    pooled = jnp.einsum(
        "fkj,fjw->fkw",
        member_wide,
        composed,
        precision=lax.Precision.HIGHEST,
        preferred_element_type=jnp.float32,
    )
    flat = pooled.astype(jnp.bfloat16).transpose(1, 0, 2).reshape(owned, feats * width)
    weight = tower_weight[0]
    pre = jnp.dot(flat, weight, preferred_element_type=jnp.float32)
    activated = jax.nn.silu(pre).astype(jnp.bfloat16)
    gain = norm_gain.astype(jnp.float32)
    joined = lax.all_to_all(activated, "tower", split_axis=0, concat_axis=1, tiled=True)
    normed, pullback = jax.vjp(lambda v: layer_norm(v, gain), joined.astype(jnp.float32))
    joint = normed.astype(jnp.bfloat16)[None]
    joined_grad = pullback(cotangent[0].astype(jnp.float32))[0].astype(jnp.bfloat16)
    tower_grad = lax.all_to_all(joined_grad, "tower", split_axis=1, concat_axis=0, tiled=True)
    sigma = jax.nn.sigmoid(pre)
    pre_grad = (tower_grad.astype(jnp.float32) * sigma * (1.0 + pre * (1.0 - sigma))).astype(
        jnp.bfloat16
    )
    weight_part = lax.dot_general(
        flat, pre_grad, (((0,), (0,)), ((), ())), preferred_element_type=jnp.float32
    )
    weight_grad = lax.psum(weight_part, "shard")[None]
    input_grad = lax.dot_general(
        pre_grad, weight, (((1,), (1,)), ((), ())), preferred_element_type=jnp.float32
    )
    bag_grad = input_grad.astype(jnp.bfloat16).reshape(owned, feats, width).transpose(1, 0, 2)
    lookup_grad = jnp.einsum(
        "fkj,fkw->fjw", member_narrow, bag_grad, preferred_element_type=jnp.float32
    )
    quot_parts = jnp.einsum(
        "flq,flw->fqw",
        quot_hot.astype(jnp.float32),
        lookup_grad * rem_looked,
        precision=lax.Precision.HIGHEST,
        preferred_element_type=jnp.float32,
    )
    rem_parts = jnp.einsum(
        "flr,flw->frw",
        rem_hot.astype(jnp.float32),
        lookup_grad * quot_looked,
        precision=lax.Precision.HIGHEST,
        preferred_element_type=jnp.float32,
    )
    quotient_grad, remainder_grad = (
        lax.psum_scatter(quot_parts, "shard", scatter_dimension=1, tiled=True),
        lax.psum_scatter(rem_parts, "shard", scatter_dimension=1, tiled=True),
    )
    return (joint, weight_grad, quotient_grad, remainder_grad)


def solution(mesh):
    in_specs = (
        P("tower", "shard", None),
        P("tower", None, None),
        P("tower", "shard", None),
        P("tower", "shard", None),
        P("tower", "shard", None),
        P("tower", None, None),
        P(),
        P("shard", "tower", None),
    )
    out_specs = (
        P("shard", "tower", None),
        P("tower", None, None),
        P("tower", "shard", None),
        P("tower", "shard", None),
    )
    return jax.shard_map(
        on_device, mesh=mesh, in_specs=in_specs, out_specs=out_specs, check_vma=False
    )
```

profile of v0, /device:TPU:1, one launch (start us, length us, event | category | flops | bytes accessed | tf_op | source)
XLA Modules:
  0.0 349.2 jit_solution(15952132533827074129)
XLA Ops:
  7.2 0.7 all-gather.2.cloned.1.call-update
  7.9 1.0 reduce_window_sum.11
  8.9 0.7 sub.39
  9.6 0.8 copy.33
  10.4 0.8 copy.32
  11.1 4.2 %fusion.7 = f32[16,512,128]{2,1,0:T(8,128)} fusion(bf16[16,128,128]{2,1,0:T(8,128)(2,1)} %param.9, s32[16,512]{1,0:T(8,128)S(1)} %bitcast.62), kind=kOutput, calls=%fused_computation.9 | convolution fusion | flops 269484032 | bytes 4751360 | tf_op jit(solution)/shard_map/flr,frw->flw/dot_general | solution.py:48
  15.4 41.6 %all-gather.2.cloned.1.call-done = bf16[16,256,128]{2,1,0:T(8,128)(2,1)} async-done(((bf16[16,16,128]{2,1,0:T(8,128)(2,1)}), bf16[16,256,128]{2,1,0:T(8,128)(2,1)}) %all-gather.2.cloned.1.call-update) | async-done | bytes 1048592 | tf_op jit(solution)/shard_map/all_gather | solution.py:44
  56.9 3.8 %fusion.1 = f32[16,512,128]{2,1,0:T(8,128)S(1)} fusion(bf16[16,256,128]{2,1,0:T(8,128)(2,1)} %all-gather.2.cloned.1.call-done, s32[16,512]{1,0:T(8,128)S(1)} %bitcast.65), kind=kOutput, calls=%fused_computation.2 | convolution fusion | flops 538968064 | bytes 5275648 | tf_op jit(solution)/shard_map/flq,fqw->flw/dot_general | solution.py:45
  60.8 4.3 %fusion.20 = bf16[16,128,128]{1,2,0:T(8,128)(2,1)S(1)} fusion(f32[16,512,128]{2,1,0:T(8,128)S(1)} %fusion.1, f32[16,512,128]{2,1,0:T(8,128)S(1)} %copy-done.1, s32[16,128]{1,0:T(8,128)S(1)} %reduce_window_sum.11, s32[16,128]{1,0:T(8,128)S(1)} %sub.39), kind=kOutput, calls=%fused_computation.24 | convolution fusion | flops 1615069184 | bytes 8929280 | tf_op jit(solution)/shard_map/fkj,fjw->fkw/dot_general | solution.py:55
  65.1 0.4 multiply_convert_fusion.2
  65.5 0.7 all_to_all.8
  66.1 9.2 %all-to-all-start = ((bf16[32,4,256]{2,1,0:T(4,128)(2,1)}), bf16[32,4,256]{2,1,0:T(4,128)(2,1)S(1)}, u32[]{:S(2)}, u32[]{:S(2)}) async-start(bf16[32,4,256]{2,1,0:T(4,128)(2,1)} %all_to_all.8), calls=%async_computation | async-start | bytes 131072 | tf_op jit(solution)/shard_map/all_to_all | solution.py:67
  75.3 0.0 all-reduce.2.cloned.1.call-start
  75.4 8.7 %all-to-all-done = bf16[32,4,256]{2,1,0:T(4,128)(2,1)S(1)} async-done(((bf16[32,4,256]{2,1,0:T(4,128)(2,1)}), bf16[32,4,256]{2,1,0:T(4,128)(2,1)S(1)}, u32[]{:S(2)}, u32[]{:S(2)}) %all-to-all-start) | async-done | bytes 65568 | tf_op jit(solution)/shard_map/all_to_all | solution.py:67
  84.1 0.2 convert_reduce_fusion
  84.3 0.3 fusion.35
  84.7 0.3 fusion.32
  84.9 0.1 fusion.31
  85.1 12.0 %all_to_all.23 = bf16[4,32,256]{2,0,1:T(4,128)(2,1)S(1)} all-to-all(bf16[4,32,256]{2,0,1:T(4,128)(2,1)S(1)} %fusion.31), channel_id=1, replica_groups=mesh['tower'=32,'shard'=16] {'tower'}, dimensions={1} | all-to-all | bytes 131072 | tf_op jit(solution)/shard_map/all_to_all | solution.py:71
  97.2 0.1 multiply_convert_fusion
  97.3 1.7 convolution_bitcast_fusion
  99.0 0.2 reduce-scatter.5.cloned.1.call-start
  99.3 0.5 fusion.25
  99.7 1.1 fusion.11
  100.8 2.0 copy-done.2
  102.8 3.9 %fusion.2 = f32[16,128,128]{2,1,0:T(8,128)} fusion(f32[16,512,128]{2,1,0:T(8,128)S(1)} %fusion.11, f32[16,512,128]{2,1,0:T(8,128)S(1)} %copy-done.4, s32[16,512]{1,0:T(8,128)S(1)} %bitcast.63), kind=kOutput, calls=%fused_computation.3 | convolution fusion | flops 1612709888 | bytes 9469952 | tf_op jit(solution)/shard_map/flr,flw->frw/dot_general | solution.py:94
  106.7 8.5 %fusion = f32[16,256,128]{2,1,0:T(8,128)} fusion(f32[16,512,128]{2,1,0:T(8,128)} %copy-done.2, f32[16,512,128]{2,1,0:T(8,128)} %fusion.7, s32[16,512]{1,0:T(8,128)S(1)} %bitcast.66), kind=kOutput, calls=%fused_computation.1 | convolution fusion | flops 3224371200 | bytes 10518528 | tf_op jit(solution)/shard_map/flq,flw->fqw/dot_general | solution.py:87
  115.3 0.7 multiply_convert_fusion.1
  116.0 98.5 %all-reduce.2.cloned.1.call-done = f32[1,2048,256]{2,1,0:T(8,128)} async-done(((f32[1,2048,256]{2,1,0:T(8,128)}), f32[1,2048,256]{2,1,0:T(8,128)}) %all-reduce.2.cloned.1.call-update) | async-done | bytes 2097168 | tf_op jit(solution)/shard_map/psum | solution.py:79
  214.5 61.1 %reduce-scatter.5.cloned.1.call-done = f32[16,8,128]{2,1,0:T(8,128)} async-done(((f32[16,128,128]{2,1,0:T(8,128)}), f32[16,8,128]{2,1,0:T(8,128)}) %reduce-scatter.5.cloned.1.call-update) | async-done | bytes 65552 | tf_op jit(solution)/shard_map/reduce_scatter | solution.py:103
  275.6 64.0 %reduce-scatter.3.cloned.1.call-done = f32[16,16,128]{2,1,0:T(8,128)} async-done(((f32[16,256,128]{2,1,0:T(8,128)}), f32[16,16,128]{2,1,0:T(8,128)}) %reduce-scatter.3.cloned.1.call-update) | async-done | bytes 131088 | tf_op jit(solution)/shard_map/reduce_scatter | solution.py:102
  339.6 3.0 copy.35
  (26 shorter events, 0.3 us)
Async XLA Ops:
  7.2 58.0 %copy-start = (bf16[1,2048,256]{2,1,0:T(8,128)(2,1)S(1)}, bf16[1,2048,256]{2,1,0:T(8,128)(2,1)}, u32[]{:S(2)}) copy-start(bf16[1,2048,256]{2,1,0:T(8,128)(2,1)} %param.13) | copy-start | bytes 3145732
  7.2 49.8 %all-gather.2.cloned.1.call-start = ((), (), s32[]{:S(2)}) async-start(), calls=%async_computation.4 | async-start | bytes 1114112 | tf_op jit(solution)/shard_map/all_gather | solution.py:44
  56.9 3.8 %copy-start.1 = (f32[16,512,128]{2,1,0:T(8,128)S(1)}, f32[16,512,128]{2,1,0:T(8,128)}, u32[]{:S(2)}) copy-start(f32[16,512,128]{2,1,0:T(8,128)} %fusion.7) | copy-start | bytes 12582916
  60.7 4.4 %copy-start.3 = (f32[16,512,128]{2,1,0:T(8,128)}, f32[16,512,128]{2,1,0:T(8,128)S(1)}, u32[]{:S(2)}) copy-start(f32[16,512,128]{2,1,0:T(8,128)S(1)} %fusion.1) | copy-start | bytes 12582916
  60.7 14.6 %copy-start.6 = (bf16[8192]{0:T(1024)(128)(2,1)S(1)}, bf16[8192]{0:T(1024)(128)(2,1)}, u32[]{:S(2)}) copy-start(bf16[8192]{0:T(1024)(128)(2,1)} %param.14) | copy-start | bytes 49156
  60.7 23.6 %copy-start.5 = (bf16[1,4,8192]{2,1,0:T(4,128)(2,1)S(1)}, bf16[1,4,8192]{2,1,0:T(4,128)(2,1)}, u32[]{:S(2)}) copy-start(bf16[1,4,8192]{2,1,0:T(4,128)(2,1)} %param.15) | copy-start | bytes 196612
  66.1 18.0 %all-to-all-start = ((bf16[32,4,256]{2,1,0:T(4,128)(2,1)}), bf16[32,4,256]{2,1,0:T(4,128)(2,1)S(1)}, u32[]{:S(2)}, u32[]{:S(2)}) async-start(bf16[32,4,256]{2,1,0:T(4,128)(2,1)} %all_to_all.8), calls=%async_computation | async-start | bytes 131072 | tf_op jit(solution)/shard_map/all_to_all | solution.py:67
  75.3 139.2 %all-reduce.2.cloned.1.call-start = ((), (), s32[]{:S(2)}) async-start(), calls=%async_computation.5 | async-start | bytes 4194304 | tf_op jit(solution)/shard_map/psum | solution.py:79
  99.0 176.6 %reduce-scatter.5.cloned.1.call-start = ((), (), s32[]{:S(2)}) async-start(), calls=%async_computation.7 | async-start | bytes 1114112 | tf_op jit(solution)/shard_map/reduce_scatter | solution.py:103
  99.2 3.5 %copy-start.4 = (f32[16,512,128]{2,1,0:T(8,128)S(1)}, f32[16,512,128]{2,1,0:T(8,128)}, u32[]{:S(2)}) copy-start(f32[16,512,128]{2,1,0:T(8,128)} %copy-done.3) | copy-start | bytes 12582916
  100.8 2.0 copy-start.2
  106.7 232.9 %reduce-scatter.3.cloned.1.call-start = ((), (), s32[]{:S(2)}) async-start(), calls=%async_computation.6 | async-start | bytes 2228224 | tf_op jit(solution)/shard_map/reduce_scatter | solution.py:102
Sparse Core Ops, SparseCore 0:
  10.1 46.8 all-gather.1
  99.1 115.3 all-reduce.1
  217.9 57.6 reduce-scatter.4
  279.1 60.4 reduce-scatter.2
where the time goes:
time: 352 us; the launch traced here: 349 us
  waiting for transfers between devices  275 us (78%)
  matrix products  28.4 us (8%)
  between operations  13.9 us (4%)
  blocking collectives  12 us (3%)
  starting transfers between devices  9.51 us (3%)
  local copies, waits for them, and re-layouts  7.26 us (2%)
    psum x1, waiting for transfers between devices, on_device(): weight_grad = lax.psum(weight_part, 'shard')[None]  98.5 us
    reduce_scatter x1, waiting for transfers between devices, on_device(): lax.psum_scatter(quot_parts, 'shard', scatter_dimension=1, tiled=True)  64 us
    reduce_scatter x1, waiting for transfers between devices, on_device(): lax.psum_scatter(rem_parts, 'shard', scatter_dimension=1, tiled=True)  61.1 us
    all_gather x1, waiting for transfers between devices, on_device(): all_rows = lax.all_gather(quotient_rows, 'shard', axis=1, tiled=True)  41.6 us
    all_to_all x1, blocking collectives, on_device(): lax.all_to_all(joined_grad, 'tower', split_axis=1, concat_axis=0, tiled=T...  12 us
    all_to_all x1, starting transfers between devices, on_device(): lax.all_to_all(activated, 'tower', split_axis=0, concat_axis=1, tiled=True)  9.17 us
    all_to_all x1, waiting for transfers between devices, on_device(): lax.all_to_all(activated, 'tower', split_axis=0, concat_axis=1, tiled=True)  8.73 us
    dot_general x1, matrix products, on_device(): jnp.einsum('flq,flw->fqw', quot_hot.astype(jnp.float32), lookup_grad * re...  8.52 us
  transfers between devices with their start and end apart: 5, of which 5 were waited for; matrix products, arithmetic and copies ran while one was open for 6% of the time, Pallas kernels for 0%

commit v1 on v0

v1 whole, which is shorter than its diff:
```python
import functools

import jax
import jax.numpy as jnp
from jax import lax
from jax.experimental import pallas as pl
from jax.experimental.pallas import tpu as pltpu
from jax.sharding import PartitionSpec as P

norm_eps = 1e-05
f32, bf16 = jnp.float32, jnp.bfloat16
NT = (((1,), (1,)), ((), ()))
VMEM_LIMIT = 48 * 1024 * 1024


def mm(a, b):
    return jnp.dot(a, b, preferred_element_type=f32)


def mm_nt(a, b):
    return lax.dot_general(a, b, NT, preferred_element_type=f32)


def triangles(n):
    row = lax.broadcasted_iota(jnp.int32, (n, n), 0)
    col = lax.broadcasted_iota(jnp.int32, (n, n), 1)
    upto = jnp.where(col <= row, 1.0, 0.0).astype(bf16)
    before = jnp.where(col < row, 1.0, 0.0).astype(bf16)
    return jnp.concatenate([upto, before], axis=0)


def masks(picks, tri):
    values = picks.astype(f32)
    row_q = lax.broadcasted_iota(jnp.int32, (256, 128), 0).astype(f32)
    row_r = lax.broadcasted_iota(jnp.int32, (128, 128), 0).astype(f32)
    lane = lax.broadcasted_iota(jnp.int32, (128, 128), 1).astype(f32)
    sums = mm_nt(tri, picks)
    ends = jnp.broadcast_to(sums[:128, 8:9], (128, 128))
    starts = jnp.broadcast_to(sums[128:, 8:9], (128, 128))
    quot, rem, member = [], [], []
    for c in range(4):
        quot.append(jnp.where(row_q == values[c : c + 1], 1.0, 0.0).astype(bf16))
        rem.append(jnp.where(row_r == values[4 + c : 5 + c], 1.0, 0.0).astype(bf16))
        here = lane + float(128 * c)
        inside = (here < ends) & (here >= starts)
        member.append(jnp.where(inside, 1.0, 0.0).astype(bf16))
    return tuple(jnp.concatenate(v, axis=1) for v in (quot, rem, member))


def pool_kernel(per_step, got_ref, rem_ref, bag_ref, bag_t_ref, quot_ref, remd_ref, qt_ref, rt_ref):
    step = pl.program_id(0)

    @pl.when(step == 0)
    def _():
        table = got_ref[:, :16, :].reshape(256, 128)
        qt_ref[...] = table.astype(f32).T.astype(bf16)
        rt_ref[...] = rem_ref[...].astype(f32).T.astype(bf16)

    tri = triangles(128)
    for i in range(per_step):
        picks = got_ref[step * per_step + i, 16:32, :]
        quot_hot, rem_hot, member = masks(picks, tri)
        quot = mm(qt_ref[...], quot_hot)
        rem = mm(rt_ref[...], rem_hot)
        composed = quot * rem
        high = composed.astype(bf16)
        low = (composed - high.astype(f32)).astype(bf16)
        pooled = mm_nt(member, high) + mm_nt(member, low)
        bag_ref[i] = pooled.astype(bf16)
        bag_t_ref[i] = pooled.T.astype(bf16)
        quot_ref[i] = quot.astype(bf16)
        remd_ref[i] = rem.astype(bf16)


def pool(got, remainder):
    groups, per_step = got.shape[0], 4
    block = lambda *dims: pl.BlockSpec((per_step, *dims), lambda i: (i, 0, 0))
    shape = lambda *dims: jax.ShapeDtypeStruct((groups, *dims), bf16)
    return pl.pallas_call(
        functools.partial(pool_kernel, per_step),
        grid=(groups // per_step,),
        in_specs=[
            pl.BlockSpec(got.shape, lambda i: (0, 0, 0)),
            pl.BlockSpec(remainder.shape, lambda i: (0, 0)),
        ],
        out_specs=[block(128, 128), block(128, 128), block(128, 512), block(128, 512)],
        out_shape=[shape(128, 128), shape(128, 128), shape(128, 512), shape(128, 512)],
        scratch_shapes=[pltpu.VMEM((128, 256), bf16), pltpu.VMEM((128, 128), bf16)],
        compiler_params=pltpu.CompilerParams(vmem_limit_bytes=VMEM_LIMIT),
        name="pool",
    )(got, remainder)


def tower_kernel(bags_ref, weight_ref, cot_ref, gain_ref, pre_ref, out_ref):
    feats = bags_ref.shape[0]
    flat = jnp.concatenate([bags_ref[f] for f in range(feats)], axis=1)
    pre = mm(flat, weight_ref[...])
    pre_ref[...] = pre
    act = (pre * jax.nn.sigmoid(pre)).astype(bf16).astype(f32)
    mean = jnp.mean(act, axis=1, keepdims=True)
    center = act - mean
    scaled = cot_ref[...].astype(f32) * gain_ref[...]
    spread = jnp.sum(center * center, axis=1, keepdims=True)
    total = jnp.sum(scaled, axis=1, keepdims=True)
    lean = jnp.sum(scaled * center, axis=1, keepdims=True)
    lane = lax.broadcasted_iota(jnp.int32, (128, 128), 1)
    table = jnp.where(
        lane == 0, mean, jnp.where(lane == 1, spread, jnp.where(lane == 2, total, lean))
    )
    stats = table.T[:8]
    for d in range(out_ref.shape[0]):
        out_ref[d, 0:4, :] = act[4 * d : 4 * d + 4, :128]
        out_ref[d, 4:8, :] = act[4 * d : 4 * d + 4, 128:]
        out_ref[d, 8:16, :] = stats


def tower_forward(bags, weight, cot, gain, towers):
    return pl.pallas_call(
        tower_kernel,
        out_shape=[
            jax.ShapeDtypeStruct((128, 256), f32),
            jax.ShapeDtypeStruct((towers, 16, 128), f32),
        ],
        compiler_params=pltpu.CompilerParams(vmem_limit_bytes=VMEM_LIMIT),
        name="tower_forward",
    )(bags, weight, cot, gain)


def back_kernel(columns, got_ref, pre_ref, cot_ref, gain_ref, out_ref):
    towers = got_ref.shape[0]
    stats = got_ref[:, 8:16, :]
    sums = jnp.sum(stats, axis=0)
    mean = sums[0:1] * (1.0 / towers)
    shift = stats[:, 0:1, :] - mean[None]
    spread = sums[1:2] + (columns / towers) * jnp.sum(shift * shift, axis=0)
    lean = sums[3:4] + jnp.sum(stats[:, 2:3, :] * shift, axis=0)
    scale = lax.rsqrt(spread * (1.0 / columns) + norm_eps)
    rows = [mean, scale, sums[2:3] * (1.0 / columns), lean * scale * scale * (1.0 / columns)]
    table = jnp.concatenate(rows + [jnp.zeros((124, 128), f32)], axis=0).T
    mean, scale, total, lean = (table[:, i : i + 1] for i in range(4))
    pre = pre_ref[...]
    sigma = jax.nn.sigmoid(pre)
    act = (pre * sigma).astype(bf16).astype(f32)
    scaled = cot_ref[...].astype(f32) * gain_ref[...]
    grad = (scale * (scaled - total - (act - mean) * lean)).astype(bf16).astype(f32)
    pre_grad = (grad * sigma * (1.0 + pre * (1.0 - sigma))).astype(bf16)
    for d in range(out_ref.shape[0]):
        out_ref[d] = pre_grad


def tower_back(got, pre, cot, gain, copies):
    columns = got.shape[0] * pre.shape[1]
    return pl.pallas_call(
        functools.partial(back_kernel, float(columns)),
        out_shape=jax.ShapeDtypeStruct((copies, *pre.shape), bf16),
        compiler_params=pltpu.CompilerParams(vmem_limit_bytes=VMEM_LIMIT),
        name="tower_back",
    )(got, pre, cot, gain)


def weight_kernel(class_ref, bag_ref, mine_ref, other_ref, out_ref):
    zs = mine_ref.shape[0]
    side = class_ref[0]
    total = jnp.zeros(out_ref.shape[1:], f32)
    for z in range(zs):
        total += mm(bag_ref[2 * z + side], mine_ref[z])
        total += mm(bag_ref[2 * z + 1 - side], other_ref[z])
    chunk = total.astype(bf16)
    for d in range(out_ref.shape[0]):
        out_ref[d] = chunk


def weight_part(side, bag_t, mine, other):
    vmem = pl.BlockSpec(memory_space=pltpu.VMEM)
    return pl.pallas_call(
        weight_kernel,
        in_specs=[pl.BlockSpec(memory_space=pltpu.SMEM), vmem, vmem, vmem],
        out_specs=vmem,
        out_shape=jax.ShapeDtypeStruct((mine.shape[0], 128, 256), bf16),
        compiler_params=pltpu.CompilerParams(vmem_limit_bytes=VMEM_LIMIT),
        name="weight_part",
    )(side, bag_t, mine, other)


def rows_kernel(per_step, side_ref, got_ref, weight_ref, quot_ref, rem_ref, grad_ref, qg_ref, rg_ref):
    @pl.when(pl.program_id(0) == 0)
    def _():
        qg_ref[...] = jnp.zeros_like(qg_ref)
        rg_ref[...] = jnp.zeros_like(rg_ref)

    tri = triangles(128)
    quot_sum, rem_sum = qg_ref[...], rg_ref[...]
    for i in range(per_step):
        quot_hot, rem_hot, member = masks(got_ref[i, 0, 16:32, :], tri)
        bag_grad = mm_nt(weight_ref[...], grad_ref[i]).astype(bf16)
        look = mm(bag_grad, member)
        quot_part = (look * rem_ref[i, 0].astype(f32)).astype(bf16)
        rem_part = (look * quot_ref[i, 0].astype(f32)).astype(bf16)
        quot_sum += mm_nt(quot_hot, quot_part)
        rem_sum += mm_nt(rem_hot, rem_part)
    qg_ref[...] = quot_sum
    rg_ref[...] = rem_sum


def rows_part(side, got, weight, quot, rem, grad):
    zs, per_step = grad.shape[0], 4
    pair = lambda a: a.reshape(zs, 2, *a.shape[1:])
    block = lambda *dims: pl.BlockSpec((per_step, 1, *dims), lambda i, s: (i, s[0], 0, 0))
    whole = lambda *dims: pl.BlockSpec(dims, lambda i, s: (0, 0))
    return pl.pallas_call(
        functools.partial(rows_kernel, per_step),
        grid_spec=pltpu.PrefetchScalarGridSpec(
            num_scalar_prefetch=1,
            grid=(zs // per_step,),
            in_specs=[
                block(32, 128),
                whole(128, 256),
                block(128, 512),
                block(128, 512),
                pl.BlockSpec((per_step, 128, 256), lambda i, s: (i, 0, 0)),
            ],
            out_specs=[whole(256, 128), whole(128, 128)],
        ),
        out_shape=[jax.ShapeDtypeStruct((256, 128), f32), jax.ShapeDtypeStruct((128, 128), f32)],
        compiler_params=pltpu.CompilerParams(vmem_limit_bytes=VMEM_LIMIT),
        name="rows_part",
    )(side, pair(got), weight, pair(quot), pair(rem), grad)


def layer_norm(values, gain):
    center = values - jnp.mean(values, axis=-1, keepdims=True)
    spread = jnp.mean(center * center, axis=-1, keepdims=True)
    return center * lax.rsqrt(spread + norm_eps) * gain


def on_device(
    quotient_rows,
    remainder_rows,
    quotient_index,
    remainder_index,
    bag_sizes,
    tower_weight,
    norm_gain,
    cotangent,
):
    feats = quotient_rows.shape[0]
    shards, towers = lax.axis_size("shard"), lax.axis_size("tower")
    shard, tower = lax.axis_index("shard"), lax.axis_index("tower")
    zs = shards // 2
    along_z = [[2 * z + c for z in range(zs)] for c in range(2)]
    across = [(i, i ^ 1) for i in range(shards)]
    swap = functools.partial(lax.all_to_all, split_axis=0, concat_axis=0, tiled=True)
    gather_z = functools.partial(swap, axis_name="shard", axis_index_groups=along_z)
    side = (shard % 2).astype(jnp.int32)
    side_arg = side[None]

    picks = jnp.concatenate(
        [
            quotient_index.reshape(feats, 4, 128),
            remainder_index.reshape(feats, 4, 128),
            bag_sizes.reshape(feats, 1, 128),
            jnp.zeros((feats, 7, 128), jnp.int32),
        ],
        axis=1,
    ).astype(bf16)
    got = swap(jnp.concatenate([quotient_rows, picks], axis=1), "shard")
    cot = lax.all_to_all(cotangent[0], "tower", split_axis=1, concat_axis=0, tiled=True)
    gain = norm_gain.astype(f32)
    gain_here = lax.dynamic_slice(gain, (tower * 256,), (256,))[None]
    remainder = lax.dynamic_index_in_dim(remainder_rows, shard, 0, keepdims=False)
    weight = tower_weight[0]
    weight_here = lax.dynamic_slice(weight, (shard * 128, 0), (128, 256))

    bag, bag_t, quot, rem = pool(got, remainder)
    bags = swap(bag, "shard")
    pre, sent = tower_forward(bags, weight, cot, gain_here, towers)
    stats = swap(sent, "tower")
    grad_copies = tower_back(stats, pre, cot, gain_here, zs)
    grad_mine = gather_z(grad_copies)
    grad_other = lax.ppermute(grad_mine, "shard", across)

    joined = stats[:, :8].reshape(towers, 2, 4, 128).transpose(2, 0, 1, 3).reshape(4, towers * 256)
    joint = layer_norm(joined, gain).astype(bf16)[None]

    chunk_copies = weight_part(side_arg, bag_t, grad_mine, grad_other)
    chunks_mine = gather_z(chunk_copies)
    quot_a, rem_a = rows_part(side_arg, got, weight_here, quot, rem, grad_mine)
    quot_b, rem_b = rows_part(1 - side_arg, got, weight_here, quot, rem, grad_other)
    rows = jnp.concatenate(
        [(quot_a + quot_b).reshape(shards, 16, 128), (rem_a + rem_b).reshape(shards, 8, 128)], axis=1
    )
    owned = swap(rows, "shard")
    chunks_other = lax.ppermute(chunks_mine, "shard", across)
    even = jnp.where(side == 0, chunks_mine, chunks_other)
    odd = jnp.where(side == 0, chunks_other, chunks_mine)
    weight_grad = jnp.stack([even, odd], axis=1).reshape(1, feats * 128, 256).astype(f32)
    return joint, weight_grad, owned[:, :16], owned[:, 16:]


def solution(mesh):
    in_specs = (
        P("tower", "shard", None),
        P("tower", None, None),
        P("tower", "shard", None),
        P("tower", "shard", None),
        P("tower", "shard", None),
        P("tower", None, None),
        P(),
        P("shard", "tower", None),
    )
    out_specs = (
        P("shard", "tower", None),
        P("tower", None, None),
        P("tower", "shard", None),
        P("tower", "shard", None),
    )
    return jax.shard_map(
        on_device, mesh=mesh, in_specs=in_specs, out_specs=out_specs, check_vma=False
    )
```

time: 352 us -> 160 us (0.45)
  waiting for transfers between devices: 275 us -> 26.9 us
  blocking collectives: 12 us -> 60 us
  matrix products: 28.4 us -> 0 us
  starting transfers between devices: 9.51 us -> 29 us
  Pallas kernels: 0 us -> 18.5 us
  between operations: 13.9 us -> 0.88 us
  local copies, waits for them, and re-layouts: 7.26 us -> 15.4 us
  other arithmetic: 3.39 us -> 8.47 us
    reduce_scatter x2 -> x0, waiting for transfers between devices: 125 us -> none  [the longest x1 64 us: on_device(): lax.psum_scatter(quot_parts, 'shard', scatter_dimension=1, tiled=True)]
    psum x1 -> x0, waiting for transfers between devices: 98.5 us -> none  [on_device(): weight_grad = lax.psum(weight_part, 'shard')[None]]
    all_to_all x1 -> x3, blocking collectives: 12 us -> 60 us  [the longest x1 21 us: on_device(): stats = swap(sent, 'tower')]
    all_gather x1 -> x0, waiting for transfers between devices: 41.6 us -> none  [on_device(): all_rows = lax.all_gather(quotient_rows, 'shard', axis=1, tiled=True)]
    dot_general x9 -> x0, matrix products: 28.4 us -> none  [the longest x1 8.52 us: on_device(): jnp.einsum('flq,flw->fqw', quot_hot.astype(jnp.float32), lookup_grad * re...]
    pallas_call x0 -> x6, Pallas kernels: none -> 18.5 us  [the longest x2 9.98 us: rows_part(): pl.pallas_call(functools.partial(rows_kernel, per_step), grid_spec=pltpu....]
    all_to_all x1 -> x4, waiting for transfers between devices: 8.73 us -> 26.9 us  [the longest x1 16.6 us: on_device(): bags = swap(bag, 'shard')]
    all_to_all x1 -> x4, starting transfers between devices: 9.17 us -> 22.5 us  [the longest x1 9.67 us: on_device(): lax.all_to_all(cotangent[0], 'tower', split_axis=1, concat_axis=0, tiled=...]
  transfers between devices with their start and end apart: 5 -> 6, of which waited for: 5 -> 3; matrix products, arithmetic and copies ran while one was open for 6% -> 5% of each run, Pallas kernels for 0% -> 10%
where the time goes in v1:
time: 160 us; the launch traced here: 159 us
  blocking collectives  60 us (38%)
  starting transfers between devices  29 us (18%)
  waiting for transfers between devices  26.9 us (17%)
  Pallas kernels  18.5 us (12%)
  local copies, waits for them, and re-layouts  15.4 us (10%)
  other arithmetic  8.47 us (5%)
    all_to_all x1, blocking collectives, on_device(): stats = swap(sent, 'tower')  21 us
    all_to_all x1, blocking collectives, on_device(): got = swap(jnp.concatenate([quotient_rows, picks], axis=1), 'shard')  20.8 us
    all_to_all x1, blocking collectives, on_device(): grad_mine = gather_z(grad_copies)  18.2 us
    all_to_all x1, waiting for transfers between devices, on_device(): bags = swap(bag, 'shard')  16.6 us
    pallas_call x2, Pallas kernels, rows_part(): pl.pallas_call(functools.partial(rows_kernel, per_step), grid_spec=pltpu....  9.98 us
    all_to_all x1, starting transfers between devices, on_device(): lax.all_to_all(cotangent[0], 'tower', split_axis=1, concat_axis=0, tiled=...  9.67 us
    unnamed x28, local copies, waits for them, and re-layouts  9.29 us
    all_to_all x1, waiting for transfers between devices, on_device(): owned = swap(rows, 'shard')  7.55 us
  transfers between devices with their start and end apart: 6, of which 3 were waited for; matrix products, arithmetic and copies ran while one was open for 5% of the time, Pallas kernels for 10%

profile of v1, /device:TPU:1, one launch (start us, length us, event | category | flops | bytes accessed | tf_op | source)
XLA Modules:
  0.0 159.2 jit_solution(4094516789429466396)
XLA Ops:
  1.4 0.8 convert_reduce_fusion.1
  2.3 0.8 convert_reduce_fusion
  3.2 0.9 concatenate.9
  4.1 20.8 %all_to_all.49.got_ref = bf16[16,32,128]{2,1,0:T(8,128)(2,1)S(1)} all-to-all(bf16[16,32,128]{2,1,0:T(8,128)(2,1)S(1)} %concatenate.9), channel_id=1, replica_groups=mesh['tower'=32,'shard'=16] {'shard'}, dimensions={0} | all-to-all | bytes 262144 | tf_op jit(solution)/shard_map/all_to_all | solution.py:266
  24.9 9.7 %all-to-all-start.2 = ((bf16[4,32,256]{2,0,1:T(4,128)(2,1)}), bf16[4,32,256]{2,0,1:T(4,128)(2,1)S(1)}, u32[]{:S(2)}, u32[]{:S(2)}) async-start(bf16[4,32,256]{2,0,1:T(4,128)(2,1)} %bitcast.39), calls=%async_computation.2 | async-start | bytes 131072 | tf_op jit(solution)/shard_map/all_to_all | solution.py:267
  34.6 6.2 %pool.1 = (bf16[16,128,128]{2,1,0:T(8,128)(2,1)S(1)}, bf16[16,128,128]{2,1,0:T(8,128)(2,1)S(1)}, bf16[16,128,512]{2,1,0:T(8,128)(2,1)S(1)}, bf16[16,128,512]{2,1,0:T(8,128)(2,1)S(1)}) custom-call(bf16[16,32,128]{2,1,0:T(8,128)(2,1)S(1)} %all_to_all.49.got_ref, bf16[128,128]{1,0:T(8,128)(2,1)S(1)} %dynamic-slice_bitcast_fusion.1.rem_ref), custom_call_target="tpu_custom_call" | custom-call | tf_op jit(solution)/shard_map/pool/pallas_call | solution.py:79
  40.8 1.3 copy-done.1
  42.1 0.8 copy-done.9
  43.8 4.3 %all-to-all-start.1 = ((bf16[16,128,128]{2,1,0:T(8,128)(2,1)}), bf16[16,128,128]{2,1,0:T(8,128)(2,1)S(1)}, u32[]{:S(2)}, u32[]{:S(2)}) async-start(bf16[16,128,128]{2,1,0:T(8,128)(2,1)} %copy-done.11), calls=%async_computation.1 | async-start | bytes 1048576 | tf_op jit(solution)/shard_map/all_to_all | solution.py:275
  48.9 16.6 %all-to-all-done.1.bags_ref = bf16[16,128,128]{2,1,0:T(8,128)(2,1)S(1)} async-done(((bf16[16,128,128]{2,1,0:T(8,128)(2,1)}), bf16[16,128,128]{2,1,0:T(8,128)(2,1)S(1)}, u32[]{:S(2)}, u32[]{:S(2)}) %all-to-all-start.1) | async-done | bytes 524320 | tf_op jit(solution)/shard_map/all_to_all | solution.py:275
  65.4 1.2 copy-done.4
  67.2 21.0 %all_to_all.50.got_ref = f32[32,16,128]{2,1,0:T(8,128)S(1)} all-to-all(f32[32,16,128]{2,1,0:T(8,128)S(1)} %get-tuple-element.15), channel_id=1, replica_groups=mesh['tower'=32,'shard'=16] {'tower'}, dimensions={0} | all-to-all | bytes 524288 | tf_op jit(solution)/shard_map/all_to_all | solution.py:277
  88.2 0.8 copy-done.8
  89.3 18.2 %all_to_all.51.mine_ref.grad_ref = bf16[8,128,256]{2,1,0:T(8,128)(2,1)S(1)} all-to-all(bf16[8,128,256]{2,1,0:T(8,128)(2,1)S(1)} %tower_back.1), channel_id=1, replica_groups={{0,2,4,6,8,10,12,14},{1,3,5,7,9,11,13,15},{16,18,20,22,24,26,28,30},{17..., dimensions={0} | all-to-all | bytes 1048576 | tf_op jit(solution)/shard_map/all_to_all | solution.py:279
  107.6 4.5 %collective-permute-start = (bf16[8,128,256]{2,1,0:T(8,128)(2,1)S(1)}, bf16[8,128,256]{2,1,0:T(8,128)(2,1)}, u32[]{:S(2)}, u32[]{:S(2)}) collective-permute-start(bf16[8,128,256]{2,1,0:T(8,128)(2,1)S(1)} %all_to_all.51.mine_ref.grad_ref), channel_id=1, source_target_pairs={{0,1},{1,0},{2,3},{3,2},{4,5},{5,4},{6,7},{7,6},{8,9},{9,8},{10,11... | collective-permute-start | bytes 1572872 | tf_op jit(solution)/shard_map/ppermute | solution.py:280
  112.1 1.3 convert_element_type.28
  113.5 1.5 dynamic-slice_bitcast_fusion.weight_ref
  114.9 1.0 copy-done.10
  116.0 1.5 weight_part.1
  117.5 0.8 copy-done.3
  118.3 4.1 %all-to-all-start.5 = ((bf16[8,128,256]{2,1,0:T(8,128)(2,1)}), bf16[8,128,256]{2,1,0:T(8,128)(2,1)}, u32[]{:S(2)}, u32[]{:S(2)}) async-start(bf16[8,128,256]{2,1,0:T(8,128)(2,1)} %copy-done.3), calls=%async_computation.5 | async-start | bytes 1048576 | tf_op jit(solution)/shard_map/all_to_all | solution.py:286
  123.3 1.2 multiply_reduce_fusion
  124.5 1.6 copy-done.2
  126.1 0.8 copy-done.5
  126.9 4.5 %rows_part.2 = (f32[256,128]{1,0:T(8,128)S(1)}, f32[128,128]{1,0:T(8,128)S(1)}) custom-call(s32[1]{0:T(128)} %bitcast.9.class_ref.side_ref, bf16[8,2,32,128]{3,2,1,0:T(8,128)(2,1)S(1)} %bitcast.29, bf16[128,256]{1,0:T(8,128)(2,1)S(1)} %copy-done.5, bf16[8,2,128,512]{3,2,1,0:T(8,128)(2,1)S(1)} %bitcast.25, bf16[8,2,128,512]{3,2,1,0:T(8,128)(2,1)S(1)} %bitcast.27, ...), custom_call_target="tpu_custom_call" | custom-call | tf_op jit(solution)/shard_map/rows_part/pallas_call | solution.py:210
  131.5 5.4 %rows_part.3 = (f32[256,128]{1,0:T(8,128)S(1)}, f32[128,128]{1,0:T(8,128)S(1)}) custom-call(s32[1]{0:T(128)S(6)} %sub.27.side_ref, bf16[8,2,32,128]{3,2,1,0:T(8,128)(2,1)S(1)} %bitcast.30, bf16[128,256]{1,0:T(8,128)(2,1)S(1)} %copy-done.6, bf16[8,2,128,512]{3,2,1,0:T(8,128)(2,1)S(1)} %bitcast.26, bf16[8,2,128,512]{3,2,1,0:T(8,128)(2,1)S(1)} %bitcast.28, ...), custom_call_target="tpu_custom_call" | custom-call | tf_op jit(solution)/shard_map/rows_part/pallas_call | solution.py:210
  137.7 2.8 %all-to-all-done.5 = bf16[8,128,256]{2,1,0:T(8,128)(2,1)} async-done(((bf16[8,128,256]{2,1,0:T(8,128)(2,1)}), bf16[8,128,256]{2,1,0:T(8,128)(2,1)}, u32[]{:S(2)}, u32[]{:S(2)}) %all-to-all-start.5) | async-done | bytes 524320 | tf_op jit(solution)/shard_map/all_to_all | solution.py:286
  140.5 4.3 %all-to-all-start.6 = ((f32[16,24,128]{2,1,0:T(8,128)}), f32[16,24,128]{2,1,0:T(8,128)S(1)}, u32[]{:S(2)}, u32[]{:S(2)}) async-start(f32[16,24,128]{2,1,0:T(8,128)} %pad_maximum_fusion), calls=%async_computation.6 | async-start | bytes 393216 | tf_op jit(solution)/shard_map/all_to_all | solution.py:292
  144.8 2.0 %collective-permute-start.1 = (bf16[8,128,256]{2,1,0:T(8,128)(2,1)}, bf16[8,128,256]{2,1,0:T(8,128)(2,1)S(1)}, u32[]{:S(2)}, u32[]{:S(2)}) collective-permute-start(bf16[8,128,256]{2,1,0:T(8,128)(2,1)} %all-to-all-done.5), channel_id=1, source_target_pairs={{0,1},{1,0},{2,3},{3,2},{4,5},{5,4},{6,7},{7,6},{8,9},{9,8},{10,11... | collective-permute-start | bytes 1572872 | tf_op jit(solution)/shard_map/ppermute | solution.py:293
  147.6 7.6 %all-to-all-done.6 = f32[16,24,128]{2,1,0:T(8,128)S(1)} async-done(((f32[16,24,128]{2,1,0:T(8,128)}), f32[16,24,128]{2,1,0:T(8,128)S(1)}, u32[]{:S(2)}, u32[]{:S(2)}) %all-to-all-start.6) | async-done | bytes 196640 | tf_op jit(solution)/shard_map/all_to_all | solution.py:292
  156.4 1.1 select_bitcast_fusion.1
  157.7 1.5 copy.16
  (44 shorter events, 7.1 us)
Async XLA Ops:
  0.6 33.9 %copy-start = (bf16[16,128,128]{2,1,0:T(8,128)(2,1)S(1)}, bf16[16,128,128]{2,1,0:T(8,128)(2,1)}, u32[]{:S(2)}) copy-start(bf16[16,128,128]{2,1,0:T(8,128)(2,1)} %param.9) | copy-start | bytes 1572868
  24.9 18.9 %all-to-all-start.2 = ((bf16[4,32,256]{2,0,1:T(4,128)(2,1)}), bf16[4,32,256]{2,0,1:T(4,128)(2,1)S(1)}, u32[]{:S(2)}, u32[]{:S(2)}) async-start(bf16[4,32,256]{2,0,1:T(4,128)(2,1)} %bitcast.39), calls=%async_computation.2 | async-start | bytes 131072 | tf_op jit(solution)/shard_map/all_to_all | solution.py:267
  40.8 1.3 copy-start.1
  42.1 0.8 copy-start.9
  42.9 0.8 copy-start.11
  43.8 21.7 %all-to-all-start.1 = ((bf16[16,128,128]{2,1,0:T(8,128)(2,1)}), bf16[16,128,128]{2,1,0:T(8,128)(2,1)S(1)}, u32[]{:S(2)}, u32[]{:S(2)}) async-start(bf16[16,128,128]{2,1,0:T(8,128)(2,1)} %copy-done.11), calls=%async_computation.1 | async-start | bytes 1048576 | tf_op jit(solution)/shard_map/all_to_all | solution.py:275
  48.9 18.3 %copy-start.7 = (bf16[128,256]{1,0:T(8,128)(2,1)}, bf16[128,256]{1,0:T(8,128)(2,1)S(1)}, u32[]{:S(2)}) copy-start(bf16[128,256]{1,0:T(8,128)(2,1)S(1)} %all_to_all.37.cot_ref) | copy-start | bytes 196612
  65.4 1.2 copy-start.4
  88.2 0.8 copy-start.8
  107.6 7.4 %collective-permute-start = (bf16[8,128,256]{2,1,0:T(8,128)(2,1)S(1)}, bf16[8,128,256]{2,1,0:T(8,128)(2,1)}, u32[]{:S(2)}, u32[]{:S(2)}) collective-permute-start(bf16[8,128,256]{2,1,0:T(8,128)(2,1)S(1)} %all_to_all.51.mine_ref.grad_ref), channel_id=1, source_target_pairs={{0,1},{1,0},{2,3},{3,2},{4,5},{5,4},{6,7},{7,6},{8,9},{9,8},{10,11... | collective-permute-start | bytes 1572872 | tf_op jit(solution)/shard_map/ppermute | solution.py:280
  114.9 1.0 copy-start.10
  117.4 0.8 copy-start.3
  118.3 22.2 %all-to-all-start.5 = ((bf16[8,128,256]{2,1,0:T(8,128)(2,1)}), bf16[8,128,256]{2,1,0:T(8,128)(2,1)}, u32[]{:S(2)}, u32[]{:S(2)}) async-start(bf16[8,128,256]{2,1,0:T(8,128)(2,1)} %copy-done.3), calls=%async_computation.5 | async-start | bytes 1048576 | tf_op jit(solution)/shard_map/all_to_all | solution.py:286
  124.5 1.6 %copy-start.2 = (bf16[16,128,512]{2,1,0:T(8,128)(2,1)S(1)}, bf16[16,128,512]{2,1,0:T(8,128)(2,1)}, u32[]{:S(2)}) copy-start(bf16[16,128,512]{2,1,0:T(8,128)(2,1)} %copy-done.1) | copy-start | bytes 6291460
  126.1 0.8 copy-start.5
  126.9 4.6 %copy-start.6 = (bf16[128,256]{1,0:T(8,128)(2,1)S(1)}, bf16[128,256]{1,0:T(8,128)(2,1)}, u32[]{:S(2)}) copy-start(bf16[128,256]{1,0:T(8,128)(2,1)} %dynamic-slice_bitcast_fusion.weight_ref) | copy-start | bytes 196612
  131.5 15.3 %copy-start.12 = (f32[32,8,128]{2,1,0:T(8,128)S(1)}, f32[32,8,128]{2,1,0:T(8,128)}, u32[]{:S(2)}) copy-start(f32[32,8,128]{2,1,0:T(8,128)} %get-tuple-element.27) | copy-start | bytes 393220
  131.5 15.3 %copy-start.13 = (f32[8192]{0:T(1024)S(1)}, f32[8192]{0:T(1024)}, u32[]{:S(2)}) copy-start(f32[8192]{0:T(1024)} %convert_element_type.28) | copy-start | bytes 98308
  140.5 14.7 %all-to-all-start.6 = ((f32[16,24,128]{2,1,0:T(8,128)}), f32[16,24,128]{2,1,0:T(8,128)S(1)}, u32[]{:S(2)}, u32[]{:S(2)}) async-start(f32[16,24,128]{2,1,0:T(8,128)} %pad_maximum_fusion), calls=%async_computation.6 | async-start | bytes 393216 | tf_op jit(solution)/shard_map/all_to_all | solution.py:292
  144.8 11.6 %collective-permute-start.1 = (bf16[8,128,256]{2,1,0:T(8,128)(2,1)}, bf16[8,128,256]{2,1,0:T(8,128)(2,1)S(1)}, u32[]{:S(2)}, u32[]{:S(2)}) collective-permute-start(bf16[8,128,256]{2,1,0:T(8,128)(2,1)} %all-to-all-done.5), channel_id=1, source_target_pairs={{0,1},{1,0},{2,3},{3,2},{4,5},{5,4},{6,7},{7,6},{8,9},{9,8},{10,11... | collective-permute-start | bytes 1572872 | tf_op jit(solution)/shard_map/ppermute | solution.py:293

commit v2 on v0

v2 whole, which is shorter than its diff:
```python
import functools

import jax
import jax.numpy as jnp
from jax import lax
from jax.experimental import pallas as pl
from jax.experimental.pallas import tpu as pltpu
from jax.sharding import PartitionSpec as P

norm_eps = 1e-05
f32, bf16 = jnp.float32, jnp.bfloat16
NT = (((1,), (1,)), ((), ()))
PARAMS = pltpu.CompilerParams(vmem_limit_bytes=20 * 1024 * 1024)
vmem = pl.BlockSpec(memory_space=pltpu.VMEM)
smem = pl.BlockSpec(memory_space=pltpu.SMEM)


def mm(a, b):
    return jnp.dot(a, b, preferred_element_type=f32)


def mm_nt(a, b):
    return lax.dot_general(a, b, NT, preferred_element_type=f32)


def cost(micros):
    return pl.CostEstimate(
        flops=int(micros * 1e8), bytes_accessed=int(micros * 3e6), transcendentals=0
    )


def triangles(n):
    row = lax.broadcasted_iota(jnp.int32, (n, n), 0)
    col = lax.broadcasted_iota(jnp.int32, (n, n), 1)
    upto = jnp.where(col <= row, 1.0, 0.0).astype(bf16)
    before = jnp.where(col < row, 1.0, 0.0).astype(bf16)
    return jnp.concatenate([upto, before], axis=0)


def masks(picks, side, tri):
    values = picks.astype(jnp.int32)
    row_q = lax.broadcasted_iota(jnp.int32, (256, 128), 0)
    row_r = lax.broadcasted_iota(jnp.int32, (128, 128), 0)
    lane = lax.broadcasted_iota(jnp.int32, (128, 128), 1).astype(f32)
    place = ((((values >> 4) & 1) ^ side) << 7) + ((values >> 5) << 4) + (values & 15)
    sums = mm_nt(tri, picks)
    ends = jnp.broadcast_to(sums[:128, 8:9], (128, 128))
    starts = jnp.broadcast_to(sums[128:, 8:9], (128, 128))
    quot, rem, member = [], [], []
    for c in range(4):
        quot.append(jnp.where(row_q == place[c : c + 1], 1.0, 0.0).astype(bf16))
        rem.append(jnp.where(row_r == values[4 + c : 5 + c], 1.0, 0.0).astype(bf16))
        here = lane + float(128 * c)
        inside = (here < ends) & (here >= starts)
        member.append(jnp.where(inside, 1.0, 0.0).astype(bf16))
    return tuple(jnp.concatenate(v, axis=1) for v in (quot, rem, member))


def look_up(quot_t, rem_t, quot_hot, rem_hot, member):
    quot = mm(quot_t, quot_hot)
    rem = mm(rem_t, rem_hot)
    composed = quot * rem
    high = composed.astype(bf16)
    low = (composed - high.astype(f32)).astype(bf16)
    return quot, rem, mm_nt(member, high) + mm_nt(member, low)


def pack_kernel(rows_ref, quot_ref, rem_ref, size_ref, out_ref, picks_ref, held):
    feats = rows_ref.shape[0]
    held[...] = jnp.zeros_like(held)
    for f in range(feats):
        for c in range(4):
            part = pl.ds(128 * c, 128)
            held[f, c : c + 1, :] = quot_ref[f, :, part].astype(f32)
            held[f, 4 + c : 5 + c, :] = rem_ref[f, :, part].astype(f32)
        held[f, 8:9, :] = size_ref[f].astype(f32)
    picks = held[...].astype(bf16)
    picks_ref[...] = picks
    rows = rows_ref[...]
    for z in range(out_ref.shape[0]):
        out_ref[z, :feats] = rows
        out_ref[z, feats:] = picks[2 * z : 2 * z + 2]


def pack(rows, quot, rem, sizes):
    feats, zs = rows.shape[0], rows.shape[0] // 2
    whole = lambda a: pl.BlockSpec(a.shape, lambda i: (0, 0, 0))
    pinned = [pltpu.with_memory_space_constraint(a, pltpu.HBM) for a in (rows, quot, rem, sizes)]
    return pl.pallas_call(
        pack_kernel,
        grid=(1,),
        in_specs=[whole(a) for a in pinned],
        out_specs=[
            pl.BlockSpec((zs, feats + 2, 16, 128), lambda i: (0, 0, 0, 0)),
            pl.BlockSpec((feats, 16, 128), lambda i: (0, 0, 0)),
        ],
        out_shape=[
            jax.ShapeDtypeStruct((zs, feats + 2, 16, 128), bf16),
            jax.ShapeDtypeStruct((feats, 16, 128), bf16),
        ],
        scratch_shapes=[pltpu.VMEM((feats, 16, 128), f32)],
        compiler_params=PARAMS,
        cost_estimate=cost(1),
        name="pack",
    )(*pinned)


def tower_kernel(side_ref, mine_ref, other_ref, rem_ref, picks_ref, weight_ref, pre_ref, out_ref, held, sem):
    fetch = pltpu.make_async_copy(weight_ref.at[0], held, sem)
    fetch.start()
    tri = triangles(128)
    side = side_ref[0]
    bags = []
    for f in range(rem_ref.shape[0]):
        table = jnp.concatenate(
            [mine_ref[:, f].reshape(128, 128), other_ref[:, f].reshape(128, 128)], axis=0
        )
        _, _, pooled = look_up(table.T, rem_ref[f].T, *masks(picks_ref[f], side, tri))
        bags.append(pooled.astype(bf16))
    fetch.wait()
    pre = mm(jnp.concatenate(bags, axis=1), held[...])
    pre_ref[...] = pre
    act = pre * jax.nn.sigmoid(pre)
    for d in range(out_ref.shape[0]):
        out_ref[d] = act[4 * d : 4 * d + 4].astype(bf16)


def tower_forward(side, mine, other, remainder, picks, weight, towers):
    return pl.pallas_call(
        tower_kernel,
        in_specs=[smem] + [vmem] * 4 + [pl.BlockSpec(memory_space=pltpu.HBM)],
        out_specs=[vmem] * 2,
        out_shape=[
            jax.ShapeDtypeStruct((128, 256), f32),
            jax.ShapeDtypeStruct((towers, 4, 256), bf16),
        ],
        scratch_shapes=[pltpu.VMEM(weight.shape[1:], bf16), pltpu.SemaphoreType.DMA],
        compiler_params=PARAMS,
        cost_estimate=cost(6),
        name="tower_forward",
    )(side, mine, other, remainder, picks, pltpu.with_memory_space_constraint(weight, pltpu.HBM))


def norm_kernel(got_ref, cot_ref, gain_ref, joint_ref, out_ref):
    towers, _, width = got_ref.shape
    columns = float(towers * width)
    part = [pl.ds(width * t, width) for t in range(towers)]
    mean = sum(got_ref[t].astype(f32) for t in range(towers))
    mean = jnp.sum(mean, axis=1, keepdims=True) * (1.0 / columns)
    center = [got_ref[t].astype(f32) - mean for t in range(towers)]
    spread = jnp.sum(sum(c * c for c in center), axis=1, keepdims=True) * (1.0 / columns)
    scale = lax.rsqrt(spread + norm_eps)
    total, lean = 0.0, 0.0
    for t in range(towers):
        gain = gain_ref[:, part[t]]
        scaled = cot_ref[0, :, part[t]].astype(f32) * gain
        joint_ref[0, :, part[t]] = (center[t] * scale * gain).astype(bf16)
        total += scaled
        lean += scaled * center[t]
    total = jnp.sum(total, axis=1, keepdims=True) * (1.0 / columns)
    lean = jnp.sum(lean, axis=1, keepdims=True) * (1.0 / columns) * scale * scale
    for t in range(towers):
        scaled = cot_ref[0, :, part[t]].astype(f32) * gain_ref[:, part[t]]
        out_ref[t] = (scale * (scaled - total - center[t] * lean)).astype(bf16)


def norm(got, cot, gain):
    return pl.pallas_call(
        norm_kernel,
        out_shape=[
            jax.ShapeDtypeStruct(cot.shape, bf16),
            jax.ShapeDtypeStruct(got.shape, bf16),
        ],
        compiler_params=PARAMS,
        cost_estimate=cost(1),
        name="norm",
    )(got, cot, gain)


def own_tables(own, mine_ref, other_ref, rem_ref):
    quot_t = jnp.concatenate([r[:, own].reshape(128, 128).T for r in (mine_ref, other_ref)], axis=1)
    return quot_t, rem_ref[own].T


def feature_kernel(where_ref, mine_ref, other_ref, rem_ref, bag_ref):
    feats, zs = rem_ref.shape[0], mine_ref.shape[0]
    own, side = where_ref[0], where_ref[1]
    tables = own_tables(own, mine_ref, other_ref, rem_ref)
    tri = triangles(128)

    def body(z, carry):
        for half, ref in enumerate((mine_ref, other_ref)):
            _, _, pooled = look_up(*tables, *masks(ref[z, feats + side], side, tri))
            bag_ref[half, z] = pooled.T.astype(bf16)
        return carry

    lax.fori_loop(0, zs, body, 0, unroll=2)


def feature_pool(where, mine, other, remainder):
    return pl.pallas_call(
        feature_kernel,
        in_specs=[smem] + [vmem] * 3,
        out_specs=vmem,
        out_shape=jax.ShapeDtypeStruct((2, mine.shape[0], 128, 128), bf16),
        compiler_params=PARAMS,
        cost_estimate=cost(6),
        name="feature_pool",
    )(where, mine, other, remainder)


def back_kernel(got_ref, pre_ref, out_ref, held):
    for d in range(got_ref.shape[0]):
        held[4 * d : 4 * d + 4] = got_ref[d].astype(f32)
    pre = pre_ref[...]
    sigma = jax.nn.sigmoid(pre)
    pre_grad = (held[...] * sigma * (1.0 + pre * (1.0 - sigma))).astype(bf16)
    for d in range(out_ref.shape[0]):
        out_ref[d] = pre_grad


def tower_back(got, pre, copies):
    return pl.pallas_call(
        back_kernel,
        out_shape=jax.ShapeDtypeStruct((copies, *pre.shape), bf16),
        scratch_shapes=[pltpu.VMEM(pre.shape, f32)],
        compiler_params=PARAMS,
        cost_estimate=cost(1),
        name="tower_back",
    )(got, pre)


def weight_kernel(bag_ref, mine_ref, other_ref, out_ref):
    total = jnp.zeros(out_ref.shape[1:], f32)
    for z in range(mine_ref.shape[0]):
        total += mm(bag_ref[0, z], mine_ref[z]) + mm(bag_ref[1, z], other_ref[z])
    chunk = total.astype(bf16)
    for d in range(out_ref.shape[0]):
        out_ref[d] = chunk


def weight_part(bag_t, mine, other):
    return pl.pallas_call(
        weight_kernel,
        out_shape=jax.ShapeDtypeStruct((mine.shape[0], 128, 256), bf16),
        compiler_params=PARAMS,
        cost_estimate=cost(1),
        name="weight_part",
    )(bag_t, mine, other)


def rows_kernel(where_ref, grad_mine_ref, grad_other_ref, weight_ref, mine_ref, other_ref, rem_ref, out_ref):
    feats, zs = rem_ref.shape[0], mine_ref.shape[0]
    own, side = where_ref[0], where_ref[1]
    weight = weight_ref[0, pl.ds(pl.multiple_of(own * 128, 128), 128), :]
    quot_t, rem_t = own_tables(own, mine_ref, other_ref, rem_ref)
    tri = triangles(128)

    def body(z, carry):
        quot_sum, rem_sum = carry
        for ref, got in ((grad_mine_ref, mine_ref), (grad_other_ref, other_ref)):
            quot_hot, rem_hot, member = masks(got[z, feats + side], side, tri)
            look = mm(mm_nt(weight, ref[z]).astype(bf16), member)
            quot_part = (look * mm(rem_t, rem_hot)).astype(bf16)
            rem_part = (look * mm(quot_t, quot_hot)).astype(bf16)
            quot_sum += mm_nt(quot_part, quot_hot)
            rem_sum += mm_nt(rem_part, rem_hot)
        return quot_sum, rem_sum

    start = jnp.zeros((128, 256), f32), jnp.zeros((128, 128), f32)
    quot_sum, rem_sum = lax.fori_loop(0, zs, body, start, unroll=2)
    quot_sum, rem_sum = quot_sum.T, rem_sum.T
    for z in range(zs):
        near = quot_sum[16 * z : 16 * z + 16]
        far = quot_sum[128 + 16 * z : 144 + 16 * z]
        out_ref[2 * z, :16] = jnp.where(side == 0, near, far)
        out_ref[2 * z + 1, :16] = jnp.where(side == 0, far, near)
    for d in range(2 * zs):
        out_ref[d, 16:] = rem_sum[8 * d : 8 * d + 8]


def rows_part(where, grad_mine, grad_other, weight, mine, other, remainder):
    return pl.pallas_call(
        rows_kernel,
        in_specs=[smem] + [vmem] * 6,
        out_specs=vmem,
        out_shape=jax.ShapeDtypeStruct((2 * mine.shape[0], 24, 128), f32),
        compiler_params=PARAMS,
        cost_estimate=cost(8),
        name="rows_part",
    )(where, grad_mine, grad_other, weight, mine, other, remainder)


def widen_kernel(side_ref, mine_ref, other_ref, out_ref):
    side = side_ref[0]
    for z in range(mine_ref.shape[0]):
        out_ref[z, side] = mine_ref[z].astype(f32)
        out_ref[z, 1 - side] = other_ref[z].astype(f32)


def widen(side, mine, other):
    zs, step = mine.shape[0], 2
    block = pl.BlockSpec((step, 128, 256), lambda i: (i, 0, 0))
    return pl.pallas_call(
        widen_kernel,
        grid=(zs // step,),
        in_specs=[smem, block, block],
        out_specs=pl.BlockSpec((step, 2, 128, 256), lambda i: (i, 0, 0, 0)),
        out_shape=jax.ShapeDtypeStruct((zs, 2, 128, 256), f32),
        compiler_params=PARAMS,
        cost_estimate=cost(1),
        name="widen",
    )(side, mine, other)


def on_device(
    quotient_rows,
    remainder_rows,
    quotient_index,
    remainder_index,
    bag_sizes,
    tower_weight,
    norm_gain,
    cotangent,
):
    feats = quotient_rows.shape[0]
    shards, towers = lax.axis_size("shard"), lax.axis_size("tower")
    shard = lax.axis_index("shard")
    zs = shards // 2
    along_z = [[2 * z + c for z in range(zs)] for c in range(2)]
    across = [(i, i ^ 1) for i in range(shards)]
    swap = functools.partial(lax.all_to_all, split_axis=0, concat_axis=0, tiled=True)
    gather_z = functools.partial(swap, axis_name="shard", axis_index_groups=along_z)
    side = (shard & 1).astype(jnp.int32)
    side_arg = side[None]
    where = jnp.stack([shard.astype(jnp.int32), side])
    gain = norm_gain.astype(f32)[None]

    packed, picks = pack(quotient_rows, quotient_index, remainder_index, bag_sizes)
    mine = gather_z(packed)
    other = lax.ppermute(mine, "shard", across)
    pre, act = tower_forward(side_arg, mine, other, remainder_rows, picks, tower_weight, towers)
    joint, joint_grad = norm(swap(act, "tower"), cotangent, gain)
    grad_copies = tower_back(swap(joint_grad, "tower"), pre, zs)
    bag_t = feature_pool(where, mine, other, remainder_rows)
    grad_mine, bag_t = lax.optimization_barrier((gather_z(grad_copies), bag_t))
    grad_other = lax.ppermute(grad_mine, "shard", across)

    chunk_copies = weight_part(bag_t, grad_mine, grad_other)
    rows = rows_part(where, grad_mine, grad_other, tower_weight, mine, other, remainder_rows)
    chunks_mine, rows = lax.optimization_barrier((gather_z(chunk_copies), rows))
    owned = swap(rows, "shard")
    chunks_other = lax.ppermute(chunks_mine, "shard", across)
    weight_grad = widen(side_arg, chunks_mine, chunks_other).reshape(1, feats * 128, 256)
    owned, weight_grad = lax.optimization_barrier((owned, weight_grad))
    return joint, weight_grad, owned[:, :16], owned[:, 16:]


def solution(mesh):
    in_specs = (
        P("tower", "shard", None),
        P("tower", None, None),
        P("tower", "shard", None),
        P("tower", "shard", None),
        P("tower", "shard", None),
        P("tower", None, None),
        P(),
        P("shard", "tower", None),
    )
    out_specs = (
        P("shard", "tower", None),
        P("tower", None, None),
        P("tower", "shard", None),
        P("tower", "shard", None),
    )
    return jax.shard_map(
        on_device, mesh=mesh, in_specs=in_specs, out_specs=out_specs, check_vma=False
    )
```

time: 352 us -> 144 us (0.41)
  waiting for transfers between devices: 275 us -> 31.2 us
  Pallas kernels: 0 us -> 30.9 us
  matrix products: 28.4 us -> 0 us
  blocking collectives: 12 us -> 40.2 us
  starting transfers between devices: 9.51 us -> 33.3 us
  between operations: 13.9 us -> 0.81 us
    reduce_scatter x2 -> x0, waiting for transfers between devices: 125 us -> none  [the longest x1 64 us: on_device(): lax.psum_scatter(quot_parts, 'shard', scatter_dimension=1, tiled=True)]
    psum x1 -> x0, waiting for transfers between devices: 98.5 us -> none  [on_device(): weight_grad = lax.psum(weight_part, 'shard')[None]]
    all_gather x1 -> x0, waiting for transfers between devices: 41.6 us -> none  [on_device(): all_rows = lax.all_gather(quotient_rows, 'shard', axis=1, tiled=True)]
    pallas_call x0 -> x8, Pallas kernels: none -> 30.9 us  [the longest x1 11.2 us: rows_part(): pl.pallas_call(rows_kernel, in_specs=[smem] + [vmem] * 6, out_specs=vmem,...]
    dot_general x9 -> x0, matrix products: 28.4 us -> none  [the longest x1 8.52 us: on_device(): jnp.einsum('flq,flw->fqw', quot_hot.astype(jnp.float32), lookup_grad * re...]
    all_to_all x1 -> x2, blocking collectives: 12 us -> 40.2 us  [the longest x1 28.2 us: on_device(): mine = gather_z(packed)]
    all_to_all x1 -> x4, waiting for transfers between devices: 8.73 us -> 28.1 us  [the longest x1 8.8 us: on_device(): joint, joint_grad = norm(swap(act, 'tower'), cotangent, gain)]
    ppermute x0 -> x3, starting transfers between devices: none -> 12.6 us  [the longest x1 5.88 us: on_device(): grad_other = lax.ppermute(grad_mine, 'shard', across)]
  transfers between devices with their start and end apart: 5 -> 7, of which waited for: 5 -> 6; matrix products, arithmetic and copies ran while one was open for 6% -> 0% of each run, Pallas kernels for 0% -> 15%
where the time goes in v2:
time: 144 us; the launch traced here: 143 us
  blocking collectives  40.2 us (28%)
  starting transfers between devices  33.3 us (23%)
  waiting for transfers between devices  31.2 us (22%)
  Pallas kernels  30.9 us (21%)
  local copies, waits for them, and re-layouts  6.8 us (5%)
    all_to_all x1, blocking collectives, on_device(): mine = gather_z(packed)  28.2 us
    all_to_all x1, blocking collectives, on_device(): grad_copies = tower_back(swap(joint_grad, 'tower'), pre, zs)  11.9 us
    pallas_call x1, Pallas kernels, rows_part(): pl.pallas_call(rows_kernel, in_specs=[smem] + [vmem] * 6, out_specs=vmem,...  11.2 us
    all_to_all x1, starting transfers between devices, on_device(): joint, joint_grad = norm(swap(act, 'tower'), cotangent, gain)  9.68 us
    all_to_all x1, waiting for transfers between devices, on_device(): joint, joint_grad = norm(swap(act, 'tower'), cotangent, gain)  8.8 us
    pallas_call x1, Pallas kernels, feature_pool(): pl.pallas_call(feature_kernel, in_specs=[smem] + [vmem] * 3, out_specs=vm...  6.79 us
    all_to_all x1, waiting for transfers between devices, on_device(): owned = swap(rows, 'shard')  6.79 us
    all_to_all x1, waiting for transfers between devices, on_device(): grad_mine, bag_t = lax.optimization_barrier((gather_z(grad_copies), bag_t))  6.7 us
  transfers between devices with their start and end apart: 7, of which 6 were waited for; matrix products, arithmetic and copies ran while one was open for 0% of the time, Pallas kernels for 15%

profile of v2, /device:TPU:1, one launch (start us, length us, event | category | flops | bytes accessed | tf_op | source)
XLA Modules:
  0.0 143.2 jit_solution(3141945545286866315)
XLA Ops:
  0.6 1.0 pack.1
  1.7 28.2 %all_to_all.30.mine_ref = bf16[8,18,16,128]{3,2,1,0:T(8,128)(2,1)S(1)} all-to-all(bf16[8,18,16,128]{3,2,1,0:T(8,128)(2,1)S(1)} %get-tuple-element.16), channel_id=1, replica_groups={{0,2,4,6,8,10,12,14},{1,3,5,7,9,11,13,15},{16,18,20,22,24,26,28,30},{17..., dimensions={0} | all-to-all | bytes 1179648 | tf_op jit(solution)/shard_map/all_to_all | solution.py:340
  29.9 4.3 %collective-permute-start = (bf16[8,18,16,128]{3,2,1,0:T(8,128)(2,1)S(1)}, bf16[8,18,16,128]{3,2,1,0:T(8,128)(2,1)S(1)}, u32[]{:S(2)}, u32[]{:S(2)}) collective-permute-start(bf16[8,18,16,128]{3,2,1,0:T(8,128)(2,1)S(1)} %all_to_all.30.mine_ref), channel_id=1, source_target_pairs={{0,1},{1,0},{2,3},{3,2},{4,5},{5,4},{6,7},{7,6},{8,9},{9,8},{10,11... | collective-permute-start | bytes 1769480 | tf_op jit(solution)/shard_map/ppermute | solution.py:341
  34.2 1.6 %collective-permute-done.other_ref = bf16[8,18,16,128]{3,2,1,0:T(8,128)(2,1)S(1)} collective-permute-done((bf16[8,18,16,128]{3,2,1,0:T(8,128)(2,1)S(1)}, bf16[8,18,16,128]{3,2,1,0:T(8,128)(2,1)S(1)}, u32[]{:S(2)}, u32[]{:S(2)}) %collective-permute-start) | collective-permute-done | bytes 589856 | tf_op jit(solution)/shard_map/ppermute | solution.py:341
  35.8 1.0 copy-done
  36.9 6.2 %tower_forward.1 = (f32[128,256]{1,0:T(8,128)S(1)}, bf16[32,4,256]{2,1,0:T(4,128)(2,1)}) custom-call(s32[1]{0:T(128)} %bitcast.side_ref, bf16[8,18,16,128]{3,2,1,0:T(8,128)(2,1)S(1)} %all_to_all.30.mine_ref, bf16[8,18,16,128]{3,2,1,0:T(8,128)(2,1)S(1)} %collective-permute-done.other_ref, bf16[16,128,128]{2,1,0:T(8,128)(2,1)S(1)} %copy-done, ...), custom_call_target="tpu_custom_call" | custom-call | flops 600000000 | bytes 18000000 | tf_op jit(solution)/shard_map/tower_forward/pallas_call | solution.py:129
  43.1 9.7 %all-to-all-start.1 = ((bf16[32,4,256]{2,1,0:T(4,128)(2,1)}), bf16[32,4,256]{2,1,0:T(4,128)(2,1)S(1)}, u32[]{:S(2)}, u32[]{:S(2)}) async-start(bf16[32,4,256]{2,1,0:T(4,128)(2,1)} %get-tuple-element.18), calls=%async_computation.1 | async-start | bytes 131072 | tf_op jit(solution)/shard_map/all_to_all | solution.py:343
  52.8 8.8 %all-to-all-done.1.got_ref = bf16[32,4,256]{2,1,0:T(4,128)(2,1)S(1)} async-done(((bf16[32,4,256]{2,1,0:T(4,128)(2,1)}), bf16[32,4,256]{2,1,0:T(4,128)(2,1)S(1)}, u32[]{:S(2)}, u32[]{:S(2)}) %all-to-all-start.1) | async-done | bytes 65568 | tf_op jit(solution)/shard_map/all_to_all | solution.py:343
  61.6 0.9 norm.1
  62.5 11.9 %all_to_all.31.got_ref = bf16[32,4,256]{2,1,0:T(4,128)(2,1)S(1)} all-to-all(bf16[32,4,256]{2,1,0:T(4,128)(2,1)S(1)} %get-tuple-element.20), channel_id=1, replica_groups=mesh['tower'=32,'shard'=16] {'tower'}, dimensions={0} | all-to-all | bytes 131072 | tf_op jit(solution)/shard_map/all_to_all | solution.py:344
  74.4 0.9 tower_back.1
  75.3 3.5 %all-to-all-start.3 = ((bf16[8,128,256]{2,1,0:T(8,128)(2,1)}), bf16[8,128,256]{2,1,0:T(8,128)(2,1)S(1)}, u32[]{:S(2)}, u32[]{:S(2)}) async-start(bf16[8,128,256]{2,1,0:T(8,128)(2,1)} %tower_back.1), calls=%async_computation.3 | async-start | bytes 1048576 | tf_op jit(solution)/shard_map/all_to_all | solution.py:346
  78.8 0.1 pad_add_fusion.where_ref
  78.9 6.8 %feature_pool.1.bag_ref = bf16[2,8,128,128]{3,2,1,0:T(8,128)(2,1)S(1)} custom-call(s32[2]{0:T(128)S(1)} %pad_add_fusion.where_ref, bf16[8,18,16,128]{3,2,1,0:T(8,128)(2,1)S(1)} %all_to_all.30.mine_ref, bf16[8,18,16,128]{3,2,1,0:T(8,128)(2,1)S(1)} %collective-permute-done.other_ref, bf16[16,128,128]{2,1,0:T(8,128)(2,1)S(1)} %copy-done.1), custom_call_target="tpu_custom_call" | custom-call | flops 600000000 | bytes 18000000 | tf_op jit(solution)/shard_map/feature_pool/pallas_call | solution.py:201
  85.7 0.8 copy-done.5
  86.5 6.7 %all-to-all-done.3.mine_ref.grad_mine_ref = bf16[8,128,256]{2,1,0:T(8,128)(2,1)S(1)} async-done(((bf16[8,128,256]{2,1,0:T(8,128)(2,1)}), bf16[8,128,256]{2,1,0:T(8,128)(2,1)S(1)}, u32[]{:S(2)}, u32[]{:S(2)}) %all-to-all-start.3) | async-done | bytes 524320 | tf_op jit(solution)/shard_map/all_to_all | solution.py:346
  93.2 5.9 %collective-permute-start.1 = (bf16[8,128,256]{2,1,0:T(8,128)(2,1)S(1)}, bf16[8,128,256]{2,1,0:T(8,128)(2,1)S(1)}, u32[]{:S(2)}, u32[]{:S(2)}) collective-permute-start(bf16[8,128,256]{2,1,0:T(8,128)(2,1)S(1)} %all-to-all-done.3.mine_ref.grad_mine_ref), channel_id=1, source_target_pairs={{0,1},{1,0},{2,3},{3,2},{4,5},{5,4},{6,7},{7,6},{8,9},{9,8},{10,11... | collective-permute-start | bytes 1572872 | tf_op jit(solution)/shard_map/ppermute | solution.py:347
  99.1 1.5 %collective-permute-done.1.other_ref.grad_other_ref = bf16[8,128,256]{2,1,0:T(8,128)(2,1)S(1)} collective-permute-done((bf16[8,128,256]{2,1,0:T(8,128)(2,1)S(1)}, bf16[8,128,256]{2,1,0:T(8,128)(2,1)S(1)}, u32[]{:S(2)}, u32[]{:S(2)}) %collective-permute-start.1) | collective-permute-done | bytes 524320 | tf_op jit(solution)/shard_map/ppermute | solution.py:347
  100.6 1.0 copy-done.6
  101.7 0.4 weight_part.1
  102.1 0.8 copy-done.3
  102.9 0.8 copy-done.7
  103.7 4.1 %all-to-all-start.4 = ((bf16[8,128,256]{2,1,0:T(8,128)(2,1)}), bf16[8,128,256]{2,1,0:T(8,128)(2,1)}, u32[]{:S(2)}, u32[]{:S(2)}) async-start(bf16[8,128,256]{2,1,0:T(8,128)(2,1)} %copy-done.7), calls=%async_computation.4 | async-start | bytes 1048576 | tf_op jit(solution)/shard_map/all_to_all | solution.py:351
  107.8 1.0 copy-done.4
  108.9 11.2 %rows_part.1 = f32[16,24,128]{2,1,0:T(8,128)} custom-call(s32[2]{0:T(128)S(1)} %pad_add_fusion.where_ref, bf16[8,128,256]{2,1,0:T(8,128)(2,1)S(1)} %all-to-all-done.3.mine_ref.grad_mine_ref, bf16[8,128,256]{2,1,0:T(8,128)(2,1)S(1)} %copy-done.4, bf16[1,2048,256]{2,1,0:T(8,128)(2,1)S(1)} %copy-done.2, bf16[8,18,16,128]{3,2,1,0:T(8,128)(2,1)S(1)} %all_to_all.30.mine_ref, ...), custom_call_target="tpu_custom_call" | custom-call | flops 800000000 | bytes 24000000 | tf_op jit(solution)/shard_map/rows_part/pallas_call | solution.py:283
  120.1 5.8 %all-to-all-done.4.mine_ref = bf16[8,128,256]{2,1,0:T(8,128)(2,1)} async-done(((bf16[8,128,256]{2,1,0:T(8,128)(2,1)}), bf16[8,128,256]{2,1,0:T(8,128)(2,1)}, u32[]{:S(2)}, u32[]{:S(2)}) %all-to-all-start.4) | async-done | bytes 524320 | tf_op jit(solution)/shard_map/all_to_all | solution.py:351
  125.8 2.4 %collective-permute-start.2 = (bf16[8,128,256]{2,1,0:T(8,128)(2,1)}, bf16[8,128,256]{2,1,0:T(8,128)(2,1)S(1)}, u32[]{:S(2)}, u32[]{:S(2)}) collective-permute-start(bf16[8,128,256]{2,1,0:T(8,128)(2,1)} %all-to-all-done.4.mine_ref), channel_id=1, source_target_pairs={{0,1},{1,0},{2,3},{3,2},{4,5},{5,4},{6,7},{7,6},{8,9},{9,8},{10,11... | collective-permute-start | bytes 1572872 | tf_op jit(solution)/shard_map/ppermute | solution.py:353
  128.2 3.4 %all-to-all-start.5 = ((f32[16,24,128]{2,1,0:T(8,128)}), f32[16,24,128]{2,1,0:T(8,128)S(1)}, u32[]{:S(2)}, u32[]{:S(2)}) async-start(f32[16,24,128]{2,1,0:T(8,128)} %rows_part.1), calls=%async_computation.5 | async-start | bytes 393216 | tf_op jit(solution)/shard_map/all_to_all | solution.py:352
  131.7 3.5 %widen.1 = f32[8,2,128,256]{3,2,1,0:T(8,128)} custom-call(s32[1]{0:T(128)} %bitcast.side_ref, bf16[8,128,256]{2,1,0:T(8,128)(2,1)} %all-to-all-done.4.mine_ref, bf16[8,128,256]{2,1,0:T(8,128)(2,1)S(1)} %collective-permute-done.2.other_ref), custom_call_target="tpu_custom_call" | custom-call | flops 100000000 | bytes 3000000 | tf_op jit(solution)/shard_map/widen/pallas_call | solution.py:304
  135.2 6.8 %all-to-all-done.5 = f32[16,24,128]{2,1,0:T(8,128)S(1)} async-done(((f32[16,24,128]{2,1,0:T(8,128)}), f32[16,24,128]{2,1,0:T(8,128)S(1)}, u32[]{:S(2)}, u32[]{:S(2)}) %all-to-all-start.5) | async-done | bytes 196640 | tf_op jit(solution)/shard_map/all_to_all | solution.py:352
  141.9 0.6 slice.7
  142.6 0.7 slice.6
  (16 shorter events, 0.0 us)
Async XLA Ops:
  1.6 51.2 %copy-start.9 = (bf16[8192]{0:T(1024)(128)(2,1)S(1)}, bf16[8192]{0:T(1024)(128)(2,1)}, u32[]{:S(2)}) copy-start(bf16[8192]{0:T(1024)(128)(2,1)} %param.14) | copy-start | bytes 49156
  1.6 60.0 %copy-start.8 = (bf16[1,4,8192]{2,1,0:T(4,128)(2,1)S(1)}, bf16[1,4,8192]{2,1,0:T(4,128)(2,1)}, u32[]{:S(2)}) copy-start(bf16[1,4,8192]{2,1,0:T(4,128)(2,1)} %cot_ref.1) | copy-start | bytes 196612
  29.9 5.9 %collective-permute-start = (bf16[8,18,16,128]{3,2,1,0:T(8,128)(2,1)S(1)}, bf16[8,18,16,128]{3,2,1,0:T(8,128)(2,1)S(1)}, u32[]{:S(2)}, u32[]{:S(2)}) collective-permute-start(bf16[8,18,16,128]{3,2,1,0:T(8,128)(2,1)S(1)} %all_to_all.30.mine_ref), channel_id=1, source_target_pairs={{0,1},{1,0},{2,3},{3,2},{4,5},{5,4},{6,7},{7,6},{8,9},{9,8},{10,11... | collective-permute-start | bytes 1769480 | tf_op jit(solution)/shard_map/ppermute | solution.py:341
  35.8 1.0 copy-start
  36.9 42.0 %copy-start.1 = (bf16[16,128,128]{2,1,0:T(8,128)(2,1)S(1)}, bf16[16,128,128]{2,1,0:T(8,128)(2,1)}, u32[]{:S(2)}) copy-start(bf16[16,128,128]{2,1,0:T(8,128)(2,1)} %rem_ref.7) | copy-start | bytes 1572868
  43.1 18.5 %all-to-all-start.1 = ((bf16[32,4,256]{2,1,0:T(4,128)(2,1)}), bf16[32,4,256]{2,1,0:T(4,128)(2,1)S(1)}, u32[]{:S(2)}, u32[]{:S(2)}) async-start(bf16[32,4,256]{2,1,0:T(4,128)(2,1)} %get-tuple-element.18), calls=%async_computation.1 | async-start | bytes 131072 | tf_op jit(solution)/shard_map/all_to_all | solution.py:343
  75.3 17.9 %all-to-all-start.3 = ((bf16[8,128,256]{2,1,0:T(8,128)(2,1)}), bf16[8,128,256]{2,1,0:T(8,128)(2,1)S(1)}, u32[]{:S(2)}, u32[]{:S(2)}) async-start(bf16[8,128,256]{2,1,0:T(8,128)(2,1)} %tower_back.1), calls=%async_computation.3 | async-start | bytes 1048576 | tf_op jit(solution)/shard_map/all_to_all | solution.py:346
  85.7 0.8 copy-start.5
  86.5 21.3 %copy-start.2 = (bf16[1,2048,256]{2,1,0:T(8,128)(2,1)S(1)}, bf16[1,2048,256]{2,1,0:T(8,128)(2,1)}, u32[]{:S(2)}) copy-start(bf16[1,2048,256]{2,1,0:T(8,128)(2,1)} %weight_ref.3) | copy-start | bytes 3145732
  93.2 7.4 %collective-permute-start.1 = (bf16[8,128,256]{2,1,0:T(8,128)(2,1)S(1)}, bf16[8,128,256]{2,1,0:T(8,128)(2,1)S(1)}, u32[]{:S(2)}, u32[]{:S(2)}) collective-permute-start(bf16[8,128,256]{2,1,0:T(8,128)(2,1)S(1)} %all-to-all-done.3.mine_ref.grad_mine_ref), channel_id=1, source_target_pairs={{0,1},{1,0},{2,3},{3,2},{4,5},{5,4},{6,7},{7,6},{8,9},{9,8},{10,11... | collective-permute-start | bytes 1572872 | tf_op jit(solution)/shard_map/ppermute | solution.py:347
  100.6 1.0 copy-start.6
  102.1 0.8 copy-start.3
  102.9 0.8 copy-start.7
  103.7 22.2 %all-to-all-start.4 = ((bf16[8,128,256]{2,1,0:T(8,128)(2,1)}), bf16[8,128,256]{2,1,0:T(8,128)(2,1)}, u32[]{:S(2)}, u32[]{:S(2)}) async-start(bf16[8,128,256]{2,1,0:T(8,128)(2,1)} %copy-done.7), calls=%async_computation.4 | async-start | bytes 1048576 | tf_op jit(solution)/shard_map/all_to_all | solution.py:351
  107.8 1.0 copy-start.4
  125.8 5.8 %collective-permute-start.2 = (bf16[8,128,256]{2,1,0:T(8,128)(2,1)}, bf16[8,128,256]{2,1,0:T(8,128)(2,1)S(1)}, u32[]{:S(2)}, u32[]{:S(2)}) collective-permute-start(bf16[8,128,256]{2,1,0:T(8,128)(2,1)} %all-to-all-done.4.mine_ref), channel_id=1, source_target_pairs={{0,1},{1,0},{2,3},{3,2},{4,5},{5,4},{6,7},{7,6},{8,9},{9,8},{10,11... | collective-permute-start | bytes 1572872 | tf_op jit(solution)/shard_map/ppermute | solution.py:353
  128.2 13.7 %all-to-all-start.5 = ((f32[16,24,128]{2,1,0:T(8,128)}), f32[16,24,128]{2,1,0:T(8,128)S(1)}, u32[]{:S(2)}, u32[]{:S(2)}) async-start(f32[16,24,128]{2,1,0:T(8,128)} %rows_part.1), calls=%async_computation.5 | async-start | bytes 393216 | tf_op jit(solution)/shard_map/all_to_all | solution.py:352

commit v3 on v2

v3 whole, which is shorter than its diff:
```python
import functools

import jax
import jax.numpy as jnp
from jax import lax
from jax.experimental import pallas as pl
from jax.experimental.pallas import tpu as pltpu
from jax.sharding import PartitionSpec as P

norm_eps = 1e-05
f32, bf16 = jnp.float32, jnp.bfloat16
NT = (((1,), (1,)), ((), ()))
PARAMS = pltpu.CompilerParams(vmem_limit_bytes=20 * 1024 * 1024)
vmem = pl.BlockSpec(memory_space=pltpu.VMEM)
smem = pl.BlockSpec(memory_space=pltpu.SMEM)
hbm = pl.BlockSpec(memory_space=pltpu.HBM)


def in_hbm(*arrays):
    return tuple(pltpu.with_memory_space_constraint(a, pltpu.HBM) for a in arrays)


def mm(a, b):
    return jnp.dot(a, b, preferred_element_type=f32)


def mm_nt(a, b):
    return lax.dot_general(a, b, NT, preferred_element_type=f32)


def cost(micros):
    return pl.CostEstimate(
        flops=int(micros * 1e8), bytes_accessed=int(micros * 3e6), transcendentals=0
    )


def triangles(n):
    row = lax.broadcasted_iota(jnp.int32, (n, n), 0)
    col = lax.broadcasted_iota(jnp.int32, (n, n), 1)
    upto = jnp.where(col <= row, 1.0, 0.0).astype(bf16)
    before = jnp.where(col < row, 1.0, 0.0).astype(bf16)
    return jnp.concatenate([upto, before], axis=0)


def masks(picks, side, tri):
    values = picks.astype(jnp.int32)
    row_q = lax.broadcasted_iota(jnp.int32, (256, 128), 0)
    row_r = lax.broadcasted_iota(jnp.int32, (128, 128), 0)
    lane = lax.broadcasted_iota(jnp.int32, (128, 128), 1).astype(f32)
    place = ((((values >> 4) & 1) ^ side) << 7) + ((values >> 5) << 4) + (values & 15)
    sums = mm_nt(tri, picks)
    ends = jnp.broadcast_to(sums[:128, 8:9], (128, 128))
    starts = jnp.broadcast_to(sums[128:, 8:9], (128, 128))
    quot, rem, member = [], [], []
    for c in range(4):
        quot.append(jnp.where(row_q == place[c : c + 1], 1.0, 0.0).astype(bf16))
        rem.append(jnp.where(row_r == values[4 + c : 5 + c], 1.0, 0.0).astype(bf16))
        here = lane + float(128 * c)
        inside = (here < ends) & (here >= starts)
        member.append(jnp.where(inside, 1.0, 0.0).astype(bf16))
    return tuple(jnp.concatenate(v, axis=1) for v in (quot, rem, member))


def look_up(quot_t, rem_t, quot_hot, rem_hot, member):
    quot = mm(quot_t, quot_hot)
    rem = mm(rem_t, rem_hot)
    composed = quot * rem
    high = composed.astype(bf16)
    low = (composed - high.astype(f32)).astype(bf16)
    return quot, rem, mm_nt(member, high) + mm_nt(member, low)


def pack_kernel(rows_ref, quot_ref, rem_ref, size_ref, out_ref, picks_ref, held):
    feats = rows_ref.shape[0]
    held[...] = jnp.zeros_like(held)
    for f in range(feats):
        for c in range(4):
            part = pl.ds(128 * c, 128)
            held[f, c : c + 1, :] = quot_ref[f, :, part].astype(f32)
            held[f, 4 + c : 5 + c, :] = rem_ref[f, :, part].astype(f32)
        held[f, 8:9, :] = size_ref[f].astype(f32)
    picks = held[...].astype(bf16)
    picks_ref[...] = picks
    rows = rows_ref[...]
    for z in range(out_ref.shape[0]):
        out_ref[z, :feats] = rows
        out_ref[z, feats:] = picks[2 * z : 2 * z + 2]


def pack(rows, quot, rem, sizes):
    feats, zs = rows.shape[0], rows.shape[0] // 2
    whole = lambda a: pl.BlockSpec(a.shape, lambda i: (0, 0, 0))
    pinned = in_hbm(rows, quot, rem, sizes)
    return pl.pallas_call(
        pack_kernel,
        grid=(1,),
        in_specs=[whole(a) for a in pinned],
        out_specs=[
            pl.BlockSpec((zs, feats + 2, 16, 128), lambda i: (0, 0, 0, 0)),
            pl.BlockSpec((feats, 16, 128), lambda i: (0, 0, 0)),
        ],
        out_shape=[
            jax.ShapeDtypeStruct((zs, feats + 2, 16, 128), bf16),
            jax.ShapeDtypeStruct((feats, 16, 128), bf16),
        ],
        scratch_shapes=[pltpu.VMEM((feats, 16, 128), f32)],
        compiler_params=PARAMS,
        cost_estimate=cost(1),
        name="pack",
    )(*pinned)


def tower_kernel(side_ref, mine_ref, other_ref, rem_ref, picks_ref, weight_ref, pre_ref):
    tri = triangles(128)
    side = side_ref[0]
    bags = []
    for f in range(rem_ref.shape[0]):
        table = jnp.concatenate(
            [mine_ref[:, f].reshape(128, 128), other_ref[:, f].reshape(128, 128)], axis=0
        )
        _, _, pooled = look_up(table.T, rem_ref[f].T, *masks(picks_ref[f], side, tri))
        bags.append(pooled.astype(bf16))
    pre_ref[...] = mm(jnp.concatenate(bags, axis=1), weight_ref[0])


def tower_forward(side, mine, other, remainder, picks, weight):
    return pl.pallas_call(
        tower_kernel,
        in_specs=[smem] + [vmem] * 5,
        out_specs=vmem,
        out_shape=jax.ShapeDtypeStruct((128, 256), f32),
        compiler_params=PARAMS,
        cost_estimate=cost(6),
        name="tower_forward",
    )(side, mine, other, remainder, picks, weight)


def silu(pre):
    return (pre * jax.nn.sigmoid(pre)).astype(bf16).astype(f32)


def stats_kernel(pre_ref, cot_ref, gain_ref, out_ref, scaled_ref):
    act = silu(pre_ref[...])
    for d in range(cot_ref.shape[0]):
        scaled_ref[4 * d : 4 * d + 4] = cot_ref[d].astype(f32) * gain_ref[...]
    mean = jnp.mean(act, axis=1, keepdims=True)
    center = act - mean
    scaled = scaled_ref[...]
    spread = jnp.sum(center * center, axis=1, keepdims=True)
    total = jnp.sum(scaled, axis=1, keepdims=True)
    lean = jnp.sum(scaled * center, axis=1, keepdims=True)
    lane = lax.broadcasted_iota(jnp.int32, (128, 128), 1)
    table = jnp.where(
        lane == 0, mean, jnp.where(lane == 1, spread, jnp.where(lane == 2, total, lean))
    )
    stats = table.T[:4]
    for d in range(out_ref.shape[0]):
        rows = act[4 * d : 4 * d + 4]
        out_ref[d, 0], out_ref[d, 1], out_ref[d, 2] = rows[:, :128], rows[:, 128:], stats


def local_stats(pre, cot, gain, towers):
    return pl.pallas_call(
        stats_kernel,
        out_shape=[
            jax.ShapeDtypeStruct((towers, 3, 4, 128), f32),
            jax.ShapeDtypeStruct(pre.shape, f32),
        ],
        compiler_params=PARAMS,
        cost_estimate=cost(1),
        name="local_stats",
    )(pre, cot, gain)


def norm_kernel(got_ref, gain_ref, joint_ref):
    towers = got_ref.shape[0]
    columns = float(towers * 256)
    pieces = [(t, h, pl.ds(256 * t + 128 * h, 128)) for t in range(towers) for h in range(2)]
    mean = sum(got_ref[t, h] for t, h, _ in pieces)
    mean = jnp.sum(mean, axis=1, keepdims=True) * (1.0 / columns)
    center = [got_ref[t, h] - mean for t, h, _ in pieces]
    spread = jnp.sum(sum(c * c for c in center), axis=1, keepdims=True) * (1.0 / columns)
    scale = lax.rsqrt(spread + norm_eps)
    for c, (_, _, part) in zip(center, pieces):
        joint_ref[0, :, part] = (c * scale * gain_ref[:, part]).astype(bf16)


def norm(got, gain):
    return pl.pallas_call(
        norm_kernel,
        out_shape=jax.ShapeDtypeStruct((1, 4, gain.shape[1]), bf16),
        compiler_params=PARAMS,
        cost_estimate=cost(1),
        name="norm",
    )(got, gain)


def feature_kernel(per_step, where_ref, mine_ref, other_ref, rem_ref, picks_ref, *refs):
    bag_ref, quot_ref, remd_ref, qhot_ref, rhot_ref, member_ref, qt_ref, rt_ref = refs

    @pl.when((pl.program_id(0) == 0) & (pl.program_id(1) == 0))
    def _():
        qt_ref[:, :128] = mine_ref[:, 0].reshape(128, 128).T
        qt_ref[:, 128:] = other_ref[:, 0].reshape(128, 128).T
        rt_ref[...] = rem_ref[0].T

    tri = triangles(128)
    for i in range(per_step):
        hot = masks(picks_ref[0, i], where_ref[1], tri)
        quot, rem, pooled = look_up(qt_ref[...], rt_ref[...], *hot)
        bag_ref[0, i] = pooled.T.astype(bf16)
        quot_ref[0, i], remd_ref[0, i] = quot.astype(bf16), rem.astype(bf16)
        qhot_ref[0, i], rhot_ref[0, i], member_ref[0, i] = hot


def step_block(per_step, *dims):
    return pl.BlockSpec((1, per_step, *dims), lambda h, i, w: (h, i, 0, 0))


def feature_pool(where, mine, other, remainder, picks):
    zs, per_step = picks.shape[1], 4
    table = pl.BlockSpec((zs, 1, 16, 128), lambda h, i, w: (0, w[0], 0, 0))
    sizes = [(128, 128), (128, 512), (128, 512), (256, 512), (128, 512), (128, 512)]
    return pl.pallas_call(
        functools.partial(feature_kernel, per_step),
        grid_spec=pltpu.PrefetchScalarGridSpec(
            num_scalar_prefetch=1,
            grid=(2, zs // per_step),
            in_specs=[
                table,
                table,
                pl.BlockSpec((1, 128, 128), lambda h, i, w: (w[0], 0, 0)),
                step_block(per_step, 16, 128),
            ],
            out_specs=[step_block(per_step, *s) for s in sizes],
            scratch_shapes=[pltpu.VMEM((128, 256), bf16), pltpu.VMEM((128, 128), bf16)],
        ),
        out_shape=[pltpu.HBM((2, zs, *s), bf16) for s in sizes],
        compiler_params=PARAMS,
        cost_estimate=cost(6),
        name="feature_pool",
    )(where, mine, other, *in_hbm(remainder), picks)


def back_kernel(columns, got_ref, pre_ref, scaled_ref, out_ref):
    towers = got_ref.shape[0]
    stats = got_ref[:, 2]
    sums = jnp.sum(stats, axis=0)
    mean = sums[0:1] * (1.0 / towers)
    shift = stats[:, 0:1, :] - mean[None]
    spread = sums[1:2] + (columns / towers) * jnp.sum(shift * shift, axis=0)
    lean = sums[3:4] + jnp.sum(stats[:, 2:3, :] * shift, axis=0)
    scale = lax.rsqrt(spread * (1.0 / columns) + norm_eps)
    rows = [mean, scale, sums[2:3] * (1.0 / columns), lean * scale * scale * (1.0 / columns)]
    table = jnp.concatenate(rows + [jnp.zeros((124, 128), f32)], axis=0).T
    mean, scale, total, lean = (table[:, i : i + 1] for i in range(4))
    pre = pre_ref[...]
    sigma = jax.nn.sigmoid(pre)
    grad = (scale * (scaled_ref[...] - total - (silu(pre) - mean) * lean)).astype(bf16).astype(f32)
    pre_grad = (grad * sigma * (1.0 + pre * (1.0 - sigma))).astype(bf16)
    for d in range(out_ref.shape[0]):
        out_ref[d] = pre_grad


def tower_back(got, pre, scaled, copies):
    columns = got.shape[0] * pre.shape[1]
    return pl.pallas_call(
        functools.partial(back_kernel, float(columns)),
        out_shape=jax.ShapeDtypeStruct((copies, *pre.shape), bf16),
        compiler_params=PARAMS,
        cost_estimate=cost(1),
        name="tower_back",
    )(got, pre, scaled)


def grads_kernel(per_step, where_ref, mine_ref, other_ref, weight_ref, *refs):
    bag_ref, quot_ref, remd_ref, qhot_ref, rhot_ref, member_ref, out_ref, wg_ref, qg_ref, rg_ref = refs
    half, step = pl.program_id(0), pl.program_id(1)

    @pl.when((half == 0) & (step == 0))
    def _():
        wg_ref[...] = jnp.zeros_like(wg_ref)
        qg_ref[...] = jnp.zeros_like(qg_ref)
        rg_ref[...] = jnp.zeros_like(rg_ref)

    weight_sum, quot_sum, rem_sum = wg_ref[...], qg_ref[...], rg_ref[...]
    for i in range(per_step):
        grad = jnp.where(half == 0, mine_ref[i], other_ref[i])
        weight_sum += mm(bag_ref[0, i], grad)
        look = mm(mm_nt(weight_ref[0], grad).astype(bf16), member_ref[0, i])
        quot_part = (look * remd_ref[0, i].astype(f32)).astype(bf16)
        rem_part = (look * quot_ref[0, i].astype(f32)).astype(bf16)
        quot_sum += mm_nt(quot_part, qhot_ref[0, i])
        rem_sum += mm_nt(rem_part, rhot_ref[0, i])
    wg_ref[...], qg_ref[...], rg_ref[...] = weight_sum, quot_sum, rem_sum

    @pl.when((half == pl.num_programs(0) - 1) & (step == pl.num_programs(1) - 1))
    def _():
        side = where_ref[1]
        chunk = weight_sum.astype(bf16)
        quot, rem = quot_sum.T, rem_sum.T
        for z in range(out_ref.shape[0]):
            near, far = quot[16 * z : 16 * z + 16], quot[128 + 16 * z : 144 + 16 * z]
            first, second = jnp.where(side == 0, near, far), jnp.where(side == 0, far, near)
            pair = jnp.concatenate([rem[16 * z : 16 * z + 8], rem[16 * z + 8 : 16 * z + 16]], axis=1)
            out_ref[z, :128] = chunk
            out_ref[z, 128:144] = jnp.concatenate([first, second], axis=1).astype(bf16)
            out_ref[z, 144:160] = jnp.concatenate([pair, jnp.zeros_like(pair)], axis=0).astype(bf16)


def grads_part(where, mine, other, weight, *looked):
    zs, per_step = mine.shape[0], 4
    grads = pl.BlockSpec((per_step, 128, 256), lambda h, i, w: (i, 0, 0))
    return pl.pallas_call(
        functools.partial(grads_kernel, per_step),
        grid_spec=pltpu.PrefetchScalarGridSpec(
            num_scalar_prefetch=1,
            grid=(2, zs // per_step),
            in_specs=[grads, grads, pl.BlockSpec((1, 128, 256), lambda h, i, w: (0, w[0], 0))]
            + [step_block(per_step, *a.shape[2:]) for a in looked],
            out_specs=pl.BlockSpec((zs, 160, 256), lambda h, i, w: (0, 0, 0)),
            scratch_shapes=[
                pltpu.VMEM((128, 256), f32),
                pltpu.VMEM((128, 256), f32),
                pltpu.VMEM((128, 128), f32),
            ],
        ),
        out_shape=jax.ShapeDtypeStruct((zs, 160, 256), bf16),
        compiler_params=PARAMS,
        cost_estimate=cost(8),
        name="grads_part",
    )(where, mine, other, *in_hbm(weight, *looked))


def spread_kernel(side_ref, mine_ref, other_ref, weight_ref, quot_ref, rem_ref):
    side = side_ref[0]
    for z in range(mine_ref.shape[0]):
        for at, ref in ((side, mine_ref), (1 - side, other_ref)):
            weight_ref[z, at] = ref[z, :128].astype(f32)
            rows = ref[z, 128:160].astype(f32)
            rows = jnp.where(side == 0, rows[:, :128], rows[:, 128:])
            quot_ref[z, at] = rows[:16]
            rem_ref[z, at] = rows[16:24]


def spread(side, mine, other):
    zs, step = mine.shape[0], 2
    block = pl.BlockSpec((step, 160, 256), lambda i: (i, 0, 0))
    sizes = [(128, 256), (16, 128), (8, 128)]
    return pl.pallas_call(
        spread_kernel,
        grid=(zs // step,),
        in_specs=[smem, block, block],
        out_specs=[pl.BlockSpec((step, 2, *s), lambda i: (i, 0, 0, 0)) for s in sizes],
        out_shape=[jax.ShapeDtypeStruct((zs, 2, *s), f32) for s in sizes],
        compiler_params=PARAMS,
        cost_estimate=cost(2),
        name="spread",
    )(side, mine, other)


def on_device(
    quotient_rows,
    remainder_rows,
    quotient_index,
    remainder_index,
    bag_sizes,
    tower_weight,
    norm_gain,
    cotangent,
):
    feats = quotient_rows.shape[0]
    shards, towers = lax.axis_size("shard"), lax.axis_size("tower")
    shard, tower = lax.axis_index("shard"), lax.axis_index("tower")
    zs = shards // 2
    along_z = [[2 * z + c for z in range(zs)] for c in range(2)]
    across = [(i, i ^ 1) for i in range(shards)]
    swap = functools.partial(lax.all_to_all, split_axis=0, concat_axis=0, tiled=True)
    gather_z = functools.partial(swap, axis_name="shard", axis_index_groups=along_z)
    side = (shard & 1).astype(jnp.int32)
    side_arg = side[None]
    where = jnp.stack([shard.astype(jnp.int32), side])
    gain = norm_gain.astype(f32)[None]

    gain_here = lax.dynamic_slice(norm_gain, (tower * 256,), (256,)).astype(f32)[None]

    packed, picks = pack(quotient_rows, quotient_index, remainder_index, bag_sizes)
    mine, late = lax.optimization_barrier((gather_z(packed), cotangent[0]))
    other = lax.ppermute(mine, "shard", across)
    late = late.reshape(4, towers, 256).transpose(1, 0, 2)
    pre = tower_forward(side_arg, mine, other, remainder_rows, picks, tower_weight)
    pre, cot = lax.optimization_barrier((pre, swap(late, "tower")))
    sent, scaled = local_stats(pre, cot, gain_here, towers)
    stats = swap(sent, "tower")
    grad_copies = tower_back(stats, pre, scaled, zs)
    joint = norm(stats, gain)
    all_picks = lax.dynamic_index_in_dim(
        jnp.stack([mine[:, feats:], other[:, feats:]]), side, 2, keepdims=False
    )
    looked = feature_pool(where, mine, other, remainder_rows, all_picks)
    grad_mine, joint, *looked = lax.optimization_barrier((gather_z(grad_copies), joint, *looked))
    grad_other = lax.ppermute(grad_mine, "shard", across)
    got_mine = gather_z(grads_part(where, grad_mine, grad_other, tower_weight, *looked))
    got_other = lax.ppermute(got_mine, "shard", across)
    weight_grad, quot_grad, rem_grad = spread(side_arg, got_mine, got_other)
    return (
        joint,
        weight_grad.reshape(1, feats * 128, 256),
        quot_grad.reshape(feats, 16, 128),
        rem_grad.reshape(feats, 8, 128),
    )


def solution(mesh):
    in_specs = (
        P("tower", "shard", None),
        P("tower", None, None),
        P("tower", "shard", None),
        P("tower", "shard", None),
        P("tower", "shard", None),
        P("tower", None, None),
        P(),
        P("shard", "tower", None),
    )
    out_specs = (
        P("shard", "tower", None),
        P("tower", None, None),
        P("tower", "shard", None),
        P("tower", "shard", None),
    )
    return jax.shard_map(
        on_device, mesh=mesh, in_specs=in_specs, out_specs=out_specs, check_vma=False
    )
```

time: 144 us -> 135 us (0.938)
  blocking collectives: 40.2 us -> 67.8 us
  waiting for transfers between devices: 31.2 us -> 9.58 us
  starting transfers between devices: 33.3 us -> 25.4 us
  local copies, waits for them, and re-layouts: 6.8 us -> 1.07 us
  Pallas kernels: 30.9 us -> 29.2 us
    all_to_all x2 -> x3, blocking collectives: 40.2 us -> 67.8 us  [the longest x1 28.1 us: on_device(): mine, late = lax.optimization_barrier((gather_z(packed), cotangent[0]))]
    all_to_all x4 -> x2, waiting for transfers between devices: 28.1 us -> 6.36 us  [the longest x1 3.92 us: on_device(): gather_z(grad_copies)]
    all_to_all x4 -> x2, starting transfers between devices: 20.7 us -> 13.2 us  [the longest x1 9.68 us: on_device(): pre, cot = lax.optimization_barrier((pre, swap(late, 'tower')))]
    unnamed x20 -> x6, local copies, waits for them, and re-layouts: 5.5 us -> 1.06 us
    pallas_call x7, Pallas kernels: 29.9 us -> 28.1 us  [the longest x1 9.68 us: feature_pool(): pl.pallas_call(functools.partial(feature_kernel, per_step), grid_spec=plt...]
    ppermute x1, waiting for transfers between devices: 0.01 us -> 1.7 us  [on_device(): got_other = lax.ppermute(got_mine, 'shard', across)]
    ppermute x1, waiting for transfers between devices: 1.6 us -> 0.01 us  [on_device(): other = lax.ppermute(mine, 'shard', across)]
  transfers between devices with their start and end apart: 7 -> 5, of which waited for: 6 -> 4; matrix products, arithmetic and copies ran while one was open for 0% -> 1% of each run, Pallas kernels for 15% -> 11%
where the time goes in v3:
time: 135 us
  blocking collectives  67.8 us (50%)
  Pallas kernels  29.2 us (22%)
  starting transfers between devices  25.4 us (19%)
  waiting for transfers between devices  9.58 us (7%)
    all_to_all x1, blocking collectives, on_device(): mine, late = lax.optimization_barrier((gather_z(packed), cotangent[0]))  28.1 us
    all_to_all x1, blocking collectives, on_device(): gather_z(grads_part(where, grad_mine, grad_other, tower_weight, *looked))  23.2 us
    all_to_all x1, blocking collectives, on_device(): stats = swap(sent, 'tower')  16.6 us
    pallas_call x1, Pallas kernels, feature_pool(): pl.pallas_call(functools.partial(feature_kernel, per_step), grid_spec=plt...  9.68 us
    all_to_all x1, starting transfers between devices, on_device(): pre, cot = lax.optimization_barrier((pre, swap(late, 'tower')))  9.68 us
    pallas_call x1, Pallas kernels, grads_part(): pl.pallas_call(functools.partial(grads_kernel, per_step), grid_spec=pltpu...  9.53 us
    ppermute x1, starting transfers between devices, on_device(): grad_other = lax.ppermute(grad_mine, 'shard', across)  5.55 us
    pallas_call x1, Pallas kernels, tower_forward(): pl.pallas_call(tower_kernel, in_specs=[smem] + [vmem] * 5, out_specs=vmem...  4.68 us
  transfers between devices with their start and end apart: 5, of which 4 were waited for; matrix products, arithmetic and copies ran while one was open for 1% of the time, Pallas kernels for 11%

profile of v3, /device:TPU:1, one launch (start us, length us, event | category | flops | bytes accessed | tf_op | source)
XLA Modules:
  0.0 134.7 jit_solution(15838535516296724666)
XLA Ops:
  0.6 0.0 copy-start
  0.6 1.1 pack.1
  1.7 28.1 %all_to_all.25.mine_ref = bf16[8,18,16,128]{3,2,1,0:T(8,128)(2,1)S(1)} all-to-all(bf16[8,18,16,128]{3,2,1,0:T(8,128)(2,1)S(1)} %get-tuple-element.29), channel_id=1, replica_groups={{0,2,4,6,8,10,12,14},{1,3,5,7,9,11,13,15},{16,18,20,22,24,26,28,30},{17..., dimensions={0} | all-to-all | bytes 1179648 | tf_op jit(solution)/shard_map/all_to_all | solution.py:388
  29.8 4.3 %collective-permute-start = (bf16[8,18,16,128]{3,2,1,0:T(8,128)(2,1)S(1)}, bf16[8,18,16,128]{3,2,1,0:T(8,128)(2,1)S(1)}, u32[]{:S(2)}, u32[]{:S(2)}) collective-permute-start(bf16[8,18,16,128]{3,2,1,0:T(8,128)(2,1)S(1)} %all_to_all.25.mine_ref), channel_id=1, source_target_pairs={{0,1},{1,0},{2,3},{3,2},{4,5},{5,4},{6,7},{7,6},{8,9},{9,8},{10,11... | collective-permute-start | bytes 1769480 | tf_op jit(solution)/shard_map/ppermute | solution.py:389
  34.2 9.7 %all-to-all-start.1 = ((bf16[32,4,256]{2,1,0:T(4,128)(2,1)}), bf16[32,4,256]{2,1,0:T(4,128)(2,1)S(1)}, u32[]{:S(2)}, u32[]{:S(2)}) async-start(bf16[32,4,256]{2,1,0:T(4,128)(2,1)} %bitcast.19), calls=%async_computation.1 | async-start | bytes 131072 | tf_op jit(solution)/shard_map/all_to_all | solution.py:392
  43.8 0.8 dynamic-slice_convert_fusion
  44.6 0.0 collective-permute-done.other_ref
  44.6 0.0 copy-done
  44.6 0.0 copy-start.1
  44.6 1.0 copy-done.1
  45.7 4.7 %tower_forward.1.pre_ref = f32[128,256]{1,0:T(8,128)S(1)} custom-call(s32[1]{0:T(128)} %bitcast.side_ref, bf16[8,18,16,128]{3,2,1,0:T(8,128)(2,1)S(1)} %all_to_all.25.mine_ref, bf16[8,18,16,128]{3,2,1,0:T(8,128)(2,1)S(1)} %collective-permute-done.other_ref, bf16[16,128,128]{2,1,0:T(8,128)(2,1)S(1)} %copy-done.1, ...), custom_call_target="tpu_custom_call" | custom-call | flops 600000000 | bytes 18000000 | tf_op jit(solution)/shard_map/tower_forward/pallas_call | solution.py:127
  50.3 0.0 copy-start.2
  50.4 2.4 %all-to-all-done.1.cot_ref = bf16[32,4,256]{2,1,0:T(4,128)(2,1)S(1)} async-done(((bf16[32,4,256]{2,1,0:T(4,128)(2,1)}), bf16[32,4,256]{2,1,0:T(4,128)(2,1)S(1)}, u32[]{:S(2)}, u32[]{:S(2)}) %all-to-all-start.1) | async-done | bytes 65568 | tf_op jit(solution)/shard_map/all_to_all | solution.py:392
  52.8 0.3 local_stats.1
  53.0 16.6 %all_to_all.26.got_ref = f32[32,3,4,128]{3,2,1,0:T(4,128)S(1)} all-to-all(f32[32,3,4,128]{3,2,1,0:T(4,128)S(1)} %get-tuple-element.35), channel_id=1, replica_groups=mesh['tower'=32,'shard'=16] {'tower'}, dimensions={0} | all-to-all | bytes 393216 | tf_op jit(solution)/shard_map/all_to_all | solution.py:394
  69.6 1.2 tower_back.1
  70.8 3.5 %all-to-all-start.3 = ((bf16[8,128,256]{2,1,0:T(8,128)(2,1)}), bf16[8,128,256]{2,1,0:T(8,128)(2,1)S(1)}, u32[]{:S(2)}, u32[]{:S(2)}) async-start(bf16[8,128,256]{2,1,0:T(8,128)(2,1)} %tower_back.1), calls=%async_computation.3 | async-start | bytes 1048576 | tf_op jit(solution)/shard_map/all_to_all | solution.py:401
  74.3 0.0 copy-done.2
  74.3 0.1 pad_add_fusion.where_ref
  74.4 9.7 %feature_pool.1 = (bf16[2,8,128,128]{3,2,1,0:T(8,128)(2,1)}, bf16[2,8,128,512]{3,2,1,0:T(8,128)(2,1)}, bf16[2,8,128,512]{3,2,1,0:T(8,128)(2,1)}, bf16[2,8,256,51...) custom-call(s32[2]{0:T(128)S(1)} %pad_add_fusion.where_ref, ...), custom_call_target="tpu_custom_call" | custom-call | flops 600000000 | bytes 18000000 | tf_op jit(solution)/shard_map/feature_pool/pallas_call | solution.py:224
  84.1 1.0 norm.1
  85.1 3.9 %all-to-all-done.3.mine_ref = bf16[8,128,256]{2,1,0:T(8,128)(2,1)S(1)} async-done(((bf16[8,128,256]{2,1,0:T(8,128)(2,1)}), bf16[8,128,256]{2,1,0:T(8,128)(2,1)S(1)}, u32[]{:S(2)}, u32[]{:S(2)}) %all-to-all-start.3) | async-done | bytes 524320 | tf_op jit(solution)/shard_map/all_to_all | solution.py:401
  89.0 5.6 %collective-permute-start.1 = (bf16[8,128,256]{2,1,0:T(8,128)(2,1)S(1)}, bf16[8,128,256]{2,1,0:T(8,128)(2,1)S(1)}, u32[]{:S(2)}, u32[]{:S(2)}) collective-permute-start(bf16[8,128,256]{2,1,0:T(8,128)(2,1)S(1)} %all-to-all-done.3.mine_ref), channel_id=1, source_target_pairs={{0,1},{1,0},{2,3},{3,2},{4,5},{5,4},{6,7},{7,6},{8,9},{9,8},{10,11... | collective-permute-start | bytes 1572872 | tf_op jit(solution)/shard_map/ppermute | solution.py:402
  94.5 1.5 %collective-permute-done.1.other_ref = bf16[8,128,256]{2,1,0:T(8,128)(2,1)S(1)} collective-permute-done((bf16[8,128,256]{2,1,0:T(8,128)(2,1)S(1)}, bf16[8,128,256]{2,1,0:T(8,128)(2,1)S(1)}, u32[]{:S(2)}, u32[]{:S(2)}) %collective-permute-start.1) | collective-permute-done | bytes 524320 | tf_op jit(solution)/shard_map/ppermute | solution.py:402
  96.1 9.5 %grads_part.1 = bf16[8,160,256]{2,1,0:T(8,128)(2,1)S(1)} custom-call(s32[2]{0:T(128)S(1)} %pad_add_fusion.where_ref, bf16[8,128,256]{2,1,0:T(8,128)(2,1)S(1)} %all-to-all-done.3.mine_ref, bf16[8,128,256]{2,1,0:T(8,128)(2,1)S(1)} %collective-permute-done.1.other_ref, bf16[1,2048,256]{2,1,0:T(8,128)(2,1)} %weight_ref.3, ...), custom_call_target="tpu_custom_call" | custom-call | flops 800000000 | bytes 24000000 | tf_op jit(solution)/shard_map/grads_part/pallas_call | solution.py:314
  105.6 23.2 %all_to_all.27.mine_ref = bf16[8,160,256]{2,1,0:T(8,128)(2,1)S(1)} all-to-all(bf16[8,160,256]{2,1,0:T(8,128)(2,1)S(1)} %grads_part.1), channel_id=1, replica_groups={{0,2,4,6,8,10,12,14},{1,3,5,7,9,11,13,15},{16,18,20,22,24,26,28,30},{17..., dimensions={0} | all-to-all | bytes 1310720 | tf_op jit(solution)/shard_map/all_to_all | solution.py:403
  128.8 2.4 %collective-permute-start.2 = (bf16[8,160,256]{2,1,0:T(8,128)(2,1)S(1)}, bf16[8,160,256]{2,1,0:T(8,128)(2,1)S(1)}, u32[]{:S(2)}, u32[]{:S(2)}) collective-permute-start(bf16[8,160,256]{2,1,0:T(8,128)(2,1)S(1)} %all_to_all.27.mine_ref), channel_id=1, source_target_pairs={{0,1},{1,0},{2,3},{3,2},{4,5},{5,4},{6,7},{7,6},{8,9},{9,8},{10,11... | collective-permute-start | bytes 1966088 | tf_op jit(solution)/shard_map/ppermute | solution.py:404
  131.2 1.7 %collective-permute-done.2.other_ref = bf16[8,160,256]{2,1,0:T(8,128)(2,1)S(1)} collective-permute-done((bf16[8,160,256]{2,1,0:T(8,128)(2,1)S(1)}, bf16[8,160,256]{2,1,0:T(8,128)(2,1)S(1)}, u32[]{:S(2)}, u32[]{:S(2)}) %collective-permute-start.2) | collective-permute-done | bytes 655392 | tf_op jit(solution)/shard_map/ppermute | solution.py:404
  132.9 1.9 %spread.1 = (f32[8,2,128,256]{3,2,1,0:T(8,128)}, f32[8,2,16,128]{3,2,1,0:T(8,128)}, f32[8,2,8,128]{3,2,1,0:T(8,128)}) custom-call(s32[1]{0:T(128)} %bitcast.side_ref, bf16[8,160,256]{2,1,0:T(8,128)(2,1)S(1)} %all_to_all.27.mine_ref, bf16[8,160,256]{2,1,0:T(8,128)(2,1)S(1)} %collective-permute-done.2.other_ref), custom_call_target="tpu_custom_call" | custom-call | flops 200000000 | bytes 6000000 | tf_op jit(solution)/shard_map/spread/pallas_call | solution.py:350
  (4 shorter events, 0.0 us)
Async XLA Ops:
  0.6 44.0 %copy-start = (bf16[1,2048,256]{2,1,0:T(8,128)(2,1)S(1)}, bf16[1,2048,256]{2,1,0:T(8,128)(2,1)}, u32[]{:S(2)}) copy-start(bf16[1,2048,256]{2,1,0:T(8,128)(2,1)} %weight_ref.3) | copy-start | bytes 3145732
  29.8 14.8 %collective-permute-start = (bf16[8,18,16,128]{3,2,1,0:T(8,128)(2,1)S(1)}, bf16[8,18,16,128]{3,2,1,0:T(8,128)(2,1)S(1)}, u32[]{:S(2)}, u32[]{:S(2)}) collective-permute-start(bf16[8,18,16,128]{3,2,1,0:T(8,128)(2,1)S(1)} %all_to_all.25.mine_ref), channel_id=1, source_target_pairs={{0,1},{1,0},{2,3},{3,2},{4,5},{5,4},{6,7},{7,6},{8,9},{9,8},{10,11... | collective-permute-start | bytes 1769480 | tf_op jit(solution)/shard_map/ppermute | solution.py:389
  34.2 18.6 %all-to-all-start.1 = ((bf16[32,4,256]{2,1,0:T(4,128)(2,1)}), bf16[32,4,256]{2,1,0:T(4,128)(2,1)S(1)}, u32[]{:S(2)}, u32[]{:S(2)}) async-start(bf16[32,4,256]{2,1,0:T(4,128)(2,1)} %bitcast.19), calls=%async_computation.1 | async-start | bytes 131072 | tf_op jit(solution)/shard_map/all_to_all | solution.py:392
  44.6 1.0 copy-start.1
  50.3 23.9 %copy-start.2 = (bf16[8192]{0:T(1024)(128)(2,1)S(1)}, bf16[8192]{0:T(1024)(128)(2,1)}, u32[]{:S(2)}) copy-start(bf16[8192]{0:T(1024)(128)(2,1)} %param.14) | copy-start | bytes 49156
  70.8 18.2 %all-to-all-start.3 = ((bf16[8,128,256]{2,1,0:T(8,128)(2,1)}), bf16[8,128,256]{2,1,0:T(8,128)(2,1)S(1)}, u32[]{:S(2)}, u32[]{:S(2)}) async-start(bf16[8,128,256]{2,1,0:T(8,128)(2,1)} %tower_back.1), calls=%async_computation.3 | async-start | bytes 1048576 | tf_op jit(solution)/shard_map/all_to_all | solution.py:401
  89.0 7.1 %collective-permute-start.1 = (bf16[8,128,256]{2,1,0:T(8,128)(2,1)S(1)}, bf16[8,128,256]{2,1,0:T(8,128)(2,1)S(1)}, u32[]{:S(2)}, u32[]{:S(2)}) collective-permute-start(bf16[8,128,256]{2,1,0:T(8,128)(2,1)S(1)} %all-to-all-done.3.mine_ref), channel_id=1, source_target_pairs={{0,1},{1,0},{2,3},{3,2},{4,5},{5,4},{6,7},{7,6},{8,9},{9,8},{10,11... | collective-permute-start | bytes 1572872 | tf_op jit(solution)/shard_map/ppermute | solution.py:402
  128.8 4.1 %collective-permute-start.2 = (bf16[8,160,256]{2,1,0:T(8,128)(2,1)S(1)}, bf16[8,160,256]{2,1,0:T(8,128)(2,1)S(1)}, u32[]{:S(2)}, u32[]{:S(2)}) collective-permute-start(bf16[8,160,256]{2,1,0:T(8,128)(2,1)S(1)} %all_to_all.27.mine_ref), channel_id=1, source_target_pairs={{0,1},{1,0},{2,3},{3,2},{4,5},{5,4},{6,7},{7,6},{8,9},{9,8},{10,11... | collective-permute-start | bytes 1966088 | tf_op jit(solution)/shard_map/ppermute | solution.py:404

commit v4 on v3

--- a/solution.py
+++ b/solution.py
@@ -18,6 +18,10 @@
 
 def in_hbm(*arrays):
     return tuple(pltpu.with_memory_space_constraint(a, pltpu.HBM) for a in arrays)
+
+
+def in_vmem(*arrays):
+    return tuple(pltpu.with_memory_space_constraint(a, pltpu.VMEM) for a in arrays)
 
 
 def mm(a, b):
@@ -139,10 +143,11 @@
     return (pre * jax.nn.sigmoid(pre)).astype(bf16).astype(f32)
 
 
-def stats_kernel(pre_ref, cot_ref, gain_ref, out_ref, scaled_ref):
+def stats_kernel(where_ref, pre_ref, cot_ref, gain_ref, out_ref, scaled_ref):
     act = silu(pre_ref[...])
+    gain = gain_ref[:, pl.ds(pl.multiple_of(where_ref[2] * 256, 256), 256)]
     for d in range(cot_ref.shape[0]):
-        scaled_ref[4 * d : 4 * d + 4] = cot_ref[d].astype(f32) * gain_ref[...]
+        scaled_ref[4 * d : 4 * d + 4] = cot_ref[d].astype(f32) * gain
     mean = jnp.mean(act, axis=1, keepdims=True)
     center = act - mean
     scaled = scaled_ref[...]
@@ -159,9 +164,11 @@
         out_ref[d, 0], out_ref[d, 1], out_ref[d, 2] = rows[:, :128], rows[:, 128:], stats
 
 
-def local_stats(pre, cot, gain, towers):
+def local_stats(where, pre, cot, gain, towers):
     return pl.pallas_call(
         stats_kernel,
+        in_specs=[smem] + [vmem] * 3,
+        out_specs=[vmem] * 2,
         out_shape=[
             jax.ShapeDtypeStruct((towers, 3, 4, 128), f32),
             jax.ShapeDtypeStruct(pre.shape, f32),
@@ -169,7 +176,7 @@
         compiler_params=PARAMS,
         cost_estimate=cost(1),
         name="local_stats",
-    )(pre, cot, gain)
+    )(where, pre, cot, gain)
 
 
 def norm_kernel(got_ref, gain_ref, joint_ref):
@@ -273,63 +280,62 @@
     )(got, pre, scaled)
 
 
-def grads_kernel(per_step, where_ref, mine_ref, other_ref, weight_ref, *refs):
-    bag_ref, quot_ref, remd_ref, qhot_ref, rhot_ref, member_ref, out_ref, wg_ref, qg_ref, rg_ref = refs
-    half, step = pl.program_id(0), pl.program_id(1)
-
-    @pl.when((half == 0) & (step == 0))
-    def _():
-        wg_ref[...] = jnp.zeros_like(wg_ref)
-        qg_ref[...] = jnp.zeros_like(qg_ref)
-        rg_ref[...] = jnp.zeros_like(rg_ref)
-
-    weight_sum, quot_sum, rem_sum = wg_ref[...], qg_ref[...], rg_ref[...]
-    for i in range(per_step):
-        grad = jnp.where(half == 0, mine_ref[i], other_ref[i])
-        weight_sum += mm(bag_ref[0, i], grad)
-        look = mm(mm_nt(weight_ref[0], grad).astype(bf16), member_ref[0, i])
-        quot_part = (look * remd_ref[0, i].astype(f32)).astype(bf16)
-        rem_part = (look * quot_ref[0, i].astype(f32)).astype(bf16)
-        quot_sum += mm_nt(quot_part, qhot_ref[0, i])
-        rem_sum += mm_nt(rem_part, rhot_ref[0, i])
-    wg_ref[...], qg_ref[...], rg_ref[...] = weight_sum, quot_sum, rem_sum
-
-    @pl.when((half == pl.num_programs(0) - 1) & (step == pl.num_programs(1) - 1))
-    def _():
-        side = where_ref[1]
-        chunk = weight_sum.astype(bf16)
-        quot, rem = quot_sum.T, rem_sum.T
-        for z in range(out_ref.shape[0]):
-            near, far = quot[16 * z : 16 * z + 16], quot[128 + 16 * z : 144 + 16 * z]
-            first, second = jnp.where(side == 0, near, far), jnp.where(side == 0, far, near)
-            pair = jnp.concatenate([rem[16 * z : 16 * z + 8], rem[16 * z + 8 : 16 * z + 16]], axis=1)
-            out_ref[z, :128] = chunk
-            out_ref[z, 128:144] = jnp.concatenate([first, second], axis=1).astype(bf16)
-            out_ref[z, 144:160] = jnp.concatenate([pair, jnp.zeros_like(pair)], axis=0).astype(bf16)
+CUTS = ((0, 0, 2), (0, 2, 4), (0, 4, 8), (1, 0, 4), (1, 4, 8))
+
+
+def grads_kernel(where_ref, mine_ref, other_ref, weight_ref, *refs):
+    kept, out_ref, held, sems = refs[:6], refs[6], refs[7:13], refs[13]
+    own, side = where_ref[0], where_ref[1]
+    loads = []
+    for c, (half, low, high) in enumerate(CUTS):
+        part = pl.ds(low, high - low)
+        loads.append(
+            [
+                pltpu.make_async_copy(a.at[half, part], b.at[half, part], sems.at[c, i])
+                for i, (a, b) in enumerate(zip(kept, held))
+            ]
+        )
+    for copies in loads:
+        for copy in copies:
+            copy.start()
+    bags, quots, rems, quot_hot, rem_hot, member = held
+    weight = weight_ref[0, pl.ds(pl.multiple_of(own * 128, 128), 128), :]
+    weight_sum, quot_sum = jnp.zeros((128, 256), f32), jnp.zeros((128, 256), f32)
+    rem_sum = jnp.zeros((128, 128), f32)
+    for copies, (half, low, high) in zip(loads, CUTS):
+        for copy in copies:
+            copy.wait()
+        for z in range(low, high):
+            grad = (mine_ref, other_ref)[half][z]
+            weight_sum += mm(bags[half, z], grad)
+            look = mm(mm_nt(weight, grad).astype(bf16), member[half, z])
+            quot_part = (look * rems[half, z].astype(f32)).astype(bf16)
+            rem_part = (look * quots[half, z].astype(f32)).astype(bf16)
+            quot_sum += mm_nt(quot_part, quot_hot[half, z])
+            rem_sum += mm_nt(rem_part, rem_hot[half, z])
+    chunk = weight_sum.astype(bf16)
+    quot, rem = quot_sum.T, rem_sum.T
+    for z in range(out_ref.shape[0]):
+        near, far = quot[16 * z : 16 * z + 16], quot[128 + 16 * z : 144 + 16 * z]
+        first, second = jnp.where(side == 0, near, far), jnp.where(side == 0, far, near)
+        pair = jnp.concatenate([rem[16 * z : 16 * z + 8], rem[16 * z + 8 : 16 * z + 16]], axis=1)
+        rows = jnp.concatenate([jnp.concatenate([first, second], axis=1), pair], axis=0)
+        out_ref[z, :128] = chunk
+        out_ref[z, 128:] = rows.astype(bf16)
 
 
 def grads_part(where, mine, other, weight, *looked):
-    zs, per_step = mine.shape[0], 4
-    grads = pl.BlockSpec((per_step, 128, 256), lambda h, i, w: (i, 0, 0))
-    return pl.pallas_call(
-        functools.partial(grads_kernel, per_step),
-        grid_spec=pltpu.PrefetchScalarGridSpec(
-            num_scalar_prefetch=1,
-            grid=(2, zs // per_step),
-            in_specs=[grads, grads, pl.BlockSpec((1, 128, 256), lambda h, i, w: (0, w[0], 0))]
-            + [step_block(per_step, *a.shape[2:]) for a in looked],
-            out_specs=pl.BlockSpec((zs, 160, 256), lambda h, i, w: (0, 0, 0)),
-            scratch_shapes=[
-                pltpu.VMEM((128, 256), f32),
-                pltpu.VMEM((128, 256), f32),
-                pltpu.VMEM((128, 128), f32),
-            ],
-        ),
-        out_shape=jax.ShapeDtypeStruct((zs, 160, 256), bf16),
+    return pl.pallas_call(
+        grads_kernel,
+        in_specs=[smem] + [vmem] * 3 + [hbm] * 6,
+        out_specs=vmem,
+        out_shape=jax.ShapeDtypeStruct((mine.shape[0], 152, 256), bf16),
+        scratch_shapes=[pltpu.VMEM(a.shape, bf16) for a in looked]
+        + [pltpu.SemaphoreType.DMA((len(CUTS), 6))],
         compiler_params=PARAMS,
         cost_estimate=cost(8),
         name="grads_part",
-    )(where, mine, other, *in_hbm(weight, *looked))
+    )(where, mine, other, weight, *in_hbm(*looked))
 
 
 def spread_kernel(side_ref, mine_ref, other_ref, weight_ref, quot_ref, rem_ref):
@@ -337,15 +343,15 @@
     for z in range(mine_ref.shape[0]):
         for at, ref in ((side, mine_ref), (1 - side, other_ref)):
             weight_ref[z, at] = ref[z, :128].astype(f32)
-            rows = ref[z, 128:160].astype(f32)
+            rows = ref[z, 128:152].astype(f32)
             rows = jnp.where(side == 0, rows[:, :128], rows[:, 128:])
             quot_ref[z, at] = rows[:16]
-            rem_ref[z, at] = rows[16:24]
+            rem_ref[z, at] = rows[16:]
 
 
 def spread(side, mine, other):
     zs, step = mine.shape[0], 2
-    block = pl.BlockSpec((step, 160, 256), lambda i: (i, 0, 0))
+    block = pl.BlockSpec((step, 152, 256), lambda i: (i, 0, 0))
     sizes = [(128, 256), (16, 128), (8, 128)]
     return pl.pallas_call(
         spread_kernel,
@@ -379,18 +385,16 @@
     gather_z = functools.partial(swap, axis_name="shard", axis_index_groups=along_z)
     side = (shard & 1).astype(jnp.int32)
     side_arg = side[None]
-    where = jnp.stack([shard.astype(jnp.int32), side])
-    gain = norm_gain.astype(f32)[None]
-
-    gain_here = lax.dynamic_slice(norm_gain, (tower * 256,), (256,)).astype(f32)[None]
-
+    where = jnp.stack([shard, side, tower]).astype(jnp.int32)
     packed, picks = pack(quotient_rows, quotient_index, remainder_index, bag_sizes)
     mine, late = lax.optimization_barrier((gather_z(packed), cotangent[0]))
     other = lax.ppermute(mine, "shard", across)
     late = late.reshape(4, towers, 256).transpose(1, 0, 2)
     pre = tower_forward(side_arg, mine, other, remainder_rows, picks, tower_weight)
-    pre, cot = lax.optimization_barrier((pre, swap(late, "tower")))
-    sent, scaled = local_stats(pre, cot, gain_here, towers)
+    pre, norm_gain = lax.optimization_barrier((pre, norm_gain))
+    gain = norm_gain.astype(f32)[None]
+    pre, gain, cot = lax.optimization_barrier((pre, gain, swap(late, "tower")))
+    sent, scaled = local_stats(where, pre, cot, gain, towers)
     stats = swap(sent, "tower")
     grad_copies = tower_back(stats, pre, scaled, zs)
     joint = norm(stats, gain)

time: 135 us -> 133 us (0.985)
  transfers between devices with their start and end apart: 5 -> 5, of which waited for: 4 -> 4; matrix products, arithmetic and copies ran while one was open for 1% -> 0% of each run, Pallas kernels for 11% -> 12%
where the time goes in v4:
time: 133 us
  blocking collectives  66.5 us (50%)
  Pallas kernels  28.6 us (22%)
  starting transfers between devices  25.5 us (19%)
  waiting for transfers between devices  10.2 us (8%)
    all_to_all x1, blocking collectives, on_device(): mine, late = lax.optimization_barrier((gather_z(packed), cotangent[0]))  28.1 us
    all_to_all x1, blocking collectives, on_device(): gather_z(grads_part(where, grad_mine, grad_other, tower_weight, *looked))  22.5 us
    all_to_all x1, blocking collectives, on_device(): stats = swap(sent, 'tower')  15.9 us
    pallas_call x1, Pallas kernels, feature_pool(): pl.pallas_call(functools.partial(feature_kernel, per_step), grid_spec=plt...  9.69 us
    all_to_all x1, starting transfers between devices, on_device(): pre, gain, cot = lax.optimization_barrier((pre, gain, swap(late, 'tower')))  9.69 us
    pallas_call x1, Pallas kernels, grads_part(): pl.pallas_call(grads_kernel, in_specs=[smem] + [vmem] * 3 + [hbm] * 6, ou...  8.41 us
    ppermute x1, starting transfers between devices, on_device(): grad_other = lax.ppermute(grad_mine, 'shard', across)  5.59 us
    pallas_call x1, Pallas kernels, tower_forward(): pl.pallas_call(tower_kernel, in_specs=[smem] + [vmem] * 5, out_specs=vmem...  4.69 us
  transfers between devices with their start and end apart: 5, of which 4 were waited for; matrix products, arithmetic and copies ran while one was open for 0% of the time, Pallas kernels for 12%

profile of v4, /device:TPU:1, one launch (start us, length us, event | category | flops | bytes accessed | tf_op | source)
XLA Modules:
  0.0 132.7 jit_solution(3946499290677239850)
XLA Ops:
  0.6 0.0 copy-start
  0.6 1.1 pack.1
  1.7 0.0 copy-start.2
  1.7 28.1 %all_to_all.25.mine_ref = bf16[8,18,16,128]{3,2,1,0:T(8,128)(2,1)S(1)} all-to-all(bf16[8,18,16,128]{3,2,1,0:T(8,128)(2,1)S(1)} %get-tuple-element.32), channel_id=1, replica_groups={{0,2,4,6,8,10,12,14},{1,3,5,7,9,11,13,15},{16,18,20,22,24,26,28,30},{17..., dimensions={0} | all-to-all | bytes 1179648 | tf_op jit(solution)/shard_map/all_to_all | solution.py:390
  29.8 4.3 %collective-permute-start = (bf16[8,18,16,128]{3,2,1,0:T(8,128)(2,1)S(1)}, bf16[8,18,16,128]{3,2,1,0:T(8,128)(2,1)S(1)}, u32[]{:S(2)}, u32[]{:S(2)}) collective-permute-start(bf16[8,18,16,128]{3,2,1,0:T(8,128)(2,1)S(1)} %all_to_all.25.mine_ref), channel_id=1, source_target_pairs={{0,1},{1,0},{2,3},{3,2},{4,5},{5,4},{6,7},{7,6},{8,9},{9,8},{10,11... | collective-permute-start | bytes 1769480 | tf_op jit(solution)/shard_map/ppermute | solution.py:391
  34.2 9.7 %all-to-all-start.1 = ((bf16[32,4,256]{2,1,0:T(4,128)(2,1)}), bf16[32,4,256]{2,1,0:T(4,128)(2,1)S(1)}, u32[]{:S(2)}, u32[]{:S(2)}) async-start(bf16[32,4,256]{2,1,0:T(4,128)(2,1)} %bitcast.19), calls=%async_computation.1 | async-start | bytes 131072 | tf_op jit(solution)/shard_map/all_to_all | solution.py:396
  43.9 0.1 pad_add_fusion.where_ref
  43.9 0.0 collective-permute-done.other_ref
  43.9 0.0 copy-done
  43.9 0.0 copy-start.1
  43.9 1.0 copy-done.1
  45.0 4.7 %tower_forward.1.pre_ref = f32[128,256]{1,0:T(8,128)S(1)} custom-call(s32[1]{0:T(128)} %bitcast.1.side_ref, bf16[8,18,16,128]{3,2,1,0:T(8,128)(2,1)S(1)} %all_to_all.25.mine_ref, bf16[8,18,16,128]{3,2,1,0:T(8,128)(2,1)S(1)} %collective-permute-done.other_ref, bf16[16,128,128]{2,1,0:T(8,128)(2,1)S(1)} %copy-done.1, ...), custom_call_target="tpu_custom_call" | custom-call | flops 600000000 | bytes 18000000 | tf_op jit(solution)/shard_map/tower_forward/pallas_call | solution.py:131
  49.7 0.0 copy-done.2
  49.7 3.1 %all-to-all-done.1.cot_ref = bf16[32,4,256]{2,1,0:T(4,128)(2,1)S(1)} async-done(((bf16[32,4,256]{2,1,0:T(4,128)(2,1)}), bf16[32,4,256]{2,1,0:T(4,128)(2,1)S(1)}, u32[]{:S(2)}, u32[]{:S(2)}) %all-to-all-start.1) | async-done | bytes 65568 | tf_op jit(solution)/shard_map/all_to_all | solution.py:396
  52.8 0.8 local_stats.1
  53.6 15.9 %all_to_all.26.got_ref = f32[32,3,4,128]{3,2,1,0:T(4,128)S(1)} all-to-all(f32[32,3,4,128]{3,2,1,0:T(4,128)S(1)} %get-tuple-element.41), channel_id=1, replica_groups=mesh['tower'=32,'shard'=16] {'tower'}, dimensions={0} | all-to-all | bytes 393216 | tf_op jit(solution)/shard_map/all_to_all | solution.py:398
  69.5 1.2 tower_back.1
  70.7 3.5 %all-to-all-start.3 = ((bf16[8,128,256]{2,1,0:T(8,128)(2,1)}), bf16[8,128,256]{2,1,0:T(8,128)(2,1)S(1)}, u32[]{:S(2)}, u32[]{:S(2)}) async-start(bf16[8,128,256]{2,1,0:T(8,128)(2,1)} %tower_back.1), calls=%async_computation.3 | async-start | bytes 1048576 | tf_op jit(solution)/shard_map/all_to_all | solution.py:405
  74.2 9.7 %feature_pool.1 = (bf16[2,8,128,128]{3,2,1,0:T(8,128)(2,1)}, bf16[2,8,128,512]{3,2,1,0:T(8,128)(2,1)}, bf16[2,8,128,512]{3,2,1,0:T(8,128)(2,1)}, bf16[2,8,256,51...) custom-call(s32[3]{0:T(128)S(1)} %pad_add_fusion.where_ref, ...), custom_call_target="tpu_custom_call" | custom-call | flops 600000000 | bytes 18000000 | tf_op jit(solution)/shard_map/feature_pool/pallas_call | solution.py:231
  83.9 1.0 norm.1
  84.9 4.0 %all-to-all-done.3.mine_ref = bf16[8,128,256]{2,1,0:T(8,128)(2,1)S(1)} async-done(((bf16[8,128,256]{2,1,0:T(8,128)(2,1)}), bf16[8,128,256]{2,1,0:T(8,128)(2,1)S(1)}, u32[]{:S(2)}, u32[]{:S(2)}) %all-to-all-start.3) | async-done | bytes 524320 | tf_op jit(solution)/shard_map/all_to_all | solution.py:405
  88.8 5.6 %collective-permute-start.1 = (bf16[8,128,256]{2,1,0:T(8,128)(2,1)S(1)}, bf16[8,128,256]{2,1,0:T(8,128)(2,1)S(1)}, u32[]{:S(2)}, u32[]{:S(2)}) collective-permute-start(bf16[8,128,256]{2,1,0:T(8,128)(2,1)S(1)} %all-to-all-done.3.mine_ref), channel_id=1, source_target_pairs={{0,1},{1,0},{2,3},{3,2},{4,5},{5,4},{6,7},{7,6},{8,9},{9,8},{10,11... | collective-permute-start | bytes 1572872 | tf_op jit(solution)/shard_map/ppermute | solution.py:406
  94.4 1.5 %collective-permute-done.1.other_ref = bf16[8,128,256]{2,1,0:T(8,128)(2,1)S(1)} collective-permute-done((bf16[8,128,256]{2,1,0:T(8,128)(2,1)S(1)}, bf16[8,128,256]{2,1,0:T(8,128)(2,1)S(1)}, u32[]{:S(2)}, u32[]{:S(2)}) %collective-permute-start.1) | collective-permute-done | bytes 524320 | tf_op jit(solution)/shard_map/ppermute | solution.py:406
  95.9 8.4 %grads_part.1 = bf16[8,152,256]{2,1,0:T(8,128)(2,1)S(1)} custom-call(s32[3]{0:T(128)S(1)} %pad_add_fusion.where_ref, bf16[8,128,256]{2,1,0:T(8,128)(2,1)S(1)} %all-to-all-done.3.mine_ref, bf16[8,128,256]{2,1,0:T(8,128)(2,1)S(1)} %collective-permute-done.1.other_ref, bf16[1,2048,256]{2,1,0:T(8,128)(2,1)S(1)} %copy-done, ...), custom_call_target="tpu_custom_call" | custom-call | flops 800000000 | bytes 24000000 | tf_op jit(solution)/shard_map/grads_part/pallas_call | solution.py:328
  104.4 22.5 %all_to_all.27.mine_ref = bf16[8,152,256]{2,1,0:T(8,128)(2,1)S(1)} all-to-all(bf16[8,152,256]{2,1,0:T(8,128)(2,1)S(1)} %grads_part.1), channel_id=1, replica_groups={{0,2,4,6,8,10,12,14},{1,3,5,7,9,11,13,15},{16,18,20,22,24,26,28,30},{17..., dimensions={0} | all-to-all | bytes 1245184 | tf_op jit(solution)/shard_map/all_to_all | solution.py:407
  126.8 2.4 %collective-permute-start.2 = (bf16[8,152,256]{2,1,0:T(8,128)(2,1)S(1)}, bf16[8,152,256]{2,1,0:T(8,128)(2,1)S(1)}, u32[]{:S(2)}, u32[]{:S(2)}) collective-permute-start(bf16[8,152,256]{2,1,0:T(8,128)(2,1)S(1)} %all_to_all.27.mine_ref), channel_id=1, source_target_pairs={{0,1},{1,0},{2,3},{3,2},{4,5},{5,4},{6,7},{7,6},{8,9},{9,8},{10,11... | collective-permute-start | bytes 1867784 | tf_op jit(solution)/shard_map/ppermute | solution.py:408
  129.2 1.7 %collective-permute-done.2.other_ref = bf16[8,152,256]{2,1,0:T(8,128)(2,1)S(1)} collective-permute-done((bf16[8,152,256]{2,1,0:T(8,128)(2,1)S(1)}, bf16[8,152,256]{2,1,0:T(8,128)(2,1)S(1)}, u32[]{:S(2)}, u32[]{:S(2)}) %collective-permute-start.2) | collective-permute-done | bytes 622624 | tf_op jit(solution)/shard_map/ppermute | solution.py:408
  130.9 1.9 %spread.1 = (f32[8,2,128,256]{3,2,1,0:T(8,128)}, f32[8,2,16,128]{3,2,1,0:T(8,128)}, f32[8,2,8,128]{3,2,1,0:T(8,128)}) custom-call(s32[1]{0:T(128)} %bitcast.1.side_ref, bf16[8,152,256]{2,1,0:T(8,128)(2,1)S(1)} %all_to_all.27.mine_ref, bf16[8,152,256]{2,1,0:T(8,128)(2,1)S(1)} %collective-permute-done.2.other_ref), custom_call_target="tpu_custom_call" | custom-call | flops 200000000 | bytes 6000000 | tf_op jit(solution)/shard_map/spread/pallas_call | solution.py:356
  (4 shorter events, 0.0 us)
Async XLA Ops:
  0.6 43.3 %copy-start = (bf16[1,2048,256]{2,1,0:T(8,128)(2,1)S(1)}, bf16[1,2048,256]{2,1,0:T(8,128)(2,1)}, u32[]{:S(2)}) copy-start(bf16[1,2048,256]{2,1,0:T(8,128)(2,1)} %weight_ref.3) | copy-start | bytes 3145732
  1.7 48.0 %copy-start.2 = (bf16[8192]{0:T(1024)(128)(2,1)S(1)}, bf16[8192]{0:T(1024)(128)(2,1)}, u32[]{:S(2)}) copy-start(bf16[8192]{0:T(1024)(128)(2,1)} %param.14) | copy-start | bytes 49156
  29.8 14.1 %collective-permute-start = (bf16[8,18,16,128]{3,2,1,0:T(8,128)(2,1)S(1)}, bf16[8,18,16,128]{3,2,1,0:T(8,128)(2,1)S(1)}, u32[]{:S(2)}, u32[]{:S(2)}) collective-permute-start(bf16[8,18,16,128]{3,2,1,0:T(8,128)(2,1)S(1)} %all_to_all.25.mine_ref), channel_id=1, source_target_pairs={{0,1},{1,0},{2,3},{3,2},{4,5},{5,4},{6,7},{7,6},{8,9},{9,8},{10,11... | collective-permute-start | bytes 1769480 | tf_op jit(solution)/shard_map/ppermute | solution.py:391
  34.2 18.6 %all-to-all-start.1 = ((bf16[32,4,256]{2,1,0:T(4,128)(2,1)}), bf16[32,4,256]{2,1,0:T(4,128)(2,1)S(1)}, u32[]{:S(2)}, u32[]{:S(2)}) async-start(bf16[32,4,256]{2,1,0:T(4,128)(2,1)} %bitcast.19), calls=%async_computation.1 | async-start | bytes 131072 | tf_op jit(solution)/shard_map/all_to_all | solution.py:396
  43.9 1.0 copy-start.1
  70.7 18.2 %all-to-all-start.3 = ((bf16[8,128,256]{2,1,0:T(8,128)(2,1)}), bf16[8,128,256]{2,1,0:T(8,128)(2,1)S(1)}, u32[]{:S(2)}, u32[]{:S(2)}) async-start(bf16[8,128,256]{2,1,0:T(8,128)(2,1)} %tower_back.1), calls=%async_computation.3 | async-start | bytes 1048576 | tf_op jit(solution)/shard_map/all_to_all | solution.py:405
  88.8 7.1 %collective-permute-start.1 = (bf16[8,128,256]{2,1,0:T(8,128)(2,1)S(1)}, bf16[8,128,256]{2,1,0:T(8,128)(2,1)S(1)}, u32[]{:S(2)}, u32[]{:S(2)}) collective-permute-start(bf16[8,128,256]{2,1,0:T(8,128)(2,1)S(1)} %all-to-all-done.3.mine_ref), channel_id=1, source_target_pairs={{0,1},{1,0},{2,3},{3,2},{4,5},{5,4},{6,7},{7,6},{8,9},{9,8},{10,11... | collective-permute-start | bytes 1572872 | tf_op jit(solution)/shard_map/ppermute | solution.py:406
  126.8 4.0 %collective-permute-start.2 = (bf16[8,152,256]{2,1,0:T(8,128)(2,1)S(1)}, bf16[8,152,256]{2,1,0:T(8,128)(2,1)S(1)}, u32[]{:S(2)}, u32[]{:S(2)}) collective-permute-start(bf16[8,152,256]{2,1,0:T(8,128)(2,1)S(1)} %all_to_all.27.mine_ref), channel_id=1, source_target_pairs={{0,1},{1,0},{2,3},{3,2},{4,5},{5,4},{6,7},{7,6},{8,9},{9,8},{10,11... | collective-permute-start | bytes 1867784 | tf_op jit(solution)/shard_map/ppermute | solution.py:408

commit v5 on v4

--- a/solution.py
+++ b/solution.py
@@ -65,13 +65,11 @@
     return tuple(jnp.concatenate(v, axis=1) for v in (quot, rem, member))
 
 
-def look_up(quot_t, rem_t, quot_hot, rem_hot, member):
-    quot = mm(quot_t, quot_hot)
-    rem = mm(rem_t, rem_hot)
+def pool(quot, rem, member):
     composed = quot * rem
     high = composed.astype(bf16)
     low = (composed - high.astype(f32)).astype(bf16)
-    return quot, rem, mm_nt(member, high) + mm_nt(member, low)
+    return mm_nt(member, high) + mm_nt(member, low)
 
 
 def pack_kernel(rows_ref, quot_ref, rem_ref, size_ref, out_ref, picks_ref, held):
@@ -114,38 +112,56 @@
     )(*pinned)
 
 
-def tower_kernel(side_ref, mine_ref, other_ref, rem_ref, picks_ref, weight_ref, pre_ref):
+AHEAD = 2
+
+
+def tower_kernel(mine_ref, other_ref, rem_ref, picks_ref, weight_ref, pre_ref, held, sem):
+    fetch = pltpu.make_async_copy(rem_ref, held, sem)
+    fetch.start()
     tri = triangles(128)
-    side = side_ref[0]
-    bags = []
-    for f in range(rem_ref.shape[0]):
-        table = jnp.concatenate(
-            [mine_ref[:, f].reshape(128, 128), other_ref[:, f].reshape(128, 128)], axis=0
-        )
-        _, _, pooled = look_up(table.T, rem_ref[f].T, *masks(picks_ref[f], side, tri))
-        bags.append(pooled.astype(bf16))
+    _, side = place()
+    bags, ahead, feats = [], [], rem_ref.shape[0]
+    for f in range(feats + AHEAD):
+        if f < feats:
+            table = jnp.concatenate(
+                [mine_ref[:, f].reshape(128, 128), other_ref[:, f].reshape(128, 128)], axis=0
+            )
+            quot_hot, rem_hot, member = masks(picks_ref[f], side, tri)
+            ahead.append((mm(table.T, quot_hot), rem_hot, member))
+        if f == AHEAD:
+            fetch.wait()
+        if f >= AHEAD:
+            quot, rem_hot, member = ahead[f - AHEAD]
+            bags.append(pool(quot, mm(held[f - AHEAD].T, rem_hot), member).astype(bf16))
     pre_ref[...] = mm(jnp.concatenate(bags, axis=1), weight_ref[0])
 
 
-def tower_forward(side, mine, other, remainder, picks, weight):
+def tower_forward(mine, other, remainder, picks, weight):
     return pl.pallas_call(
         tower_kernel,
-        in_specs=[smem] + [vmem] * 5,
+        in_specs=[vmem] * 2 + [hbm] + [vmem] * 2,
         out_specs=vmem,
         out_shape=jax.ShapeDtypeStruct((128, 256), f32),
+        scratch_shapes=[pltpu.VMEM(remainder.shape, bf16), pltpu.SemaphoreType.DMA],
         compiler_params=PARAMS,
         cost_estimate=cost(6),
         name="tower_forward",
-    )(side, mine, other, remainder, picks, weight)
+    )(mine, other, *in_hbm(remainder), picks, weight)
+
+
+def place():
+    shard = lax.axis_index("shard").astype(jnp.int32)
+    return shard, shard & 1
 
 
 def silu(pre):
     return (pre * jax.nn.sigmoid(pre)).astype(bf16).astype(f32)
 
 
-def stats_kernel(where_ref, pre_ref, cot_ref, gain_ref, out_ref, scaled_ref):
+def stats_kernel(pre_ref, cot_ref, gain_ref, out_ref, scaled_ref):
     act = silu(pre_ref[...])
-    gain = gain_ref[:, pl.ds(pl.multiple_of(where_ref[2] * 256, 256), 256)]
+    tower = lax.axis_index("tower").astype(jnp.int32)
+    gain = gain_ref[:, pl.ds(pl.multiple_of(tower * 256, 256), 256)]
     for d in range(cot_ref.shape[0]):
         scaled_ref[4 * d : 4 * d + 4] = cot_ref[d].astype(f32) * gain
     mean = jnp.mean(act, axis=1, keepdims=True)
@@ -164,10 +180,10 @@
         out_ref[d, 0], out_ref[d, 1], out_ref[d, 2] = rows[:, :128], rows[:, 128:], stats
 
 
-def local_stats(where, pre, cot, gain, towers):
+def local_stats(pre, cot, gain, towers):
     return pl.pallas_call(
         stats_kernel,
-        in_specs=[smem] + [vmem] * 3,
+        in_specs=[vmem] * 3,
         out_specs=[vmem] * 2,
         out_shape=[
             jax.ShapeDtypeStruct((towers, 3, 4, 128), f32),
@@ -176,7 +192,7 @@
         compiler_params=PARAMS,
         cost_estimate=cost(1),
         name="local_stats",
-    )(where, pre, cot, gain)
+    )(pre, cot, gain)
 
 
 def norm_kernel(got_ref, gain_ref, joint_ref):
@@ -214,8 +230,8 @@
     tri = triangles(128)
     for i in range(per_step):
         hot = masks(picks_ref[0, i], where_ref[1], tri)
-        quot, rem, pooled = look_up(qt_ref[...], rt_ref[...], *hot)
-        bag_ref[0, i] = pooled.T.astype(bf16)
+        quot, rem = mm(qt_ref[...], hot[0]), mm(rt_ref[...], hot[1])
+        bag_ref[0, i] = pool(quot, rem, hot[2]).T.astype(bf16)
         quot_ref[0, i], remd_ref[0, i] = quot.astype(bf16), rem.astype(bf16)
         qhot_ref[0, i], rhot_ref[0, i], member_ref[0, i] = hot
 
@@ -280,18 +296,17 @@
     )(got, pre, scaled)
 
 
-CUTS = ((0, 0, 2), (0, 2, 4), (0, 4, 8), (1, 0, 4), (1, 4, 8))
-
-
-def grads_kernel(where_ref, mine_ref, other_ref, weight_ref, *refs):
-    kept, out_ref, held, sems = refs[:6], refs[6], refs[7:13], refs[13]
-    own, side = where_ref[0], where_ref[1]
+CUTS = ((0, 2), (2, 4), (4, 8))
+
+
+def half_sums(half, grad_ref, weight_ref, kept, held, sems, sums):
+    own, _ = place()
     loads = []
-    for c, (half, low, high) in enumerate(CUTS):
+    for c, (low, high) in enumerate(CUTS):
         part = pl.ds(low, high - low)
         loads.append(
             [
-                pltpu.make_async_copy(a.at[half, part], b.at[half, part], sems.at[c, i])
+                pltpu.make_async_copy(a.at[half, part], b.at[part], sems.at[c, i])
                 for i, (a, b) in enumerate(zip(kept, held))
             ]
         )
@@ -300,21 +315,36 @@
             copy.start()
     bags, quots, rems, quot_hot, rem_hot, member = held
     weight = weight_ref[0, pl.ds(pl.multiple_of(own * 128, 128), 128), :]
-    weight_sum, quot_sum = jnp.zeros((128, 256), f32), jnp.zeros((128, 256), f32)
-    rem_sum = jnp.zeros((128, 128), f32)
-    for copies, (half, low, high) in zip(loads, CUTS):
+    weight_sum, quot_sum, rem_sum = sums
+    for copies, (low, high) in zip(loads, CUTS):
         for copy in copies:
             copy.wait()
         for z in range(low, high):
-            grad = (mine_ref, other_ref)[half][z]
-            weight_sum += mm(bags[half, z], grad)
-            look = mm(mm_nt(weight, grad).astype(bf16), member[half, z])
-            quot_part = (look * rems[half, z].astype(f32)).astype(bf16)
-            rem_part = (look * quots[half, z].astype(f32)).astype(bf16)
-            quot_sum += mm_nt(quot_part, quot_hot[half, z])
-            rem_sum += mm_nt(rem_part, rem_hot[half, z])
-    chunk = weight_sum.astype(bf16)
-    quot, rem = quot_sum.T, rem_sum.T
+            grad = grad_ref[z]
+            weight_sum += mm(bags[z], grad)
+            look = mm(mm_nt(weight, grad).astype(bf16), member[z])
+            quot_part = (look * rems[z].astype(f32)).astype(bf16)
+            rem_part = (look * quots[z].astype(f32)).astype(bf16)
+            quot_sum += mm_nt(quot_part, quot_hot[z])
+            rem_sum += mm_nt(rem_part, rem_hot[z])
+    return weight_sum, quot_sum, rem_sum
+
+
+SUMS = ((128, 256), (128, 256), (128, 128))
+
+
+def first_kernel(grad_ref, weight_ref, *refs):
+    kept, outs, held, sems = refs[:6], refs[6:9], refs[9:15], refs[15]
+    sums = tuple(jnp.zeros(s, f32) for s in SUMS)
+    for ref, value in zip(outs, half_sums(0, grad_ref, weight_ref, kept, held, sems, sums)):
+        ref[...] = value
+
+
+def second_kernel(grad_ref, weight_ref, *refs):
+    kept, begun, out_ref, held, sems = refs[:6], refs[6:9], refs[9], refs[10:16], refs[16]
+    sums = half_sums(1, grad_ref, weight_ref, kept, held, sems, tuple(ref[...] for ref in begun))
+    _, side = place()
+    chunk, quot, rem = sums[0].astype(bf16), sums[1].T, sums[2].T
     for z in range(out_ref.shape[0]):
         near, far = quot[16 * z : 16 * z + 16], quot[128 + 16 * z : 144 + 16 * z]
         first, second = jnp.where(side == 0, near, far), jnp.where(side == 0, far, near)
@@ -324,45 +354,78 @@
         out_ref[z, 128:] = rows.astype(bf16)
 
 
-def grads_part(where, mine, other, weight, *looked):
-    return pl.pallas_call(
-        grads_kernel,
-        in_specs=[smem] + [vmem] * 3 + [hbm] * 6,
-        out_specs=vmem,
-        out_shape=jax.ShapeDtypeStruct((mine.shape[0], 152, 256), bf16),
-        scratch_shapes=[pltpu.VMEM(a.shape, bf16) for a in looked]
+def grads_call(kernel, name, out_shape, grad, weight, looked, *begun):
+    return pl.pallas_call(
+        kernel,
+        in_specs=[vmem] * 2 + [hbm] * 6 + [vmem] * len(begun),
+        out_specs=jax.tree.map(lambda _: vmem, out_shape),
+        out_shape=out_shape,
+        scratch_shapes=[pltpu.VMEM(a.shape[1:], bf16) for a in looked]
         + [pltpu.SemaphoreType.DMA((len(CUTS), 6))],
         compiler_params=PARAMS,
-        cost_estimate=cost(8),
-        name="grads_part",
-    )(where, mine, other, weight, *in_hbm(*looked))
-
-
-def spread_kernel(side_ref, mine_ref, other_ref, weight_ref, quot_ref, rem_ref):
+        cost_estimate=cost(4),
+        name=name,
+    )(grad, weight, *in_hbm(*looked), *begun)
+
+
+def grads_part(mine, other, weight, *looked):
+    begun = [jax.ShapeDtypeStruct(s, f32) for s in SUMS]
+    begun = grads_call(first_kernel, "grads_first", begun, mine, weight, looked)
+    sent = jax.ShapeDtypeStruct((mine.shape[0], 152, 256), bf16)
+    return grads_call(second_kernel, "grads_second", sent, other, weight, looked, *begun)
+
+
+def widen_kernel(side_ref, got_ref, out_ref):
+    out_ref[:, 0] = got_ref[...].astype(f32)
+
+
+def widen(side, mine):
+    zs, step = mine.shape[0], 4
+    return pl.pallas_call(
+        widen_kernel,
+        grid_spec=pltpu.PrefetchScalarGridSpec(
+            num_scalar_prefetch=1,
+            grid=(zs // step,),
+            in_specs=[pl.BlockSpec((step, 128, 256), lambda i, s: (i, 0, 0))],
+            out_specs=pl.BlockSpec((step, 1, 128, 256), lambda i, s: (i, s[0], 0, 0)),
+        ),
+        out_shape=jax.ShapeDtypeStruct((zs, 2, 128, 256), f32),
+        compiler_params=PARAMS,
+        cost_estimate=cost(1),
+        name="widen",
+    )(side, mine)
+
+
+def spread_kernel(side_ref, begun_ref, mine_ref, other_ref, weight_ref, quot_ref, rem_ref):
     side = side_ref[0]
+    weight_ref[:, 0] = other_ref[:, :128].astype(f32)
     for z in range(mine_ref.shape[0]):
         for at, ref in ((side, mine_ref), (1 - side, other_ref)):
-            weight_ref[z, at] = ref[z, :128].astype(f32)
-            rows = ref[z, 128:152].astype(f32)
+            rows = ref[z, 128:].astype(f32)
             rows = jnp.where(side == 0, rows[:, :128], rows[:, 128:])
             quot_ref[z, at] = rows[:16]
             rem_ref[z, at] = rows[16:]
 
 
-def spread(side, mine, other):
-    zs, step = mine.shape[0], 2
-    block = pl.BlockSpec((step, 152, 256), lambda i: (i, 0, 0))
+def spread(side, begun, mine, other):
+    zs, step = mine.shape[0], 4
+    block = pl.BlockSpec((step, 152, 256), lambda i, s: (i, 0, 0))
     sizes = [(128, 256), (16, 128), (8, 128)]
     return pl.pallas_call(
         spread_kernel,
-        grid=(zs // step,),
-        in_specs=[smem, block, block],
-        out_specs=[pl.BlockSpec((step, 2, *s), lambda i: (i, 0, 0, 0)) for s in sizes],
+        grid_spec=pltpu.PrefetchScalarGridSpec(
+            num_scalar_prefetch=1,
+            grid=(zs // step,),
+            in_specs=[hbm, block, block],
+            out_specs=[pl.BlockSpec((step, 1, 128, 256), lambda i, s: (i, 1 - s[0], 0, 0))]
+            + [pl.BlockSpec((step, 2, *s), lambda i, s: (i, 0, 0, 0)) for s in sizes[1:]],
+        ),
         out_shape=[jax.ShapeDtypeStruct((zs, 2, *s), f32) for s in sizes],
+        input_output_aliases={1: 0},
         compiler_params=PARAMS,
         cost_estimate=cost(2),
         name="spread",
-    )(side, mine, other)
+    )(side, begun, mine, other)
 
 
 def on_device(
@@ -377,7 +440,7 @@
 ):
     feats = quotient_rows.shape[0]
     shards, towers = lax.axis_size("shard"), lax.axis_size("tower")
-    shard, tower = lax.axis_index("shard"), lax.axis_index("tower")
+    shard = lax.axis_index("shard")
     zs = shards // 2
     along_z = [[2 * z + c for z in range(zs)] for c in range(2)]
     across = [(i, i ^ 1) for i in range(shards)]
@@ -385,16 +448,16 @@
     gather_z = functools.partial(swap, axis_name="shard", axis_index_groups=along_z)
     side = (shard & 1).astype(jnp.int32)
     side_arg = side[None]
-    where = jnp.stack([shard, side, tower]).astype(jnp.int32)
+    where = jnp.stack([shard, side]).astype(jnp.int32)
     packed, picks = pack(quotient_rows, quotient_index, remainder_index, bag_sizes)
     mine, late = lax.optimization_barrier((gather_z(packed), cotangent[0]))
     other = lax.ppermute(mine, "shard", across)
     late = late.reshape(4, towers, 256).transpose(1, 0, 2)
-    pre = tower_forward(side_arg, mine, other, remainder_rows, picks, tower_weight)
+    pre = tower_forward(mine, other, remainder_rows, picks, tower_weight)
     pre, norm_gain = lax.optimization_barrier((pre, norm_gain))
     gain = norm_gain.astype(f32)[None]
     pre, gain, cot = lax.optimization_barrier((pre, gain, swap(late, "tower")))
-    sent, scaled = local_stats(where, pre, cot, gain, towers)
+    sent, scaled = local_stats(pre, cot, gain, towers)
     stats = swap(sent, "tower")
     grad_copies = tower_back(stats, pre, scaled, zs)
     joint = norm(stats, gain)
@@ -404,9 +467,10 @@
     looked = feature_pool(where, mine, other, remainder_rows, all_picks)
     grad_mine, joint, *looked = lax.optimization_barrier((gather_z(grad_copies), joint, *looked))
     grad_other = lax.ppermute(grad_mine, "shard", across)
-    got_mine = gather_z(grads_part(where, grad_mine, grad_other, tower_weight, *looked))
+    got_mine = gather_z(grads_part(grad_mine, grad_other, tower_weight, *looked))
     got_other = lax.ppermute(got_mine, "shard", across)
-    weight_grad, quot_grad, rem_grad = spread(side_arg, got_mine, got_other)
+    begun = widen(side_arg, got_mine)
+    weight_grad, quot_grad, rem_grad = spread(side_arg, begun, got_mine, got_other)
     return (
         joint,
         weight_grad.reshape(1, feats * 128, 256),

time: 133 us -> 131 us (0.985)
  waiting for transfers between devices: 10.2 us -> 7.9 us
  Pallas kernels: 28.6 us -> 30 us
    ppermute x1, waiting for transfers between devices: 1.51 us -> 0.01 us  [on_device(): grad_other = lax.ppermute(grad_mine, 'shard', across)]
    pallas_call x4 -> x6, Pallas kernels: 15.8 us -> 17.1 us  [the longest x2 9.21 us: grads_call(): pl.pallas_call(kernel, in_specs=[vmem] * 2 + [hbm] * 6 + [vmem] * len(beg...]
  transfers between devices with their start and end apart: 5 -> 5, of which waited for: 4 -> 3; matrix products, arithmetic and copies ran while one was open for 0% -> 0% of each run, Pallas kernels for 12% -> 17%
where the time goes in v5:
time: 131 us; the launch traced here: 130 us
  blocking collectives  66.2 us (51%)
  Pallas kernels  30 us (23%)
  starting transfers between devices  25.4 us (19%)
  waiting for transfers between devices  7.9 us (6%)
    all_to_all x1, blocking collectives, on_device(): mine, late = lax.optimization_barrier((gather_z(packed), cotangent[0]))  28.1 us
    all_to_all x1, blocking collectives, on_device(): gather_z(grads_part(grad_mine, grad_other, tower_weight, *looked))  22.5 us
    all_to_all x1, blocking collectives, on_device(): stats = swap(sent, 'tower')  15.6 us
    pallas_call x1, Pallas kernels, feature_pool(): pl.pallas_call(functools.partial(feature_kernel, per_step), grid_spec=plt...  9.68 us
    all_to_all x1, starting transfers between devices, on_device(): pre, gain, cot = lax.optimization_barrier((pre, gain, swap(late, 'tower')))  9.68 us
    pallas_call x2, Pallas kernels, grads_call(): pl.pallas_call(kernel, in_specs=[vmem] * 2 + [hbm] * 6 + [vmem] * len(beg...  9.21 us
    ppermute x1, starting transfers between devices, on_device(): grad_other = lax.ppermute(grad_mine, 'shard', across)  5.59 us
    pallas_call x1, Pallas kernels, tower_forward(): pl.pallas_call(tower_kernel, in_specs=[vmem] * 2 + [hbm] + [vmem] * 2, ou...  5.48 us
  transfers between devices with their start and end apart: 5, of which 3 were waited for; matrix products, arithmetic and copies ran while one was open for 0% of the time, Pallas kernels for 17%

profile of v5, /device:TPU:1, one launch (start us, length us, event | category | flops | bytes accessed | tf_op | source)
XLA Modules:
  0.0 130.4 jit_solution(15680047704089624307)
XLA Ops:
  0.6 0.0 copy-start
  0.6 1.1 pack.1
  1.7 0.0 copy-start.1
  1.7 28.1 %all_to_all.25.mine_ref = bf16[8,18,16,128]{3,2,1,0:T(8,128)(2,1)S(1)} all-to-all(bf16[8,18,16,128]{3,2,1,0:T(8,128)(2,1)S(1)} %get-tuple-element.35), channel_id=1, replica_groups={{0,2,4,6,8,10,12,14},{1,3,5,7,9,11,13,15},{16,18,20,22,24,26,28,30},{17..., dimensions={0} | all-to-all | bytes 1179648 | tf_op jit(solution)/shard_map/all_to_all | solution.py:453
  29.8 4.3 %collective-permute-start = (bf16[8,18,16,128]{3,2,1,0:T(8,128)(2,1)S(1)}, bf16[8,18,16,128]{3,2,1,0:T(8,128)(2,1)S(1)}, u32[]{:S(2)}, u32[]{:S(2)}) collective-permute-start(bf16[8,18,16,128]{3,2,1,0:T(8,128)(2,1)S(1)} %all_to_all.25.mine_ref), channel_id=1, source_target_pairs={{0,1},{1,0},{2,3},{3,2},{4,5},{5,4},{6,7},{7,6},{8,9},{9,8},{10,11... | collective-permute-start | bytes 1769480 | tf_op jit(solution)/shard_map/ppermute | solution.py:454
  34.2 9.7 %all-to-all-start.1 = ((bf16[32,4,256]{2,1,0:T(4,128)(2,1)}), bf16[32,4,256]{2,1,0:T(4,128)(2,1)S(1)}, u32[]{:S(2)}, u32[]{:S(2)}) async-start(bf16[32,4,256]{2,1,0:T(4,128)(2,1)} %bitcast.19), calls=%async_computation.1 | async-start | bytes 131072 | tf_op jit(solution)/shard_map/all_to_all | solution.py:459
  43.8 0.0 collective-permute-done.other_ref
  43.9 0.0 copy-done
  43.9 5.5 %tower_forward.1.pre_ref = f32[128,256]{1,0:T(8,128)S(1)} custom-call(bf16[8,18,16,128]{3,2,1,0:T(8,128)(2,1)S(1)} %all_to_all.25.mine_ref, bf16[8,18,16,128]{3,2,1,0:T(8,128)(2,1)S(1)} %collective-permute-done.other_ref, bf16[16,128,128]{2,1,0:T(8,128)(2,1)} %rem_ref.5, bf16[16,16,128]{2,1,0:T(8,128)(2,1)S(1)} %get-tuple-element.37.picks_ref, ...), custom_call_target="tpu_custom_call" | custom-call | flops 600000000 | bytes 18000000 | tf_op jit(solution)/shard_map/tower_forward/pallas_call | solution.py:140
  49.4 0.0 copy-done.1
  49.4 3.4 %all-to-all-done.1.cot_ref = bf16[32,4,256]{2,1,0:T(4,128)(2,1)S(1)} async-done(((bf16[32,4,256]{2,1,0:T(4,128)(2,1)}), bf16[32,4,256]{2,1,0:T(4,128)(2,1)S(1)}, u32[]{:S(2)}, u32[]{:S(2)}) %all-to-all-start.1) | async-done | bytes 65568 | tf_op jit(solution)/shard_map/all_to_all | solution.py:459
  52.8 0.3 local_stats.1
  53.1 15.6 %all_to_all.26.got_ref = f32[32,3,4,128]{3,2,1,0:T(4,128)S(1)} all-to-all(f32[32,3,4,128]{3,2,1,0:T(4,128)S(1)} %get-tuple-element.44), channel_id=1, replica_groups=mesh['tower'=32,'shard'=16] {'tower'}, dimensions={0} | all-to-all | bytes 393216 | tf_op jit(solution)/shard_map/all_to_all | solution.py:461
  68.6 1.2 tower_back.1
  69.8 3.5 %all-to-all-start.3 = ((bf16[8,128,256]{2,1,0:T(8,128)(2,1)}), bf16[8,128,256]{2,1,0:T(8,128)(2,1)S(1)}, u32[]{:S(2)}, u32[]{:S(2)}) async-start(bf16[8,128,256]{2,1,0:T(8,128)(2,1)} %tower_back.1), calls=%async_computation.3 | async-start | bytes 1048576 | tf_op jit(solution)/shard_map/all_to_all | solution.py:468
  73.3 0.1 pad_add_fusion.where_ref
  73.4 9.7 %feature_pool.1 = (bf16[2,8,128,128]{3,2,1,0:T(8,128)(2,1)}, bf16[2,8,128,512]{3,2,1,0:T(8,128)(2,1)}, bf16[2,8,128,512]{3,2,1,0:T(8,128)(2,1)}, bf16[2,8,256,51...) custom-call(s32[2]{0:T(128)S(1)} %pad_add_fusion.where_ref, ...), custom_call_target="tpu_custom_call" | custom-call | flops 600000000 | bytes 18000000 | tf_op jit(solution)/shard_map/feature_pool/pallas_call | solution.py:247
  83.1 1.0 norm.1
  84.1 3.9 %all-to-all-done.3.grad_ref = bf16[8,128,256]{2,1,0:T(8,128)(2,1)S(1)} async-done(((bf16[8,128,256]{2,1,0:T(8,128)(2,1)}), bf16[8,128,256]{2,1,0:T(8,128)(2,1)S(1)}, u32[]{:S(2)}, u32[]{:S(2)}) %all-to-all-start.3) | async-done | bytes 524320 | tf_op jit(solution)/shard_map/all_to_all | solution.py:468
  88.0 5.6 %collective-permute-start.1 = (bf16[8,128,256]{2,1,0:T(8,128)(2,1)S(1)}, bf16[8,128,256]{2,1,0:T(8,128)(2,1)S(1)}, u32[]{:S(2)}, u32[]{:S(2)}) collective-permute-start(bf16[8,128,256]{2,1,0:T(8,128)(2,1)S(1)} %all-to-all-done.3.grad_ref), channel_id=1, source_target_pairs={{0,1},{1,0},{2,3},{3,2},{4,5},{5,4},{6,7},{7,6},{8,9},{9,8},{10,11... | collective-permute-start | bytes 1572872 | tf_op jit(solution)/shard_map/ppermute | solution.py:469
  93.6 4.7 %grads_first.1 = (f32[128,256]{1,0:T(8,128)S(1)}, f32[128,256]{1,0:T(8,128)S(1)}, f32[128,128]{1,0:T(8,128)S(1)}) custom-call(bf16[8,128,256]{2,1,0:T(8,128)(2,1)S(1)} %all-to-all-done.3.grad_ref, bf16[1,2048,256]{2,1,0:T(8,128)(2,1)S(1)} %copy-done, bf16[2,8,128,128]{3,2,1,0:T(8,128)(2,1)} %get-tuple-element.54.refs_0_, ...), custom_call_target="tpu_custom_call" | custom-call | flops 400000000 | bytes 12000000 | tf_op jit(solution)/shard_map/grads_first/pallas_call | solution.py:358
  98.2 0.0 collective-permute-done.1.grad_ref
  98.2 4.6 %grads_second.1 = bf16[8,152,256]{2,1,0:T(8,128)(2,1)S(1)} custom-call(bf16[8,128,256]{2,1,0:T(8,128)(2,1)S(1)} %collective-permute-done.1.grad_ref, bf16[1,2048,256]{2,1,0:T(8,128)(2,1)S(1)} %copy-done, bf16[2,8,128,128]{3,2,1,0:T(8,128)(2,1)} %get-tuple-element.54.refs_0_, bf16[2,8,128,512]{3,2,1,0:T(8,128)(2,1)} %get-tuple-element.55.refs_1_, ...), custom_call_target="tpu_custom_call" | custom-call | flops 400000000 | bytes 12000000 | tf_op jit(solution)/shard_map/grads_second/pallas_call | solution.py:358
  102.8 22.5 %all_to_all.27.got_ref.mine_ref = bf16[8,152,256]{2,1,0:T(8,128)(2,1)S(1)} all-to-all(bf16[8,152,256]{2,1,0:T(8,128)(2,1)S(1)} %grads_second.1), channel_id=1, replica_groups={{0,2,4,6,8,10,12,14},{1,3,5,7,9,11,13,15},{16,18,20,22,24,26,28,30},{17..., dimensions={0} | all-to-all | bytes 1245184 | tf_op jit(solution)/shard_map/all_to_all | solution.py:470
  125.3 2.3 %collective-permute-start.2 = (bf16[8,152,256]{2,1,0:T(8,128)(2,1)S(1)}, bf16[8,152,256]{2,1,0:T(8,128)(2,1)S(1)}, u32[]{:S(2)}, u32[]{:S(2)}) collective-permute-start(bf16[8,152,256]{2,1,0:T(8,128)(2,1)S(1)} %all_to_all.27.got_ref.mine_ref), channel_id=1, source_target_pairs={{0,1},{1,0},{2,3},{3,2},{4,5},{5,4},{6,7},{7,6},{8,9},{9,8},{10,11... | collective-permute-start | bytes 1867784 | tf_op jit(solution)/shard_map/ppermute | solution.py:471
  127.6 1.1 widen.1.begun_ref
  128.7 0.6 collective-permute-done.2.other_ref
  129.3 1.1 spread.1
  (4 shorter events, 0.0 us)
Async XLA Ops:
  0.6 43.2 %copy-start = (bf16[1,2048,256]{2,1,0:T(8,128)(2,1)S(1)}, bf16[1,2048,256]{2,1,0:T(8,128)(2,1)}, u32[]{:S(2)}) copy-start(bf16[1,2048,256]{2,1,0:T(8,128)(2,1)} %weight_ref.5) | copy-start | bytes 3145732
  1.7 47.6 %copy-start.1 = (bf16[8192]{0:T(1024)(128)(2,1)S(1)}, bf16[8192]{0:T(1024)(128)(2,1)}, u32[]{:S(2)}) copy-start(bf16[8192]{0:T(1024)(128)(2,1)} %param.14) | copy-start | bytes 49156
  29.8 14.0 %collective-permute-start = (bf16[8,18,16,128]{3,2,1,0:T(8,128)(2,1)S(1)}, bf16[8,18,16,128]{3,2,1,0:T(8,128)(2,1)S(1)}, u32[]{:S(2)}, u32[]{:S(2)}) collective-permute-start(bf16[8,18,16,128]{3,2,1,0:T(8,128)(2,1)S(1)} %all_to_all.25.mine_ref), channel_id=1, source_target_pairs={{0,1},{1,0},{2,3},{3,2},{4,5},{5,4},{6,7},{7,6},{8,9},{9,8},{10,11... | collective-permute-start | bytes 1769480 | tf_op jit(solution)/shard_map/ppermute | solution.py:454
  34.2 18.6 %all-to-all-start.1 = ((bf16[32,4,256]{2,1,0:T(4,128)(2,1)}), bf16[32,4,256]{2,1,0:T(4,128)(2,1)S(1)}, u32[]{:S(2)}, u32[]{:S(2)}) async-start(bf16[32,4,256]{2,1,0:T(4,128)(2,1)} %bitcast.19), calls=%async_computation.1 | async-start | bytes 131072 | tf_op jit(solution)/shard_map/all_to_all | solution.py:459
  69.8 18.2 %all-to-all-start.3 = ((bf16[8,128,256]{2,1,0:T(8,128)(2,1)}), bf16[8,128,256]{2,1,0:T(8,128)(2,1)S(1)}, u32[]{:S(2)}, u32[]{:S(2)}) async-start(bf16[8,128,256]{2,1,0:T(8,128)(2,1)} %tower_back.1), calls=%async_computation.3 | async-start | bytes 1048576 | tf_op jit(solution)/shard_map/all_to_all | solution.py:468
  88.0 10.3 %collective-permute-start.1 = (bf16[8,128,256]{2,1,0:T(8,128)(2,1)S(1)}, bf16[8,128,256]{2,1,0:T(8,128)(2,1)S(1)}, u32[]{:S(2)}, u32[]{:S(2)}) collective-permute-start(bf16[8,128,256]{2,1,0:T(8,128)(2,1)S(1)} %all-to-all-done.3.grad_ref), channel_id=1, source_target_pairs={{0,1},{1,0},{2,3},{3,2},{4,5},{5,4},{6,7},{7,6},{8,9},{9,8},{10,11... | collective-permute-start | bytes 1572872 | tf_op jit(solution)/shard_map/ppermute | solution.py:469
  125.3 4.0 %collective-permute-start.2 = (bf16[8,152,256]{2,1,0:T(8,128)(2,1)S(1)}, bf16[8,152,256]{2,1,0:T(8,128)(2,1)S(1)}, u32[]{:S(2)}, u32[]{:S(2)}) collective-permute-start(bf16[8,152,256]{2,1,0:T(8,128)(2,1)S(1)} %all_to_all.27.got_ref.mine_ref), channel_id=1, source_target_pairs={{0,1},{1,0},{2,3},{3,2},{4,5},{5,4},{6,7},{7,6},{8,9},{9,8},{10,11... | collective-permute-start | bytes 1867784 | tf_op jit(solution)/shard_map/ppermute | solution.py:471

commit v6 on v5

--- a/solution.py
+++ b/solution.py
@@ -12,16 +12,11 @@
 NT = (((1,), (1,)), ((), ()))
 PARAMS = pltpu.CompilerParams(vmem_limit_bytes=20 * 1024 * 1024)
 vmem = pl.BlockSpec(memory_space=pltpu.VMEM)
-smem = pl.BlockSpec(memory_space=pltpu.SMEM)
 hbm = pl.BlockSpec(memory_space=pltpu.HBM)
 
 
 def in_hbm(*arrays):
     return tuple(pltpu.with_memory_space_constraint(a, pltpu.HBM) for a in arrays)
-
-
-def in_vmem(*arrays):
-    return tuple(pltpu.with_memory_space_constraint(a, pltpu.VMEM) for a in arrays)
 
 
 def mm(a, b):
@@ -72,7 +67,8 @@
     return mm_nt(member, high) + mm_nt(member, low)
 
 
-def pack_kernel(rows_ref, quot_ref, rem_ref, size_ref, out_ref, picks_ref, held):
+def pack_kernel(rows_ref, quot_ref, rem_ref, size_ref, table_ref, out_ref, picks_ref, copy_ref, held):
+    copy_ref[...] = table_ref[...]
     feats = rows_ref.shape[0]
     held[...] = jnp.zeros_like(held)
     for f in range(feats):
@@ -89,10 +85,10 @@
         out_ref[z, feats:] = picks[2 * z : 2 * z + 2]
 
 
-def pack(rows, quot, rem, sizes):
+def pack(rows, quot, rem, sizes, table):
     feats, zs = rows.shape[0], rows.shape[0] // 2
     whole = lambda a: pl.BlockSpec(a.shape, lambda i: (0, 0, 0))
-    pinned = in_hbm(rows, quot, rem, sizes)
+    pinned = in_hbm(rows, quot, rem, sizes, table)
     return pl.pallas_call(
         pack_kernel,
         grid=(1,),
@@ -100,10 +96,12 @@
         out_specs=[
             pl.BlockSpec((zs, feats + 2, 16, 128), lambda i: (0, 0, 0, 0)),
             pl.BlockSpec((feats, 16, 128), lambda i: (0, 0, 0)),
+            whole(table),
         ],
         out_shape=[
             jax.ShapeDtypeStruct((zs, feats + 2, 16, 128), bf16),
             jax.ShapeDtypeStruct((feats, 16, 128), bf16),
+            pltpu.VMEM(table.shape, bf16),
         ],
         scratch_shapes=[pltpu.VMEM((feats, 16, 128), f32)],
         compiler_params=PARAMS,
@@ -112,41 +110,30 @@
     )(*pinned)
 
 
-AHEAD = 2
-
-
-def tower_kernel(mine_ref, other_ref, rem_ref, picks_ref, weight_ref, pre_ref, held, sem):
-    fetch = pltpu.make_async_copy(rem_ref, held, sem)
-    fetch.start()
+def tower_kernel(mine_ref, other_ref, rem_ref, picks_ref, weight_ref, pre_ref):
     tri = triangles(128)
     _, side = place()
-    bags, ahead, feats = [], [], rem_ref.shape[0]
-    for f in range(feats + AHEAD):
-        if f < feats:
-            table = jnp.concatenate(
-                [mine_ref[:, f].reshape(128, 128), other_ref[:, f].reshape(128, 128)], axis=0
-            )
-            quot_hot, rem_hot, member = masks(picks_ref[f], side, tri)
-            ahead.append((mm(table.T, quot_hot), rem_hot, member))
-        if f == AHEAD:
-            fetch.wait()
-        if f >= AHEAD:
-            quot, rem_hot, member = ahead[f - AHEAD]
-            bags.append(pool(quot, mm(held[f - AHEAD].T, rem_hot), member).astype(bf16))
+    bags = []
+    for f in range(rem_ref.shape[0]):
+        table = jnp.concatenate(
+            [mine_ref[:, f].reshape(128, 128), other_ref[:, f].reshape(128, 128)], axis=0
+        )
+        quot_hot, rem_hot, member = masks(picks_ref[f], side, tri)
+        bag = pool(mm(table.T, quot_hot), mm(rem_ref[f].T, rem_hot), member)
+        bags.append(bag.astype(bf16))
     pre_ref[...] = mm(jnp.concatenate(bags, axis=1), weight_ref[0])
 
 
 def tower_forward(mine, other, remainder, picks, weight):
     return pl.pallas_call(
         tower_kernel,
-        in_specs=[vmem] * 2 + [hbm] + [vmem] * 2,
+        in_specs=[vmem] * 5,
         out_specs=vmem,
         out_shape=jax.ShapeDtypeStruct((128, 256), f32),
-        scratch_shapes=[pltpu.VMEM(remainder.shape, bf16), pltpu.SemaphoreType.DMA],
         compiler_params=PARAMS,
         cost_estimate=cost(6),
         name="tower_forward",
-    )(mine, other, *in_hbm(remainder), picks, weight)
+    )(mine, other, remainder, picks, weight)
 
 
 def place():
@@ -449,11 +436,13 @@
     side = (shard & 1).astype(jnp.int32)
     side_arg = side[None]
     where = jnp.stack([shard, side]).astype(jnp.int32)
-    packed, picks = pack(quotient_rows, quotient_index, remainder_index, bag_sizes)
+    packed, picks, tables = pack(
+        quotient_rows, quotient_index, remainder_index, bag_sizes, remainder_rows
+    )
     mine, late = lax.optimization_barrier((gather_z(packed), cotangent[0]))
     other = lax.ppermute(mine, "shard", across)
     late = late.reshape(4, towers, 256).transpose(1, 0, 2)
-    pre = tower_forward(mine, other, remainder_rows, picks, tower_weight)
+    pre = tower_forward(mine, other, tables, picks, tower_weight)
     pre, norm_gain = lax.optimization_barrier((pre, norm_gain))
     gain = norm_gain.astype(f32)[None]
     pre, gain, cot = lax.optimization_barrier((pre, gain, swap(late, "tower")))

time: 131 us -> 130 us (level)
  transfers between devices with their start and end apart: 5 -> 5, of which waited for: 3 -> 3; matrix products, arithmetic and copies ran while one was open for 0% -> 0% of each run, Pallas kernels for 17% -> 16%
where the time goes in v6:
time: 130 us
  blocking collectives  65.4 us (50%)
  Pallas kernels  29.5 us (23%)
  starting transfers between devices  25.4 us (20%)
  waiting for transfers between devices  8.71 us (7%)
    all_to_all x1, blocking collectives, on_device(): mine, late = lax.optimization_barrier((gather_z(packed), cotangent[0]))  28.1 us
    all_to_all x1, blocking collectives, on_device(): gather_z(grads_part(grad_mine, grad_other, tower_weight, *looked))  22.5 us
    all_to_all x1, blocking collectives, on_device(): stats = swap(sent, 'tower')  14.8 us
    pallas_call x1, Pallas kernels, feature_pool(): pl.pallas_call(functools.partial(feature_kernel, per_step), grid_spec=plt...  9.68 us
    all_to_all x1, starting transfers between devices, on_device(): pre, gain, cot = lax.optimization_barrier((pre, gain, swap(late, 'tower')))  9.68 us
    pallas_call x2, Pallas kernels, grads_call(): pl.pallas_call(kernel, in_specs=[vmem] * 2 + [hbm] * 6 + [vmem] * len(beg...  9.21 us
    ppermute x1, starting transfers between devices, on_device(): grad_other = lax.ppermute(grad_mine, 'shard', across)  5.59 us
    pallas_call x1, Pallas kernels, tower_forward(): pl.pallas_call(tower_kernel, in_specs=[vmem] * 5, out_specs=vmem, out_sha...  4.68 us
  transfers between devices with their start and end apart: 5, of which 3 were waited for; matrix products, arithmetic and copies ran while one was open for 0% of the time, Pallas kernels for 16%

profile of v6, /device:TPU:1, one launch (start us, length us, event | category | flops | bytes accessed | tf_op | source)
XLA Modules:
  0.0 129.8 jit_solution(17792629446456220792)
XLA Ops:
  0.6 0.0 copy-start
  0.6 1.4 %pack.1 = (bf16[8,18,16,128]{3,2,1,0:T(8,128)(2,1)S(1)}, bf16[16,16,128]{2,1,0:T(8,128)(2,1)S(1)}, bf16[16,128,128]{2,1,0:T(8,128)(2,1)S(1)}) custom-call(bf16[16,16,128]{2,1,0:T(8,128)(2,1)} %rows_ref.1, s32[16,1,512]{2,1,0:T(1,128)} %quot_ref.1, s32[16,1,512]{2,1,0:T(1,128)} %rem_ref.2, s32[16,1,128]{2,1,0:T(1,128)} %size_ref.1, bf16[16,128,128]{2,1,0:T(8,128)(2,1)} %rem_ref.3), custom_call_target="tpu_custom_call" | custom-call | flops 100000000 | bytes 3000000 | tf_op jit(solution)/shard_map/pack/pallas_call | solution.py:92
  2.0 0.0 copy-start.1
  2.0 28.1 %all_to_all.25.mine_ref = bf16[8,18,16,128]{3,2,1,0:T(8,128)(2,1)S(1)} all-to-all(bf16[8,18,16,128]{3,2,1,0:T(8,128)(2,1)S(1)} %get-tuple-element.36), channel_id=1, replica_groups={{0,2,4,6,8,10,12,14},{1,3,5,7,9,11,13,15},{16,18,20,22,24,26,28,30},{17..., dimensions={0} | all-to-all | bytes 1179648 | tf_op jit(solution)/shard_map/all_to_all | solution.py:442
  30.1 4.3 %collective-permute-start = (bf16[8,18,16,128]{3,2,1,0:T(8,128)(2,1)S(1)}, bf16[8,18,16,128]{3,2,1,0:T(8,128)(2,1)S(1)}, u32[]{:S(2)}, u32[]{:S(2)}) collective-permute-start(bf16[8,18,16,128]{3,2,1,0:T(8,128)(2,1)S(1)} %all_to_all.25.mine_ref), channel_id=1, source_target_pairs={{0,1},{1,0},{2,3},{3,2},{4,5},{5,4},{6,7},{7,6},{8,9},{9,8},{10,11... | collective-permute-start | bytes 1769480 | tf_op jit(solution)/shard_map/ppermute | solution.py:443
  34.5 9.7 %all-to-all-start.1 = ((bf16[32,4,256]{2,1,0:T(4,128)(2,1)}), bf16[32,4,256]{2,1,0:T(4,128)(2,1)S(1)}, u32[]{:S(2)}, u32[]{:S(2)}) async-start(bf16[32,4,256]{2,1,0:T(4,128)(2,1)} %bitcast.19), calls=%async_computation.1 | async-start | bytes 131072 | tf_op jit(solution)/shard_map/all_to_all | solution.py:448
  44.1 0.0 collective-permute-done.other_ref
  44.2 0.0 copy-done
  44.2 4.7 %tower_forward.1.pre_ref = f32[128,256]{1,0:T(8,128)S(1)} custom-call(bf16[8,18,16,128]{3,2,1,0:T(8,128)(2,1)S(1)} %all_to_all.25.mine_ref, bf16[8,18,16,128]{3,2,1,0:T(8,128)(2,1)S(1)} %collective-permute-done.other_ref, bf16[16,128,128]{2,1,0:T(8,128)(2,1)S(1)} %get-tuple-element.38.rem_ref, bf16[16,16,128]{2,1,0:T(8,128)(2,1)S(1)} %get-tuple-element.39.picks_ref, ...), custom_call_target="tpu_custom_call" | custom-call | flops 600000000 | bytes 18000000 | tf_op jit(solution)/shard_map/tower_forward/pallas_call | solution.py:128
  48.8 0.0 copy-done.1
  48.9 4.2 %all-to-all-done.1.cot_ref = bf16[32,4,256]{2,1,0:T(4,128)(2,1)S(1)} async-done(((bf16[32,4,256]{2,1,0:T(4,128)(2,1)}), bf16[32,4,256]{2,1,0:T(4,128)(2,1)S(1)}, u32[]{:S(2)}, u32[]{:S(2)}) %all-to-all-start.1) | async-done | bytes 65568 | tf_op jit(solution)/shard_map/all_to_all | solution.py:448
  53.1 0.3 local_stats.1
  53.4 14.8 %all_to_all.26.got_ref = f32[32,3,4,128]{3,2,1,0:T(4,128)S(1)} all-to-all(f32[32,3,4,128]{3,2,1,0:T(4,128)S(1)} %get-tuple-element.46), channel_id=1, replica_groups=mesh['tower'=32,'shard'=16] {'tower'}, dimensions={0} | all-to-all | bytes 393216 | tf_op jit(solution)/shard_map/all_to_all | solution.py:450
  68.1 1.2 tower_back.1
  69.3 3.5 %all-to-all-start.3 = ((bf16[8,128,256]{2,1,0:T(8,128)(2,1)}), bf16[8,128,256]{2,1,0:T(8,128)(2,1)S(1)}, u32[]{:S(2)}, u32[]{:S(2)}) async-start(bf16[8,128,256]{2,1,0:T(8,128)(2,1)} %tower_back.1), calls=%async_computation.3 | async-start | bytes 1048576 | tf_op jit(solution)/shard_map/all_to_all | solution.py:457
  72.8 0.1 pad_add_fusion.where_ref
  72.9 9.7 %feature_pool.1 = (bf16[2,8,128,128]{3,2,1,0:T(8,128)(2,1)}, bf16[2,8,128,512]{3,2,1,0:T(8,128)(2,1)}, bf16[2,8,128,512]{3,2,1,0:T(8,128)(2,1)}, bf16[2,8,256,51...) custom-call(s32[2]{0:T(128)S(1)} %pad_add_fusion.where_ref, ...), custom_call_target="tpu_custom_call" | custom-call | flops 600000000 | bytes 18000000 | tf_op jit(solution)/shard_map/feature_pool/pallas_call | solution.py:234
  82.6 1.0 norm.1
  83.5 3.9 %all-to-all-done.3.grad_ref = bf16[8,128,256]{2,1,0:T(8,128)(2,1)S(1)} async-done(((bf16[8,128,256]{2,1,0:T(8,128)(2,1)}), bf16[8,128,256]{2,1,0:T(8,128)(2,1)S(1)}, u32[]{:S(2)}, u32[]{:S(2)}) %all-to-all-start.3) | async-done | bytes 524320 | tf_op jit(solution)/shard_map/all_to_all | solution.py:457
  87.5 5.6 %collective-permute-start.1 = (bf16[8,128,256]{2,1,0:T(8,128)(2,1)S(1)}, bf16[8,128,256]{2,1,0:T(8,128)(2,1)S(1)}, u32[]{:S(2)}, u32[]{:S(2)}) collective-permute-start(bf16[8,128,256]{2,1,0:T(8,128)(2,1)S(1)} %all-to-all-done.3.grad_ref), channel_id=1, source_target_pairs={{0,1},{1,0},{2,3},{3,2},{4,5},{5,4},{6,7},{7,6},{8,9},{9,8},{10,11... | collective-permute-start | bytes 1572872 | tf_op jit(solution)/shard_map/ppermute | solution.py:458
  93.0 4.7 %grads_first.1 = (f32[128,256]{1,0:T(8,128)S(1)}, f32[128,256]{1,0:T(8,128)S(1)}, f32[128,128]{1,0:T(8,128)S(1)}) custom-call(bf16[8,128,256]{2,1,0:T(8,128)(2,1)S(1)} %all-to-all-done.3.grad_ref, bf16[1,2048,256]{2,1,0:T(8,128)(2,1)S(1)} %copy-done, bf16[2,8,128,128]{3,2,1,0:T(8,128)(2,1)} %get-tuple-element.56.refs_0_, ...), custom_call_target="tpu_custom_call" | custom-call | flops 400000000 | bytes 12000000 | tf_op jit(solution)/shard_map/grads_first/pallas_call | solution.py:345
  97.7 0.0 collective-permute-done.1.grad_ref
  97.7 4.6 %grads_second.1 = bf16[8,152,256]{2,1,0:T(8,128)(2,1)S(1)} custom-call(bf16[8,128,256]{2,1,0:T(8,128)(2,1)S(1)} %collective-permute-done.1.grad_ref, bf16[1,2048,256]{2,1,0:T(8,128)(2,1)S(1)} %copy-done, bf16[2,8,128,128]{3,2,1,0:T(8,128)(2,1)} %get-tuple-element.56.refs_0_, bf16[2,8,128,512]{3,2,1,0:T(8,128)(2,1)} %get-tuple-element.57.refs_1_, ...), custom_call_target="tpu_custom_call" | custom-call | flops 400000000 | bytes 12000000 | tf_op jit(solution)/shard_map/grads_second/pallas_call | solution.py:345
  102.3 22.5 %all_to_all.27.got_ref.mine_ref = bf16[8,152,256]{2,1,0:T(8,128)(2,1)S(1)} all-to-all(bf16[8,152,256]{2,1,0:T(8,128)(2,1)S(1)} %grads_second.1), channel_id=1, replica_groups={{0,2,4,6,8,10,12,14},{1,3,5,7,9,11,13,15},{16,18,20,22,24,26,28,30},{17..., dimensions={0} | all-to-all | bytes 1245184 | tf_op jit(solution)/shard_map/all_to_all | solution.py:459
  124.8 2.3 %collective-permute-start.2 = (bf16[8,152,256]{2,1,0:T(8,128)(2,1)S(1)}, bf16[8,152,256]{2,1,0:T(8,128)(2,1)S(1)}, u32[]{:S(2)}, u32[]{:S(2)}) collective-permute-start(bf16[8,152,256]{2,1,0:T(8,128)(2,1)S(1)} %all_to_all.27.got_ref.mine_ref), channel_id=1, source_target_pairs={{0,1},{1,0},{2,3},{3,2},{4,5},{5,4},{6,7},{7,6},{8,9},{9,8},{10,11... | collective-permute-start | bytes 1867784 | tf_op jit(solution)/shard_map/ppermute | solution.py:460
  127.1 1.1 widen.1.begun_ref
  128.2 0.6 collective-permute-done.2.other_ref
  128.8 1.1 spread.1
  (4 shorter events, 0.0 us)
Async XLA Ops:
  0.6 43.5 %copy-start = (bf16[1,2048,256]{2,1,0:T(8,128)(2,1)S(1)}, bf16[1,2048,256]{2,1,0:T(8,128)(2,1)}, u32[]{:S(2)}) copy-start(bf16[1,2048,256]{2,1,0:T(8,128)(2,1)} %weight_ref.5) | copy-start | bytes 3145732
  2.0 46.8 %copy-start.1 = (bf16[8192]{0:T(1024)(128)(2,1)S(1)}, bf16[8192]{0:T(1024)(128)(2,1)}, u32[]{:S(2)}) copy-start(bf16[8192]{0:T(1024)(128)(2,1)} %param.14) | copy-start | bytes 49156
  30.1 14.0 %collective-permute-start = (bf16[8,18,16,128]{3,2,1,0:T(8,128)(2,1)S(1)}, bf16[8,18,16,128]{3,2,1,0:T(8,128)(2,1)S(1)}, u32[]{:S(2)}, u32[]{:S(2)}) collective-permute-start(bf16[8,18,16,128]{3,2,1,0:T(8,128)(2,1)S(1)} %all_to_all.25.mine_ref), channel_id=1, source_target_pairs={{0,1},{1,0},{2,3},{3,2},{4,5},{5,4},{6,7},{7,6},{8,9},{9,8},{10,11... | collective-permute-start | bytes 1769480 | tf_op jit(solution)/shard_map/ppermute | solution.py:443
  34.5 18.6 %all-to-all-start.1 = ((bf16[32,4,256]{2,1,0:T(4,128)(2,1)}), bf16[32,4,256]{2,1,0:T(4,128)(2,1)S(1)}, u32[]{:S(2)}, u32[]{:S(2)}) async-start(bf16[32,4,256]{2,1,0:T(4,128)(2,1)} %bitcast.19), calls=%async_computation.1 | async-start | bytes 131072 | tf_op jit(solution)/shard_map/all_to_all | solution.py:448
  69.3 18.2 %all-to-all-start.3 = ((bf16[8,128,256]{2,1,0:T(8,128)(2,1)}), bf16[8,128,256]{2,1,0:T(8,128)(2,1)S(1)}, u32[]{:S(2)}, u32[]{:S(2)}) async-start(bf16[8,128,256]{2,1,0:T(8,128)(2,1)} %tower_back.1), calls=%async_computation.3 | async-start | bytes 1048576 | tf_op jit(solution)/shard_map/all_to_all | solution.py:457
  87.5 10.3 %collective-permute-start.1 = (bf16[8,128,256]{2,1,0:T(8,128)(2,1)S(1)}, bf16[8,128,256]{2,1,0:T(8,128)(2,1)S(1)}, u32[]{:S(2)}, u32[]{:S(2)}) collective-permute-start(bf16[8,128,256]{2,1,0:T(8,128)(2,1)S(1)} %all-to-all-done.3.grad_ref), channel_id=1, source_target_pairs={{0,1},{1,0},{2,3},{3,2},{4,5},{5,4},{6,7},{7,6},{8,9},{9,8},{10,11... | collective-permute-start | bytes 1572872 | tf_op jit(solution)/shard_map/ppermute | solution.py:458
  124.8 4.0 %collective-permute-start.2 = (bf16[8,152,256]{2,1,0:T(8,128)(2,1)S(1)}, bf16[8,152,256]{2,1,0:T(8,128)(2,1)S(1)}, u32[]{:S(2)}, u32[]{:S(2)}) collective-permute-start(bf16[8,152,256]{2,1,0:T(8,128)(2,1)S(1)} %all_to_all.27.got_ref.mine_ref), channel_id=1, source_target_pairs={{0,1},{1,0},{2,3},{3,2},{4,5},{5,4},{6,7},{7,6},{8,9},{9,8},{10,11... | collective-permute-start | bytes 1867784 | tf_op jit(solution)/shard_map/ppermute | solution.py:460

commit v7 on v6

--- a/solution.py
+++ b/solution.py
@@ -41,23 +41,29 @@
     return jnp.concatenate([upto, before], axis=0)
 
 
-def masks(picks, side, tri):
+def one_hots(picks, side):
     values = picks.astype(jnp.int32)
     row_q = lax.broadcasted_iota(jnp.int32, (256, 128), 0)
     row_r = lax.broadcasted_iota(jnp.int32, (128, 128), 0)
+    spot = ((((values >> 4) & 1) ^ side) << 7) + ((values >> 5) << 4) + (values & 15)
+    quot, rem = [], []
+    for c in range(4):
+        quot.append(jnp.where(row_q == spot[c : c + 1], 1.0, 0.0).astype(bf16))
+        rem.append(jnp.where(row_r == values[4 + c : 5 + c], 1.0, 0.0).astype(bf16))
+    return jnp.concatenate(quot, axis=1), jnp.concatenate(rem, axis=1)
+
+
+def masks(picks, side, tri):
     lane = lax.broadcasted_iota(jnp.int32, (128, 128), 1).astype(f32)
-    place = ((((values >> 4) & 1) ^ side) << 7) + ((values >> 5) << 4) + (values & 15)
     sums = mm_nt(tri, picks)
     ends = jnp.broadcast_to(sums[:128, 8:9], (128, 128))
     starts = jnp.broadcast_to(sums[128:, 8:9], (128, 128))
-    quot, rem, member = [], [], []
+    member = []
     for c in range(4):
-        quot.append(jnp.where(row_q == place[c : c + 1], 1.0, 0.0).astype(bf16))
-        rem.append(jnp.where(row_r == values[4 + c : 5 + c], 1.0, 0.0).astype(bf16))
         here = lane + float(128 * c)
         inside = (here < ends) & (here >= starts)
         member.append(jnp.where(inside, 1.0, 0.0).astype(bf16))
-    return tuple(jnp.concatenate(v, axis=1) for v in (quot, rem, member))
+    return *one_hots(picks, side), jnp.concatenate(member, axis=1)
 
 
 def pool(quot, rem, member):
@@ -206,7 +212,7 @@
 
 
 def feature_kernel(per_step, where_ref, mine_ref, other_ref, rem_ref, picks_ref, *refs):
-    bag_ref, quot_ref, remd_ref, qhot_ref, rhot_ref, member_ref, qt_ref, rt_ref = refs
+    bag_ref, quot_ref, remd_ref, member_ref, qt_ref, rt_ref = refs
 
     @pl.when((pl.program_id(0) == 0) & (pl.program_id(1) == 0))
     def _():
@@ -220,7 +226,7 @@
         quot, rem = mm(qt_ref[...], hot[0]), mm(rt_ref[...], hot[1])
         bag_ref[0, i] = pool(quot, rem, hot[2]).T.astype(bf16)
         quot_ref[0, i], remd_ref[0, i] = quot.astype(bf16), rem.astype(bf16)
-        qhot_ref[0, i], rhot_ref[0, i], member_ref[0, i] = hot
+        member_ref[0, i] = hot[2]
 
 
 def step_block(per_step, *dims):
@@ -230,7 +236,7 @@
 def feature_pool(where, mine, other, remainder, picks):
     zs, per_step = picks.shape[1], 4
     table = pl.BlockSpec((zs, 1, 16, 128), lambda h, i, w: (0, w[0], 0, 0))
-    sizes = [(128, 128), (128, 512), (128, 512), (256, 512), (128, 512), (128, 512)]
+    sizes = [(128, 128), (128, 512), (128, 512), (128, 512)]
     return pl.pallas_call(
         functools.partial(feature_kernel, per_step),
         grid_spec=pltpu.PrefetchScalarGridSpec(
@@ -286,8 +292,9 @@
 CUTS = ((0, 2), (2, 4), (4, 8))
 
 
-def half_sums(half, grad_ref, weight_ref, kept, held, sems, sums):
-    own, _ = place()
+def half_sums(half, grad_ref, got_ref, weight_ref, kept, held, sems, sums):
+    own, side = place()
+    feats = 2 * got_ref.shape[0]
     loads = []
     for c, (low, high) in enumerate(CUTS):
         part = pl.ds(low, high - low)
@@ -300,7 +307,7 @@
     for copies in loads:
         for copy in copies:
             copy.start()
-    bags, quots, rems, quot_hot, rem_hot, member = held
+    bags, quots, rems, member = held
     weight = weight_ref[0, pl.ds(pl.multiple_of(own * 128, 128), 128), :]
     weight_sum, quot_sum, rem_sum = sums
     for copies, (low, high) in zip(loads, CUTS):
@@ -312,24 +319,26 @@
             look = mm(mm_nt(weight, grad).astype(bf16), member[z])
             quot_part = (look * rems[z].astype(f32)).astype(bf16)
             rem_part = (look * quots[z].astype(f32)).astype(bf16)
-            quot_sum += mm_nt(quot_part, quot_hot[z])
-            rem_sum += mm_nt(rem_part, rem_hot[z])
+            quot_hot, rem_hot = one_hots(got_ref[z, feats + side], side)
+            quot_sum += mm_nt(quot_part, quot_hot)
+            rem_sum += mm_nt(rem_part, rem_hot)
     return weight_sum, quot_sum, rem_sum
 
 
 SUMS = ((128, 256), (128, 256), (128, 128))
 
 
-def first_kernel(grad_ref, weight_ref, *refs):
-    kept, outs, held, sems = refs[:6], refs[6:9], refs[9:15], refs[15]
+def first_kernel(grad_ref, got_ref, weight_ref, *refs):
+    kept, outs, held, sems = refs[:4], refs[4:7], refs[7:11], refs[11]
     sums = tuple(jnp.zeros(s, f32) for s in SUMS)
-    for ref, value in zip(outs, half_sums(0, grad_ref, weight_ref, kept, held, sems, sums)):
+    for ref, value in zip(outs, half_sums(0, grad_ref, got_ref, weight_ref, kept, held, sems, sums)):
         ref[...] = value
 
 
-def second_kernel(grad_ref, weight_ref, *refs):
-    kept, begun, out_ref, held, sems = refs[:6], refs[6:9], refs[9], refs[10:16], refs[16]
-    sums = half_sums(1, grad_ref, weight_ref, kept, held, sems, tuple(ref[...] for ref in begun))
+def second_kernel(grad_ref, got_ref, weight_ref, *refs):
+    kept, begun, out_ref, held, sems = refs[:4], refs[4:7], refs[7], refs[8:12], refs[12]
+    sums = tuple(ref[...] for ref in begun)
+    sums = half_sums(1, grad_ref, got_ref, weight_ref, kept, held, sems, sums)
     _, side = place()
     chunk, quot, rem = sums[0].astype(bf16), sums[1].T, sums[2].T
     for z in range(out_ref.shape[0]):
@@ -341,25 +350,25 @@
         out_ref[z, 128:] = rows.astype(bf16)
 
 
-def grads_call(kernel, name, out_shape, grad, weight, looked, *begun):
+def grads_call(kernel, name, out_shape, grad, got, weight, looked, *begun):
     return pl.pallas_call(
         kernel,
-        in_specs=[vmem] * 2 + [hbm] * 6 + [vmem] * len(begun),
+        in_specs=[vmem] * 3 + [hbm] * 4 + [vmem] * len(begun),
         out_specs=jax.tree.map(lambda _: vmem, out_shape),
         out_shape=out_shape,
         scratch_shapes=[pltpu.VMEM(a.shape[1:], bf16) for a in looked]
-        + [pltpu.SemaphoreType.DMA((len(CUTS), 6))],
+        + [pltpu.SemaphoreType.DMA((len(CUTS), 4))],
         compiler_params=PARAMS,
         cost_estimate=cost(4),
         name=name,
-    )(grad, weight, *in_hbm(*looked), *begun)
-
-
-def grads_part(mine, other, weight, *looked):
+    )(grad, got, weight, *in_hbm(*looked), *begun)
+
+
+def grads_part(mine, other, got_mine, got_other, weight, *looked):
     begun = [jax.ShapeDtypeStruct(s, f32) for s in SUMS]
-    begun = grads_call(first_kernel, "grads_first", begun, mine, weight, looked)
+    begun = grads_call(first_kernel, "grads_first", begun, mine, got_mine, weight, looked)
     sent = jax.ShapeDtypeStruct((mine.shape[0], 152, 256), bf16)
-    return grads_call(second_kernel, "grads_second", sent, other, weight, looked, *begun)
+    return grads_call(second_kernel, "grads_second", sent, other, got_other, weight, looked, *begun)
 
 
 def widen_kernel(side_ref, got_ref, out_ref):
@@ -456,7 +465,7 @@
     looked = feature_pool(where, mine, other, remainder_rows, all_picks)
     grad_mine, joint, *looked = lax.optimization_barrier((gather_z(grad_copies), joint, *looked))
     grad_other = lax.ppermute(grad_mine, "shard", across)
-    got_mine = gather_z(grads_part(grad_mine, grad_other, tower_weight, *looked))
+    got_mine = gather_z(grads_part(grad_mine, grad_other, mine, other, tower_weight, *looked))
     got_other = lax.ppermute(got_mine, "shard", across)
     begun = widen(side_arg, got_mine)
     weight_grad, quot_grad, rem_grad = spread(side_arg, begun, got_mine, got_other)

time: 130 us -> 130 us (level)
  Pallas kernels: 29.5 us -> 27.9 us
  transfers between devices with their start and end apart: 5 -> 5, of which waited for: 3 -> 3; matrix products, arithmetic and copies ran while one was open for 0% -> 0% of each run, Pallas kernels for 16% -> 15%
where the time goes in v7:
time: 130 us; the launch traced here: 129 us
  blocking collectives  65.4 us (50%)
  Pallas kernels  27.9 us (21%)
  starting transfers between devices  25.4 us (20%)
  waiting for transfers between devices  9.67 us (7%)
    all_to_all x1, blocking collectives, on_device(): mine, late = lax.optimization_barrier((gather_z(packed), cotangent[0]))  28.1 us
    all_to_all x1, blocking collectives, on_device(): gather_z(grads_part(grad_mine, grad_other, mine, other, tower_weight, *lo...  22.5 us
    all_to_all x1, blocking collectives, on_device(): stats = swap(sent, 'tower')  14.8 us
    all_to_all x1, starting transfers between devices, on_device(): pre, gain, cot = lax.optimization_barrier((pre, gain, swap(late, 'tower')))  9.68 us
    pallas_call x1, Pallas kernels, feature_pool(): pl.pallas_call(functools.partial(feature_kernel, per_step), grid_spec=plt...  8.72 us
    pallas_call x2, Pallas kernels, grads_call(): pl.pallas_call(kernel, in_specs=[vmem] * 3 + [hbm] * 4 + [vmem] * len(beg...  8.64 us
    ppermute x1, starting transfers between devices, on_device(): grad_other = lax.ppermute(grad_mine, 'shard', across)  5.59 us
    all_to_all x1, waiting for transfers between devices, on_device(): gather_z(grad_copies)  4.87 us
  transfers between devices with their start and end apart: 5, of which 3 were waited for; matrix products, arithmetic and copies ran while one was open for 0% of the time, Pallas kernels for 15%

profile of v7, /device:TPU:1, one launch (start us, length us, event | category | flops | bytes accessed | tf_op | source)
XLA Modules:
  0.0 129.3 jit_solution(9800247756344398099)
XLA Ops:
  0.6 0.0 copy-start
  0.6 1.4 %pack.1 = (bf16[8,18,16,128]{3,2,1,0:T(8,128)(2,1)S(1)}, bf16[16,16,128]{2,1,0:T(8,128)(2,1)S(1)}, bf16[16,128,128]{2,1,0:T(8,128)(2,1)S(1)}) custom-call(bf16[16,16,128]{2,1,0:T(8,128)(2,1)} %rows_ref.1, s32[16,1,512]{2,1,0:T(1,128)} %quot_ref.1, s32[16,1,512]{2,1,0:T(1,128)} %rem_ref.2, s32[16,1,128]{2,1,0:T(1,128)} %size_ref.1, bf16[16,128,128]{2,1,0:T(8,128)(2,1)} %rem_ref.3), custom_call_target="tpu_custom_call" | custom-call | flops 100000000 | bytes 3000000 | tf_op jit(solution)/shard_map/pack/pallas_call | solution.py:98
  2.0 0.0 copy-start.1
  2.0 28.1 %all_to_all.25.mine_ref.got_ref = bf16[8,18,16,128]{3,2,1,0:T(8,128)(2,1)S(1)} all-to-all(bf16[8,18,16,128]{3,2,1,0:T(8,128)(2,1)S(1)} %get-tuple-element.32), channel_id=1, replica_groups={{0,2,4,6,8,10,12,14},{1,3,5,7,9,11,13,15},{16,18,20,22,24,26,28,30},{17..., dimensions={0} | all-to-all | bytes 1179648 | tf_op jit(solution)/shard_map/all_to_all | solution.py:451
  30.1 4.3 %collective-permute-start = (bf16[8,18,16,128]{3,2,1,0:T(8,128)(2,1)S(1)}, bf16[8,18,16,128]{3,2,1,0:T(8,128)(2,1)S(1)}, u32[]{:S(2)}, u32[]{:S(2)}) collective-permute-start(bf16[8,18,16,128]{3,2,1,0:T(8,128)(2,1)S(1)} %all_to_all.25.mine_ref.got_ref), channel_id=1, source_target_pairs={{0,1},{1,0},{2,3},{3,2},{4,5},{5,4},{6,7},{7,6},{8,9},{9,8},{10,11... | collective-permute-start | bytes 1769480 | tf_op jit(solution)/shard_map/ppermute | solution.py:452
  34.5 9.7 %all-to-all-start.1 = ((bf16[32,4,256]{2,1,0:T(4,128)(2,1)}), bf16[32,4,256]{2,1,0:T(4,128)(2,1)S(1)}, u32[]{:S(2)}, u32[]{:S(2)}) async-start(bf16[32,4,256]{2,1,0:T(4,128)(2,1)} %bitcast.19), calls=%async_computation.1 | async-start | bytes 131072 | tf_op jit(solution)/shard_map/all_to_all | solution.py:457
  44.1 0.0 collective-permute-done.other_ref.got_ref
  44.2 0.0 copy-done
  44.2 4.7 %tower_forward.1.pre_ref = f32[128,256]{1,0:T(8,128)S(1)} custom-call(bf16[8,18,16,128]{3,2,1,0:T(8,128)(2,1)S(1)} %all_to_all.25.mine_ref.got_ref, bf16[8,18,16,128]{3,2,1,0:T(8,128)(2,1)S(1)} %collective-permute-done.other_ref.got_ref, bf16[16,128,128]{2,1,0:T(8,128)(2,1)S(1)} %get-tuple-element.34.rem_ref, ...), custom_call_target="tpu_custom_call" | custom-call | flops 600000000 | bytes 18000000 | tf_op jit(solution)/shard_map/tower_forward/pallas_call | solution.py:134
  48.8 0.0 copy-done.1
  48.9 4.2 %all-to-all-done.1.cot_ref = bf16[32,4,256]{2,1,0:T(4,128)(2,1)S(1)} async-done(((bf16[32,4,256]{2,1,0:T(4,128)(2,1)}), bf16[32,4,256]{2,1,0:T(4,128)(2,1)S(1)}, u32[]{:S(2)}, u32[]{:S(2)}) %all-to-all-start.1) | async-done | bytes 65568 | tf_op jit(solution)/shard_map/all_to_all | solution.py:457
  53.1 0.3 local_stats.1
  53.4 14.8 %all_to_all.26.got_ref = f32[32,3,4,128]{3,2,1,0:T(4,128)S(1)} all-to-all(f32[32,3,4,128]{3,2,1,0:T(4,128)S(1)} %get-tuple-element.42), channel_id=1, replica_groups=mesh['tower'=32,'shard'=16] {'tower'}, dimensions={0} | all-to-all | bytes 393216 | tf_op jit(solution)/shard_map/all_to_all | solution.py:459
  68.1 1.1 tower_back.1
  69.3 3.5 %all-to-all-start.3 = ((bf16[8,128,256]{2,1,0:T(8,128)(2,1)}), bf16[8,128,256]{2,1,0:T(8,128)(2,1)S(1)}, u32[]{:S(2)}, u32[]{:S(2)}) async-start(bf16[8,128,256]{2,1,0:T(8,128)(2,1)} %tower_back.1), calls=%async_computation.3 | async-start | bytes 1048576 | tf_op jit(solution)/shard_map/all_to_all | solution.py:466
  72.8 0.1 pad_add_fusion.where_ref
  72.9 8.7 %feature_pool.1 = (bf16[2,8,128,128]{3,2,1,0:T(8,128)(2,1)}, bf16[2,8,128,512]{3,2,1,0:T(8,128)(2,1)}, bf16[2,8,128,512]{3,2,1,0:T(8,128)(2,1)}, bf16[2,8,128,512]{3,2,1,0:T(8,128)(2,1)}) custom-call(s32[2]{0:T(128)S(1)} %pad_add_fusion.where_ref, bf16[8,18,16,128]{3,2,1,0:T(8,128)(2,1)S(1)} %all_to_all.25.mine_ref.got_ref, ...), custom_call_target="tpu_custom_call" | custom-call | flops 600000000 | bytes 18000000 | tf_op jit(solution)/shard_map/feature_pool/pallas_call | solution.py:240
  81.6 1.0 norm.1
  82.6 4.9 %all-to-all-done.3.grad_ref = bf16[8,128,256]{2,1,0:T(8,128)(2,1)S(1)} async-done(((bf16[8,128,256]{2,1,0:T(8,128)(2,1)}), bf16[8,128,256]{2,1,0:T(8,128)(2,1)S(1)}, u32[]{:S(2)}, u32[]{:S(2)}) %all-to-all-start.3) | async-done | bytes 524320 | tf_op jit(solution)/shard_map/all_to_all | solution.py:466
  87.4 5.6 %collective-permute-start.1 = (bf16[8,128,256]{2,1,0:T(8,128)(2,1)S(1)}, bf16[8,128,256]{2,1,0:T(8,128)(2,1)S(1)}, u32[]{:S(2)}, u32[]{:S(2)}) collective-permute-start(bf16[8,128,256]{2,1,0:T(8,128)(2,1)S(1)} %all-to-all-done.3.grad_ref), channel_id=1, source_target_pairs={{0,1},{1,0},{2,3},{3,2},{4,5},{5,4},{6,7},{7,6},{8,9},{9,8},{10,11... | collective-permute-start | bytes 1572872 | tf_op jit(solution)/shard_map/ppermute | solution.py:467
  93.0 4.4 %grads_first.1 = (f32[128,256]{1,0:T(8,128)S(1)}, f32[128,256]{1,0:T(8,128)S(1)}, f32[128,128]{1,0:T(8,128)S(1)}) custom-call(bf16[8,128,256]{2,1,0:T(8,128)(2,1)S(1)} %all-to-all-done.3.grad_ref, bf16[8,18,16,128]{3,2,1,0:T(8,128)(2,1)S(1)} %all_to_all.25.mine_ref.got_ref, bf16[1,2048,256]{2,1,0:T(8,128)(2,1)S(1)} %copy-done, ...), custom_call_target="tpu_custom_call" | custom-call | flops 400000000 | bytes 12000000 | tf_op jit(solution)/shard_map/grads_first/pallas_call | solution.py:354
  97.4 0.0 collective-permute-done.1.grad_ref
  97.4 4.2 %grads_second.1 = bf16[8,152,256]{2,1,0:T(8,128)(2,1)S(1)} custom-call(bf16[8,128,256]{2,1,0:T(8,128)(2,1)S(1)} %collective-permute-done.1.grad_ref, bf16[8,18,16,128]{3,2,1,0:T(8,128)(2,1)S(1)} %collective-permute-done.other_ref.got_ref, bf16[1,2048,256]{2,1,0:T(8,128)(2,1)S(1)} %copy-done, bf16[2,8,128,128]{3,2,1,0:T(8,128)(2,1)} %get-tuple-element.50.refs_0_, ...), custom_call_target="tpu_custom_call" | custom-call | flops 400000000 | bytes 12000000 | tf_op jit(solution)/shard_map/grads_second/pallas_call | solution.py:354
  101.7 22.5 %all_to_all.27.got_ref.mine_ref = bf16[8,152,256]{2,1,0:T(8,128)(2,1)S(1)} all-to-all(bf16[8,152,256]{2,1,0:T(8,128)(2,1)S(1)} %grads_second.1), channel_id=1, replica_groups={{0,2,4,6,8,10,12,14},{1,3,5,7,9,11,13,15},{16,18,20,22,24,26,28,30},{17..., dimensions={0} | all-to-all | bytes 1245184 | tf_op jit(solution)/shard_map/all_to_all | solution.py:468
  124.2 2.3 %collective-permute-start.2 = (bf16[8,152,256]{2,1,0:T(8,128)(2,1)S(1)}, bf16[8,152,256]{2,1,0:T(8,128)(2,1)S(1)}, u32[]{:S(2)}, u32[]{:S(2)}) collective-permute-start(bf16[8,152,256]{2,1,0:T(8,128)(2,1)S(1)} %all_to_all.27.got_ref.mine_ref), channel_id=1, source_target_pairs={{0,1},{1,0},{2,3},{3,2},{4,5},{5,4},{6,7},{7,6},{8,9},{9,8},{10,11... | collective-permute-start | bytes 1867784 | tf_op jit(solution)/shard_map/ppermute | solution.py:469
  126.5 1.1 widen.1.begun_ref
  127.6 0.6 collective-permute-done.2.other_ref
  128.2 1.1 spread.1
  (4 shorter events, 0.0 us)
Async XLA Ops:
  0.6 43.5 %copy-start = (bf16[1,2048,256]{2,1,0:T(8,128)(2,1)S(1)}, bf16[1,2048,256]{2,1,0:T(8,128)(2,1)}, u32[]{:S(2)}) copy-start(bf16[1,2048,256]{2,1,0:T(8,128)(2,1)} %weight_ref.5) | copy-start | bytes 3145732
  2.0 46.8 %copy-start.1 = (bf16[8192]{0:T(1024)(128)(2,1)S(1)}, bf16[8192]{0:T(1024)(128)(2,1)}, u32[]{:S(2)}) copy-start(bf16[8192]{0:T(1024)(128)(2,1)} %param.14) | copy-start | bytes 49156
  30.1 14.0 %collective-permute-start = (bf16[8,18,16,128]{3,2,1,0:T(8,128)(2,1)S(1)}, bf16[8,18,16,128]{3,2,1,0:T(8,128)(2,1)S(1)}, u32[]{:S(2)}, u32[]{:S(2)}) collective-permute-start(bf16[8,18,16,128]{3,2,1,0:T(8,128)(2,1)S(1)} %all_to_all.25.mine_ref.got_ref), channel_id=1, source_target_pairs={{0,1},{1,0},{2,3},{3,2},{4,5},{5,4},{6,7},{7,6},{8,9},{9,8},{10,11... | collective-permute-start | bytes 1769480 | tf_op jit(solution)/shard_map/ppermute | solution.py:452
  34.5 18.6 %all-to-all-start.1 = ((bf16[32,4,256]{2,1,0:T(4,128)(2,1)}), bf16[32,4,256]{2,1,0:T(4,128)(2,1)S(1)}, u32[]{:S(2)}, u32[]{:S(2)}) async-start(bf16[32,4,256]{2,1,0:T(4,128)(2,1)} %bitcast.19), calls=%async_computation.1 | async-start | bytes 131072 | tf_op jit(solution)/shard_map/all_to_all | solution.py:457
  69.3 18.2 %all-to-all-start.3 = ((bf16[8,128,256]{2,1,0:T(8,128)(2,1)}), bf16[8,128,256]{2,1,0:T(8,128)(2,1)S(1)}, u32[]{:S(2)}, u32[]{:S(2)}) async-start(bf16[8,128,256]{2,1,0:T(8,128)(2,1)} %tower_back.1), calls=%async_computation.3 | async-start | bytes 1048576 | tf_op jit(solution)/shard_map/all_to_all | solution.py:466
  87.4 10.0 %collective-permute-start.1 = (bf16[8,128,256]{2,1,0:T(8,128)(2,1)S(1)}, bf16[8,128,256]{2,1,0:T(8,128)(2,1)S(1)}, u32[]{:S(2)}, u32[]{:S(2)}) collective-permute-start(bf16[8,128,256]{2,1,0:T(8,128)(2,1)S(1)} %all-to-all-done.3.grad_ref), channel_id=1, source_target_pairs={{0,1},{1,0},{2,3},{3,2},{4,5},{5,4},{6,7},{7,6},{8,9},{9,8},{10,11... | collective-permute-start | bytes 1572872 | tf_op jit(solution)/shard_map/ppermute | solution.py:467
  124.2 4.0 %collective-permute-start.2 = (bf16[8,152,256]{2,1,0:T(8,128)(2,1)S(1)}, bf16[8,152,256]{2,1,0:T(8,128)(2,1)S(1)}, u32[]{:S(2)}, u32[]{:S(2)}) collective-permute-start(bf16[8,152,256]{2,1,0:T(8,128)(2,1)S(1)} %all_to_all.27.got_ref.mine_ref), channel_id=1, source_target_pairs={{0,1},{1,0},{2,3},{3,2},{4,5},{5,4},{6,7},{7,6},{8,9},{9,8},{10,11... | collective-permute-start | bytes 1867784 | tf_op jit(solution)/shard_map/ppermute | solution.py:469
